TPU v7x, 32 devices: a whole 2x2x4 slice. The times are simulated.
32 devices in a mesh: gr: 4 (over x, core), gc: 8 (over z, y).
Axes of the slice: x: 2, y: 2, z: 4, core: 2. Of those that a mesh axis runs over, the one named last changes fastest.
Arguments:
- factor_window: bfloat16 [13312, 2048], P('gr', 'gc'), may hold values from -0.125 to 0.125
- upper_panel: bfloat16 [2048, 512], P('gc', 'gr'), may hold values from -6 to 6
- panel_block: float32 [13312, 512], P(('gr', 'gc'))
- first_block: int32 [16], P('gc'), may hold values from 0 to 52
Outputs:
- panel_factor: float32 [13312, 512], P(('gr', 'gc'))
All inputs are finite; a program needn't handle non-finite values.
Results may differ from a plain program's by a relative error of at most 0.0003.
Values may be sent and summed in bfloat16 or wider, within the bound.
No kernel may reach another device: no remote copies, remote signals or barrier semaphores. Data moves between devices by JAX's collectives and lax.ppermute only.
A program may use at most 64 MiB of HBM per device.

v0:
```python
import jax
import jax.numpy as jnp
from jax import lax
from jax.sharding import PartitionSpec as P

BLK = 128
NS_ITERS = 3


def masked_rows(window_rows, slab_start, col_first):
    row_ids = slab_start + jnp.arange(window_rows.shape[0], dtype=jnp.int32)
    inside = (row_ids // BLK)[:, None] >= col_first[None, :]
    return jnp.where(inside, window_rows, jnp.zeros_like(window_rows))


def body(factor_window, upper_panel, panel_block, first_block):
    row_groups = lax.axis_size("gr")
    col_groups = lax.axis_size("gc")
    local_rows = factor_window.shape[0]
    own_rows = local_rows // col_groups
    panel_width = upper_panel.shape[1] * row_groups
    row_base = lax.axis_index("gr") * local_rows
    col_first = jnp.repeat(first_block, BLK)
    whole_panel = lax.all_gather(upper_panel, "gr", axis=1, tiled=True)
    own_update = lax.psum_scatter(
        jnp.dot(
            masked_rows(factor_window, row_base, col_first),
            whole_panel,
            preferred_element_type=jnp.float32,
        ),
        "gc",
        scatter_dimension=0,
        tiled=True,
    )
    schur_rows = panel_block - own_update
    global_start = (lax.axis_index("gr") * col_groups + lax.axis_index("gc")) * own_rows
    positions = jnp.arange(panel_width, dtype=jnp.int32) - global_start
    inside = (positions >= 0) & (positions < own_rows)
    picked = jnp.take(schur_rows, jnp.clip(positions, 0, own_rows - 1), axis=0)
    pivot_term = jnp.where(inside[:, None], picked, jnp.zeros_like(picked))
    pivot_block = lax.psum(pivot_term, ("gr", "gc"))
    pivot_scale = jnp.mean(jnp.diagonal(pivot_block))
    scaled = pivot_block / pivot_scale
    inverse = jnp.eye(panel_width, dtype=jnp.float32)
    for iteration in range(NS_ITERS):
        partial_value = jnp.dot(scaled, inverse, precision=lax.Precision.HIGHEST)
        inverse = 2.0 * inverse - jnp.dot(inverse, partial_value, precision=lax.Precision.HIGHEST)
    factor = jnp.dot(schur_rows, inverse, precision=lax.Precision.HIGHEST) / pivot_scale
    rows_global = global_start + jnp.arange(own_rows, dtype=jnp.int32)
    from_inverse = jnp.take(inverse, jnp.clip(rows_global, 0, panel_width - 1), axis=0)
    return jnp.where((rows_global < panel_width)[:, None], from_inverse, factor)


def solution(mesh):
    return jax.shard_map(
        body,
        mesh=mesh,
        in_specs=(P("gr", "gc"), P("gc", "gr"), P(("gr", "gc"), None), P("gc")),
        out_specs=P(("gr", "gc"), None),
        check_vma=False,
    )
```

profile of v0, /device:TPU:0, one launch (start us, length us, event | category | flops | bytes accessed | tf_op | source)
XLA Modules:
  0.0 310.8 jit_solution(1503556689882492118)
XLA Ops:
  6.5 0.0 reduce-scatter.2.cloned.1.call-start
  6.5 7.5 %all_gather.3 = bf16[256,512]{1,0:T(8,128)(2,1)S(1)} all-gather(bf16[256,128]{1,0:T(8,128)(2,1)} %param.5), channel_id=1, replica_groups=mesh['gr'=4,'gc'=8] {'gr'}, dimensions={1}, use_global_device_ids=true | all-gather | bytes 327680 | tf_op jit(solution)/shard_map/all_gather | solution.py:24
  14.1 0.0 copy-done
  14.1 0.1 broadcast_bitcast_fusion
  14.2 5.3 %fusion = f32[3328,512]{1,0:T(8,128)} fusion(bf16[256,512]{1,0:T(8,128)(2,1)S(1)} %all_gather.3, bf16[3328,256]{1,0:T(8,128)(2,1)} %param.4, s32[256]{0:T(256)S(1)} %broadcast_bitcast_fusion, s32[3328]{0:T(1024)S(1)} %add_select_fusion), kind=kOutput, calls=%fused_computation.4 | convolution fusion | flops 874119168 | bytes 8796160 | tf_op jit(solution)/shard_map/dot_general | solution.py:26
  19.5 0.0 reduce-scatter.2.cloned.1.call-update
  19.5 0.0 all-reduce.2.cloned.1.call-start
  19.7 126.7 %reduce-scatter.2.cloned.1.call-done = f32[416,512]{1,0:T(8,128)} async-done(((f32[3328,512]{1,0:T(8,128)}), f32[416,512]{1,0:T(8,128)}) %reduce-scatter.2.cloned.1.call-update) | async-done | bytes 851984 | tf_op jit(solution)/shard_map/reduce_scatter | solution.py:25
  146.4 0.0 copy-done.2
  146.4 1.3 sub.43
  147.7 1.6 gather_fusion
  149.4 1.2 select_select_fusion
  150.6 0.0 all-reduce.2.cloned.1.call-update
  150.7 129.7 %all-reduce.2.cloned.1.call-done = f32[512,512]{1,0:T(8,128)} async-done(((f32[512,512]{1,0:T(8,128)}), f32[512,512]{1,0:T(8,128)}) %all-reduce.2.cloned.1.call-update) | async-done | bytes 1048592 | tf_op jit(solution)/shard_map/psum | solution.py:41
  280.4 8.6 %gather_fusion.1 = f32[512]{0:T(512)S(1)} fusion(f32[512,512]{1,0:T(8,128)} %all-reduce.2.cloned.1.call-done, s32[512]{0:T(512)S(1)} %bitcast.15), kind=kCustom, calls=%fused_computation.1 | custom fusion | bytes 8192 | tf_op jit(solution)/shard_map/jit(diagonal)/cond/branch_0_fun/gather | solution.py:42
  289.0 0.6 reduce_sum.9
  290.3 1.0 fusion.4
  291.3 1.1 convolution_subtract_fusion.2
  292.4 1.9 fusion.15
  294.2 1.9 convolution_subtract_fusion.1
  296.1 1.9 fusion.14
  298.0 1.9 convolution_subtract_fusion
  299.9 1.6 gather_fusion.2
  301.5 2.5 fusion.3
  (12 shorter events, 0.1 us)
Async XLA Ops:
  6.5 7.5 %copy-start = (s32[2]{0:T(128)S(1)}, s32[2]{0:T(128)}, u32[]{:S(2)}) copy-start(s32[2]{0:T(128)} %param.7) | copy-start | bytes 28
  6.5 139.8 %reduce-scatter.2.cloned.1.call-start = ((), (), s32[]{:S(2)}) async-start(), calls=%async_computation.1 | async-start | bytes 7667712 | tf_op jit(solution)/shard_map/reduce_scatter | solution.py:25
  19.5 126.9 %copy-start.2 = (f32[416,512]{1,0:T(8,128)S(1)}, f32[416,512]{1,0:T(8,128)}, u32[]{:S(2)}) copy-start(f32[416,512]{1,0:T(8,128)} %param.6) | copy-start | bytes 2555908
  19.5 260.9 %all-reduce.2.cloned.1.call-start = ((), (), s32[]{:S(2)}) async-start(), calls=%async_computation.2 | async-start | bytes 2097152 | tf_op jit(solution)/shard_map/psum | solution.py:41
  280.4 9.9 %copy-start.1 = (f32[512,512]{1,0:T(8,128)S(1)}, f32[512,512]{1,0:T(8,128)}, u32[]{:S(2)}) copy-start(f32[512,512]{1,0:T(8,128)} %all-reduce.2.cloned.1.call-done) | copy-start | bytes 3145732
Sparse Core Ops, SparseCore 0:
  19.7 126.6 reduce-scatter.1
  151.6 128.8 all-reduce.1
where the time goes:
time: 311 us
  waiting for transfers between devices  256 us (82%)
  matrix products  17.3 us (6%)
  between operations  14.2 us (5%)
  local copies, waits for them, and re-layouts  12 us (4%)
  blocking collectives  7.54 us (2%)
  other arithmetic  3.25 us (1%)
    psum x1, waiting for transfers between devices, body(): pivot_block = lax.psum(pivot_term, ('gr', 'gc'))  130 us
    reduce_scatter x1, waiting for transfers between devices, body(): lax.psum_scatter(jnp.dot(masked_rows(factor_window, row_base, col_first),...  127 us
    gather x1, local copies, waits for them, and re-layouts, body(): pivot_scale = jnp.mean(jnp.diagonal(pivot_block))  8.61 us
    all_gather x1, blocking collectives, body(): whole_panel = lax.all_gather(upper_panel, 'gr', axis=1, tiled=True)  7.54 us
  transfers between devices with their start and end apart: 2, of which 2 were waited for; matrix products, arithmetic and copies ran while one was open for 0% of the time, Pallas kernels for 0%

commit v1 on v0

v1 whole, which is shorter than its diff:
```python
import jax
import jax.numpy as jnp
from jax import lax
from jax.sharding import PartitionSpec as P

BLK = 128
NS_ITERS = 3
CORES = 2
WIRE = jnp.float16


def inner_size(n):
    return max(d for d in range(1, n + 1) if n % d == 0 and d * d <= n)


class Grid:
    def __init__(self):
        self.gr = lax.axis_size("gr")
        self.gc = lax.axis_size("gc")
        self.cores = CORES if self.gr % CORES == 0 else 1
        self.xs = self.gr // self.cores
        self.ys = inner_size(self.gc)
        self.zs = self.gc // self.ys
        gr, gc = lax.axis_index("gr"), lax.axis_index("gc")
        self.x, self.core = gr // self.cores, gr % self.cores
        self.z, self.y = gc // self.ys, gc % self.ys
        self.gr_index, self.gc_index = gr, gc

    def swap(self, value, dx=0, dcore=0, dz=0, dy=0, sources=None):
        pairs = []
        for gr in range(self.gr):
            for gc in range(self.gc):
                if sources is not None and not sources(gr, gc):
                    continue
                to_gr = ((gr // self.cores) ^ dx) * self.cores + ((gr % self.cores) ^ dcore)
                to_gc = ((gc // self.ys) ^ dz) * self.ys + ((gc % self.ys) ^ dy)
                pairs.append((gr * self.gc + gc, to_gr * self.gc + to_gc))
        return lax.ppermute(value, ("gr", "gc"), pairs)


def rows_of(value, start, count):
    return lax.dynamic_slice_in_dim(value, start, count, axis=0)


def body(factor_window, upper_panel, panel_block, first_block):
    grid = Grid()
    local_rows, depth = factor_window.shape
    own_rows, panel_width = panel_block.shape
    row_base = grid.gr_index * local_rows
    col_first = jnp.repeat(first_block, BLK)
    global_start = (grid.gr_index * grid.gc + grid.gc_index) * own_rows

    def masked(start, count):
        row_ids = row_base + start + jnp.arange(count, dtype=jnp.int32)
        inside = (row_ids // BLK)[:, None] >= col_first[None, :]
        part = rows_of(factor_window, start, count)
        return jnp.where(inside, part, jnp.zeros_like(part))

    def chunk(k, j):
        return masked(((grid.z ^ k) * grid.ys + (grid.y ^ j)) * own_rows, own_rows)

    plane = [(a, b) for b in range(grid.ys) for a in range(grid.xs)]
    piece = panel_width // (grid.gr * grid.ys)
    chip_rows = piece * grid.cores

    def chip_start(x, y):
        return (y * grid.xs + x) * chip_rows

    shards, pivot_rows = {}, {}
    halves = depth // upper_panel.shape[1]
    for a, b in plane:
        rows = masked(chip_start(grid.x ^ a, grid.y ^ b), chip_rows)
        if (a, b) == (0, 0):
            shards[a, b], pivot_rows[a, b] = upper_panel, rows
            continue
        packed = jnp.concatenate([upper_panel] + jnp.split(rows, halves, axis=1), axis=0)
        packed = grid.swap(packed, dx=a, dy=b)
        shards[a, b] = packed[:depth]
        pivot_rows[a, b] = jnp.concatenate(jnp.split(packed[depth:], halves, axis=0), axis=1)
    picked = []
    for b in range(grid.ys):
        stack = jnp.stack([pivot_rows[a, b] for a in range(grid.xs)])
        picked.append(lax.dynamic_index_in_dim(stack, grid.x, 0, keepdims=False))
    picked = jnp.concatenate(picked, axis=1)
    shard_stack = jnp.stack([shards[a, b] for a, b in plane])
    other_stack = grid.swap(shard_stack, dcore=1) if grid.cores > 1 else None

    def panel_columns(b):
        blocks = []
        for gr in range(grid.gr):
            x, core = gr // grid.cores, gr % grid.cores
            index = b * grid.xs + (grid.x ^ x)
            mine = lax.dynamic_index_in_dim(shard_stack, index, 0, keepdims=False)
            if other_stack is not None:
                theirs = lax.dynamic_index_in_dim(other_stack, index, 0, keepdims=False)
                mine = jnp.where(grid.core == core, mine, theirs)
            blocks.append(mine)
        return jnp.concatenate(blocks, axis=1)

    panel = jnp.concatenate([panel_columns(b) for b in range(grid.ys)], axis=0)
    if grid.cores > 1:
        others = grid.swap(rows_of(picked, piece, piece), dcore=1, sources=lambda gr, gc: gr == 0 or gr % grid.cores == 0)
        pivot_part = jnp.where(grid.core == 0, picked[:piece], others)
    else:
        pivot_part = picked

    def holds(gr, gc):
        return gr == 0 and gc * own_rows < panel_width

    padded = jnp.zeros((panel_width + own_rows, panel_width), jnp.float32)
    padded = lax.dynamic_update_slice_in_dim(padded, panel_block, jnp.minimum(global_start, panel_width), axis=0)
    before = None
    for a, b in plane:
        rows = rows_of(padded, chip_start(grid.x ^ a, grid.y ^ b), chip_rows)
        if (a, b) == (0, 0):
            rows = jnp.where(grid.gr_index == 0, rows, 0.0)
        else:
            rows = grid.swap(rows, dx=a, dy=b, sources=holds)
        before = rows if before is None else before + rows
    if grid.cores > 1:
        others = grid.swap(before[piece:], dcore=1, sources=lambda gr, gc: gr % grid.cores == 0)
        before = jnp.where(grid.core == 0, before[:piece], others)

    total = before - jnp.dot(pivot_part, panel, preferred_element_type=jnp.float32)
    step = 1
    while step < grid.zs:
        total = total + grid.swap(total, dz=step)
        step *= 2
    pieces = {(0, 0): total}
    for a, b in plane[1:]:
        pieces[a, b] = grid.swap(total, dx=a, dy=b)
    piece_stack = jnp.stack([pieces[a, b] for a, b in plane])
    other_pieces = grid.swap(piece_stack, dcore=1) if grid.cores > 1 else None
    blocks = []
    for y in range(grid.ys):
        for x in range(grid.xs):
            index = (grid.y ^ y) * grid.xs + (grid.x ^ x)
            mine = lax.dynamic_index_in_dim(piece_stack, index, 0, keepdims=False)
            if other_pieces is None:
                blocks.append(mine)
                continue
            theirs = lax.dynamic_index_in_dim(other_pieces, index, 0, keepdims=False)
            for core in range(grid.cores):
                blocks.append(jnp.where(grid.core == core, mine, theirs))
    pivot_block = jnp.concatenate(blocks, axis=0)

    order = list(range(grid.zs - 1, -1, -1))
    arrived = {}
    for ks in ([order[0]], order[1:]):
        if not ks:
            continue
        for j in range(1, grid.ys):
            got = grid.swap(jnp.concatenate([chunk(k, j) for k in ks], axis=0), dy=j)
            for n, k in enumerate(ks):
                arrived[k, j] = got[n * own_rows : (n + 1) * own_rows]
    sums = {}
    for k in order:
        whole = jnp.concatenate([chunk(k, 0)] + [arrived[k, j] for j in range(1, grid.ys)], axis=1)
        sums[k] = jnp.dot(whole, panel, preferred_element_type=jnp.float32)
    step = 1
    while step < grid.zs:
        for k in sorted((k for k in sums if k & step), reverse=True):
            got = grid.swap(sums.pop(k).astype(WIRE), dz=step)
            sums[k ^ step] = sums[k ^ step] + got.astype(jnp.float32)
        step *= 2
    schur_rows = panel_block - sums[0]

    pivot_scale = jnp.mean(jnp.diagonal(pivot_block))
    scaled = pivot_block / pivot_scale
    eye = jnp.eye(panel_width, dtype=jnp.float32)
    inverse = 2.0 * eye - scaled
    for iteration in range(NS_ITERS - 1):
        partial_value = jnp.dot(scaled, inverse, precision=lax.Precision.HIGHEST)
        inverse = 2.0 * inverse - jnp.dot(inverse, partial_value, precision=lax.Precision.HIGHEST)
    factor = jnp.dot(schur_rows, inverse, precision=lax.Precision.HIGHEST) / pivot_scale
    tail = jnp.pad(inverse, ((0, own_rows), (0, 0)))
    from_inverse = rows_of(tail, jnp.minimum(global_start, panel_width), own_rows)
    rows_global = global_start + jnp.arange(own_rows, dtype=jnp.int32)
    return jnp.where((rows_global < panel_width)[:, None], from_inverse, factor)


def solution(mesh):
    return jax.shard_map(
        body,
        mesh=mesh,
        in_specs=(P("gr", "gc"), P("gc", "gr"), P(("gr", "gc"), None), P("gc")),
        out_specs=P(("gr", "gc"), None),
        check_vma=False,
    )
```

time: 311 us -> 96.9 us (0.31)
  waiting for transfers between devices: 256 us -> 30.8 us
  starting transfers between devices: 0.04 us -> 28 us
  between operations: 14.2 us -> 1.25 us
  blocking collectives: 7.54 us -> 0 us
  other arithmetic: 3.25 us -> 10.2 us
    psum x1 -> x0, waiting for transfers between devices: 130 us -> none  [body(): pivot_block = lax.psum(pivot_term, ('gr', 'gc'))]
    reduce_scatter x1 -> x0, waiting for transfers between devices: 127 us -> none  [body(): lax.psum_scatter(jnp.dot(masked_rows(factor_window, row_base, col_first),...]
    ppermute x0 -> x20, waiting for transfers between devices: none -> 30.8 us  [swap(): return lax.ppermute(value, ('gr', 'gc'), pairs)]
    ppermute x0 -> x20, starting transfers between devices: none -> 28 us  [swap(): return lax.ppermute(value, ('gr', 'gc'), pairs)]
    all_gather x1 -> x0, blocking collectives: 7.54 us -> none  [body(): whole_panel = lax.all_gather(upper_panel, 'gr', axis=1, tiled=True)]
    gather x1, local copies, waits for them, and re-layouts: 8.61 us -> 4.52 us  [body(): pivot_scale = jnp.mean(jnp.diagonal(pivot_block))]
    select_n x4 -> x9, other arithmetic: 1.26 us -> 4.54 us  [the longest x1 2.64 us: masked(): return jnp.where(inside, part, jnp.zeros_like(part))]
    gather x2 -> x0, local copies, waits for them, and re-layouts: 3.26 us -> none  [the longest x1 1.64 us: body(): jnp.take(inverse, jnp.clip(rows_global, 0, panel_width - 1), axis=0)]
  transfers between devices with their start and end apart: 2 -> 20, of which waited for: 2 -> 7; matrix products, arithmetic and copies ran while one was open for 0% -> 17% of each run, Pallas kernels for 0% -> 0%
where the time goes in v1:
time: 96.9 us; the launch traced here: 96.1 us
  waiting for transfers between devices  30.8 us (32%)
  starting transfers between devices  28 us (29%)
  matrix products  14.7 us (15%)
  local copies, waits for them, and re-layouts  11.2 us (12%)
  other arithmetic  10.2 us (11%)
  between operations  1.25 us (1%)
    ppermute x20, waiting for transfers between devices, swap(): return lax.ppermute(value, ('gr', 'gc'), pairs)  30.8 us
    ppermute x20, starting transfers between devices, swap(): return lax.ppermute(value, ('gr', 'gc'), pairs)  28 us
    gather x1, local copies, waits for them, and re-layouts, body(): pivot_scale = jnp.mean(jnp.diagonal(pivot_block))  4.52 us
    dot_general x4, matrix products, body(): sums[k] = jnp.dot(whole, panel, preferred_element_type=jnp.float32)  4.33 us
    dot_general x2, matrix products, body(): partial_value = jnp.dot(scaled, inverse, precision=lax.Precision.HIGHEST)  3.83 us
    dot_general x2, matrix products, body(): jnp.dot(inverse, partial_value, precision=lax.Precision.HIGHEST)  3.83 us
    select_n x1, other arithmetic, masked(): return jnp.where(inside, part, jnp.zeros_like(part))  2.64 us
    another operation x3, local copies, waits for them, and re-layouts, body(): shard_stack = jnp.stack([shards[a, b] for a, b in plane])  2.53 us
  transfers between devices with their start and end apart: 20, of which 7 were waited for; matrix products, arithmetic and copies ran while one was open for 17% of the time, Pallas kernels for 0%

profile of v1, /device:TPU:0, one launch (start us, length us, event | category | flops | bytes accessed | tf_op | source)
XLA Modules:
  0.0 96.1 jit_solution(16440663708305166916)
XLA Ops:
  0.8 1.8 %fusion.25 = (bf16[1,128,256]{2,1,0:T(8,128)(2,1)}, bf16[128,256]{1,0:T(8,128)(2,1)S(1)}, bf16[128,256]{1,0:T(8,128)(2,1)S(1)}, bf16[128,256]{1,0:T(8,128)(2,1)S(1)}) fusion(bf16[3328,256]{1,0:T(8,128)(2,1)} %param.4, s32[]{:T(128)S(6)} %select_n.409, s32[256]{0:T(256)S(1)} %broadcast_bitcast_fusion, s32[128]{0:T(128)S(1)} %and_select_fusion.3, ...), kind=kLoop, calls=%fused_computation.72 | loop fusion | flops 262144 | bytes 527376 | tf_op jit(solution)/shard_map/stack | solution.py:82
  2.5 1.6 %fusion.21 = (bf16[512,128]{1,0:T(8,128)(2,1)}, bf16[512,128]{1,0:T(8,128)(2,1)}, bf16[512,128]{1,0:T(8,128)(2,1)}) fusion(bf16[256,128]{1,0:T(8,128)(2,1)} %param.5, bf16[128,128]{1,0:T(8,128)(2,1)S(1)} %get-tuple-element.41, bf16[128,128]{1,0:T(8,128)(2,1)S(1)} %get-tuple-element.40, bf16[128,128]{1,0:T(8,128)(2,1)S(1)} %get-tuple-element.43, ...), kind=kLoop, calls=%fused_computation.49 | loop fusion | flops 1048576 | bytes 655360 | tf_op jit(solution)/shard_map/concatenate | solution.py:76
  4.2 3.0 %collective-permute-start.5 = (bf16[512,128]{1,0:T(8,128)(2,1)}, bf16[512,128]{1,0:T(8,128)(2,1)}, u32[]{:S(2)}, u32[]{:S(2)}) collective-permute-start(bf16[512,128]{1,0:T(8,128)(2,1)} %get-tuple-element.38), channel_id=1, source_target_pairs={{0,1},{1,0},{2,3},{3,2},{4,5},{5,4},{6,7},{7,6},{8,9},{9,8},{10,11... | collective-permute-start | bytes 393224 | tf_op jit(solution)/shard_map/ppermute | solution.py:38
  9.7 4.6 %collective-permute-start = (f32[128,512]{1,0:T(8,128)S(1)}, f32[128,512]{1,0:T(8,128)}, u32[]{:S(2)}, u32[]{:S(2)}) collective-permute-start(f32[128,512]{1,0:T(8,128)S(1)} %get-tuple-element.5), channel_id=1, source_target_pairs={{0,16},{1,17}} | collective-permute-start | bytes 786440 | tf_op jit(solution)/shard_map/ppermute | solution.py:38
  14.3 3.4 %collective-permute-start.1 = (f32[128,512]{1,0:T(8,128)S(1)}, f32[128,512]{1,0:T(8,128)}, u32[]{:S(2)}, u32[]{:S(2)}) collective-permute-start(f32[128,512]{1,0:T(8,128)S(1)} %get-tuple-element.7), channel_id=1, source_target_pairs={{0,1},{1,0}} | collective-permute-start | bytes 786440 | tf_op jit(solution)/shard_map/ppermute | solution.py:38
  19.7 2.6 %compare_select_fusion.7 = (bf16[416,256]{1,0:T(8,128)(2,1)}, bf16[416,256]{1,0:T(8,128)(2,1)S(1)}, bf16[416,256]{1,0:T(8,128)(2,1)S(1)}, bf16[416,256]{1,0:T(8,...) fusion(bf16[3328,256]{1,0:T(8,128)(2,1)} %param.4, ...), kind=kLoop, calls=%fused_computation.43 | loop fusion | flops 1703936 | bytes 3422240 | tf_op jit(solution)/shard_map/jit(_where)/select_n | solution.py:57
  25.9 1.6 %collective-permute-start.17 = (bf16[416,256]{1,0:T(8,128)(2,1)S(1)}, bf16[416,256]{1,0:T(8,128)(2,1)S(1)}, u32[]{:S(2)}, u32[]{:S(2)}) collective-permute-start(bf16[416,256]{1,0:T(8,128)(2,1)S(1)} %get-tuple-element.18), channel_id=1, source_target_pairs={{0,1},{1,0},{2,3},{3,2},{4,5},{5,4},{6,7},{7,6},{8,9},{9,8},{10,11... | collective-permute-start | bytes 638984 | tf_op jit(solution)/shard_map/ppermute | solution.py:38
  32.2 2.4 %collective-permute-start.3 = (f32[64,512]{1,0:T(8,128)S(1)}, f32[64,512]{1,0:T(8,128)S(1)}, u32[]{:S(2)}, u32[]{:S(2)}) collective-permute-start(f32[64,512]{1,0:T(8,128)S(1)} %slice.48), channel_id=1, source_target_pairs={{0,8},{1,9},{2,10},{3,11},{4,12},{5,13},{6,14},{7,15},{16,24},{17,... | collective-permute-start | bytes 393224 | tf_op jit(solution)/shard_map/ppermute | solution.py:38
  34.6 1.5 %collective-permute-start.7 = (bf16[64,512]{1,0:T(8,128)(2,1)S(1)}, bf16[64,512]{1,0:T(8,128)(2,1)S(1)}, u32[]{:S(2)}, u32[]{:S(2)}) collective-permute-start(bf16[64,512]{1,0:T(8,128)(2,1)S(1)} %pad_maximum_fusion.6), channel_id=1, source_target_pairs={{0,8},{1,9},{2,10},{3,11},{4,12},{5,13},{6,14},{7,15},{16,24},{17,... | collective-permute-start | bytes 196616 | tf_op jit(solution)/shard_map/ppermute | solution.py:38
  37.1 3.7 %collective-permute-done.17 = bf16[416,256]{1,0:T(8,128)(2,1)S(1)} collective-permute-done((bf16[416,256]{1,0:T(8,128)(2,1)S(1)}, bf16[416,256]{1,0:T(8,128)(2,1)S(1)}, u32[]{:S(2)}, u32[]{:S(2)}) %collective-permute-start.17) | collective-permute-done | bytes 213024 | tf_op jit(solution)/shard_map/ppermute | solution.py:38
  41.3 2.2 %collective-permute-done.9 = f32[64,512]{1,0:T(8,128)S(1)} collective-permute-done((f32[64,512]{1,0:T(8,128)S(1)}, f32[64,512]{1,0:T(8,128)S(1)}, u32[]{:S(2)}, u32[]{:S(2)}) %collective-permute-start.9) | collective-permute-done | bytes 131104 | tf_op jit(solution)/shard_map/ppermute | solution.py:38
  44.5 9.8 %collective-permute-done.10 = f32[64,512]{1,0:T(8,128)S(1)} collective-permute-done((f32[64,512]{1,0:T(8,128)S(1)}, f32[64,512]{1,0:T(8,128)S(1)}, u32[]{:S(2)}, u32[]{:S(2)}) %collective-permute-start.10) | collective-permute-done | bytes 131104 | tf_op jit(solution)/shard_map/ppermute | solution.py:38
  54.4 2.4 %collective-permute-start.11 = (f32[64,512]{1,0:T(8,128)S(1)}, f32[64,512]{1,0:T(8,128)S(1)}, u32[]{:S(2)}, u32[]{:S(2)}) collective-permute-start(f32[64,512]{1,0:T(8,128)S(1)} %add.461), channel_id=1, source_target_pairs={{0,16},{1,17},{2,18},{3,19},{4,20},{5,21},{6,22},{7,23},{8,24},{9,... | collective-permute-start | bytes 393224 | tf_op jit(solution)/shard_map/ppermute | solution.py:38
  56.8 1.5 %collective-permute-start.12 = (f32[64,512]{1,0:T(8,128)S(1)}, f32[64,512]{1,0:T(8,128)S(1)}, u32[]{:S(2)}, u32[]{:S(2)}) collective-permute-start(f32[64,512]{1,0:T(8,128)S(1)} %add.461), channel_id=1, source_target_pairs={{0,1},{1,0},{2,3},{3,2},{4,5},{5,4},{6,7},{7,6},{8,9},{9,8},{10,11... | collective-permute-start | bytes 393224 | tf_op jit(solution)/shard_map/ppermute | solution.py:38
  59.5 3.4 %collective-permute-start.19 = (f16[416,512]{1,0:T(8,128)(2,1)}, f16[416,512]{1,0:T(8,128)(2,1)}, u32[]{:S(2)}, u32[]{:S(2)}) collective-permute-start(f16[416,512]{1,0:T(8,128)(2,1)} %fusion.3), channel_id=1, source_target_pairs={{0,4},{1,5},{2,6},{3,7},{4,0},{5,1},{6,2},{7,3},{8,12},{9,13},{10,... | collective-permute-start | bytes 1277960 | tf_op jit(solution)/shard_map/ppermute | solution.py:38
  64.3 3.7 %collective-permute-done.16 = f16[416,512]{1,0:T(8,128)(2,1)S(1)} collective-permute-done((f16[416,512]{1,0:T(8,128)(2,1)S(1)}, f16[416,512]{1,0:T(8,128)(2,1)S(1)}, u32[]{:S(2)}, u32[]{:S(2)}) %collective-permute-start.16) | collective-permute-done | bytes 426016 | tf_op jit(solution)/shard_map/ppermute | solution.py:38
  68.0 9.4 %collective-permute-done.19 = f16[416,512]{1,0:T(8,128)(2,1)} collective-permute-done((f16[416,512]{1,0:T(8,128)(2,1)}, f16[416,512]{1,0:T(8,128)(2,1)}, u32[]{:S(2)}, u32[]{:S(2)}) %collective-permute-start.19) | collective-permute-done | bytes 426016 | tf_op jit(solution)/shard_map/ppermute | solution.py:38
  77.4 2.4 %fusion.1 = f32[416,512]{1,0:T(8,128)} fusion(f32[416,512]{1,0:T(8,128)S(1)} %copy-done.1, f16[416,512]{1,0:T(8,128)(2,1)} %collective-permute-done.19, f16[416,512]{1,0:T(8,128)(2,1)S(1)} %collective-permute-done.16, bf16[416,256]{1,0:T(8,128)(2,1)S(1)} %get-tuple-element.20, bf16[416,256]{1,0:T(8,128)(2,1)S(1)} %copy-done.4, ...), kind=kOutput, calls=%fused_computation.8 | convolution fusion | flops 224215040 | bytes 3506176 | tf_op jit(solution)/shard_map/dot_general | solution.py:159
  80.1 4.5 %gather_fusion = f32[512]{0:T(512)S(1)} fusion(f32[512,512]{1,0:T(8,128)S(1)} %bitcast_dynamic-update-slice_fusion, s32[512]{0:T(512)S(1)} %bitcast.64), kind=kCustom, calls=%fused_computation | custom fusion | bytes 8192 | tf_op jit(solution)/shard_map/jit(diagonal)/cond/branch_0_fun/gather | solution.py:168
  85.9 1.9 %fusion.4 = f32[512,512]{1,0:T(8,128)S(1)} fusion(f32[512,512]{1,0:T(8,128)S(1)} %bitcast_dynamic-update-slice_fusion, f32[]{:T(128)S(6)} %div.150), kind=kOutput, calls=%fused_computation.14 | convolution fusion | flops 1611923456 | bytes 2097156 | tf_op jit(solution)/shard_map/dot_general | solution.py:173
  87.9 2.0 %convolution_subtract_fusion.1 = f32[512,512]{1,0:T(8,128)S(1)} fusion(f32[512,512]{1,0:T(8,128)S(1)} %fusion.4, f32[512,512]{1,0:T(8,128)S(1)} %bitcast_dynamic-update-slice_fusion, f32[]{:T(128)S(6)} %div.150), kind=kOutput, calls=%fused_computation.3 | convolution fusion | flops 1613234176 | bytes 3145732 | tf_op jit(solution)/shard_map/dot_general | solution.py:174
  89.8 1.9 %fusion.70 = f32[512,512]{1,0:T(8,128)S(1)} fusion(f32[512,512]{1,0:T(8,128)S(1)} %convolution_subtract_fusion.1, f32[512,512]{1,0:T(8,128)S(1)} %bitcast_dynamic-update-slice_fusion, f32[]{:T(128)S(6)} %div.150), kind=kOutput, calls=%fused_computation.199 | convolution fusion | flops 1610874880 | bytes 3145732 | tf_op jit(solution)/shard_map/dot_general | solution.py:173
  91.7 1.9 %convolution_subtract_fusion = f32[512,512]{1,0:T(8,128)S(1)} fusion(f32[512,512]{1,0:T(8,128)S(1)} %convolution_subtract_fusion.1, f32[512,512]{1,0:T(8,128)S(1)} %fusion.70), kind=kOutput, calls=%fused_computation.2 | convolution fusion | flops 1611137024 | bytes 3145728 | tf_op jit(solution)/shard_map/dot_general | solution.py:174
  93.6 2.5 %fusion.2 = f32[416,512]{1,0:T(8,128)} fusion(f32[416,512]{1,0:T(8,128)S(1)} %copy-done.6, f32[512,512]{1,0:T(8,128)S(1)} %convolution_subtract_fusion, s32[]{:T(128)S(6)} %select_n.399, f32[]{:T(128)S(6)} %div.150, pred[416]{0:T(512)(128)(4,1)S(1)} %add_compare_fusion), kind=kOutput, calls=%fused_computation.9 | convolution fusion | flops 1309048832 | bytes 3801608 | tf_op jit(solution)/shard_map/dot_general | solution.py:175
  (90 shorter events, 19.3 us)
Async XLA Ops:
  0.7 8.1 %copy-start.1 = (f32[416,512]{1,0:T(8,128)S(1)}, f32[416,512]{1,0:T(8,128)}, u32[]{:S(2)}) copy-start(f32[416,512]{1,0:T(8,128)} %param.6) | copy-start | bytes 2555908
  4.2 18.2 %collective-permute-start.5 = (bf16[512,128]{1,0:T(8,128)(2,1)}, bf16[512,128]{1,0:T(8,128)(2,1)}, u32[]{:S(2)}, u32[]{:S(2)}) collective-permute-start(bf16[512,128]{1,0:T(8,128)(2,1)} %get-tuple-element.38), channel_id=1, source_target_pairs={{0,1},{1,0},{2,3},{3,2},{4,5},{5,4},{6,7},{7,6},{8,9},{9,8},{10,11... | collective-permute-start | bytes 393224 | tf_op jit(solution)/shard_map/ppermute | solution.py:38
  7.1 17.4 %collective-permute-start.6 = (bf16[512,128]{1,0:T(8,128)(2,1)}, bf16[512,128]{1,0:T(8,128)(2,1)}, u32[]{:S(2)}, u32[]{:S(2)}) collective-permute-start(bf16[512,128]{1,0:T(8,128)(2,1)} %get-tuple-element.39), channel_id=1, source_target_pairs={{0,17},{1,16},{2,19},{3,18},{4,21},{5,20},{6,23},{7,22},{8,25},{9,... | collective-permute-start | bytes 393224 | tf_op jit(solution)/shard_map/ppermute | solution.py:38
  8.6 17.3 %collective-permute-start.4 = (bf16[512,128]{1,0:T(8,128)(2,1)}, bf16[512,128]{1,0:T(8,128)(2,1)}, u32[]{:S(2)}, u32[]{:S(2)}) collective-permute-start(bf16[512,128]{1,0:T(8,128)(2,1)} %get-tuple-element.37), channel_id=1, source_target_pairs={{0,16},{1,17},{2,18},{3,19},{4,20},{5,21},{6,22},{7,23},{8,24},{9,... | collective-permute-start | bytes 393224 | tf_op jit(solution)/shard_map/ppermute | solution.py:38
  9.7 21.3 %collective-permute-start = (f32[128,512]{1,0:T(8,128)S(1)}, f32[128,512]{1,0:T(8,128)}, u32[]{:S(2)}, u32[]{:S(2)}) collective-permute-start(f32[128,512]{1,0:T(8,128)S(1)} %get-tuple-element.5), channel_id=1, source_target_pairs={{0,16},{1,17}} | collective-permute-start | bytes 786440 | tf_op jit(solution)/shard_map/ppermute | solution.py:38
  14.3 16.8 %collective-permute-start.1 = (f32[128,512]{1,0:T(8,128)S(1)}, f32[128,512]{1,0:T(8,128)}, u32[]{:S(2)}, u32[]{:S(2)}) collective-permute-start(f32[128,512]{1,0:T(8,128)S(1)} %get-tuple-element.7), channel_id=1, source_target_pairs={{0,1},{1,0}} | collective-permute-start | bytes 786440 | tf_op jit(solution)/shard_map/ppermute | solution.py:38
  22.3 8.5 %copy-start.3 = (bf16[1,128,256]{2,1,0:T(8,128)(2,1)S(1)}, bf16[1,128,256]{2,1,0:T(8,128)(2,1)}, u32[]{:S(2)}) copy-start(bf16[1,128,256]{2,1,0:T(8,128)(2,1)} %get-tuple-element.8) | copy-start | bytes 196612
  22.3 8.6 %copy-start.2 = (bf16[256,128]{1,0:T(8,128)(2,1)S(1)}, bf16[256,128]{1,0:T(8,128)(2,1)}, u32[]{:S(2)}) copy-start(bf16[256,128]{1,0:T(8,128)(2,1)} %param.5) | copy-start | bytes 196612
  22.4 8.7 %collective-permute-start.2 = (f32[128,512]{1,0:T(8,128)S(1)}, f32[128,512]{1,0:T(8,128)S(1)}, u32[]{:S(2)}, u32[]{:S(2)}) collective-permute-start(f32[128,512]{1,0:T(8,128)S(1)} %get-tuple-element.6), channel_id=1, source_target_pairs={{0,17},{1,16}} | collective-permute-start | bytes 786440 | tf_op jit(solution)/shard_map/ppermute | solution.py:38
  24.5 19.1 %collective-permute-start.15 = (bf16[1248,256]{1,0:T(8,128)(2,1)S(1)}, bf16[1248,256]{1,0:T(8,128)(2,1)S(1)}, u32[]{:S(2)}, u32[]{:S(2)}) collective-permute-start(bf16[1248,256]{1,0:T(8,128)(2,1)S(1)} %pad_maximum_fusion), channel_id=1, source_target_pairs={{0,1},{1,0},{2,3},{3,2},{4,5},{5,4},{6,7},{7,6},{8,9},{9,8},{10,11... | collective-permute-start | bytes 1916936 | tf_op jit(solution)/shard_map/ppermute | solution.py:38
  25.9 14.9 %collective-permute-start.17 = (bf16[416,256]{1,0:T(8,128)(2,1)S(1)}, bf16[416,256]{1,0:T(8,128)(2,1)S(1)}, u32[]{:S(2)}, u32[]{:S(2)}) collective-permute-start(bf16[416,256]{1,0:T(8,128)(2,1)S(1)} %get-tuple-element.18), channel_id=1, source_target_pairs={{0,1},{1,0},{2,3},{3,2},{4,5},{5,4},{6,7},{7,6},{8,9},{9,8},{10,11... | collective-permute-start | bytes 638984 | tf_op jit(solution)/shard_map/ppermute | solution.py:38
  31.0 5.2 %collective-permute-start.8 = (bf16[4,256,128]{2,1,0:T(8,128)(2,1)S(1)}, bf16[4,256,128]{2,1,0:T(8,128)(2,1)S(1)}, u32[]{:S(2)}, u32[]{:S(2)}) collective-permute-start(bf16[4,256,128]{2,1,0:T(8,128)(2,1)S(1)} %pad_maximum_fusion.2), channel_id=1, source_target_pairs={{0,8},{1,9},{2,10},{3,11},{4,12},{5,13},{6,14},{7,15},{8,0},{9,1},... | collective-permute-start | bytes 786440 | tf_op jit(solution)/shard_map/ppermute | solution.py:38
  32.2 4.6 %collective-permute-start.3 = (f32[64,512]{1,0:T(8,128)S(1)}, f32[64,512]{1,0:T(8,128)S(1)}, u32[]{:S(2)}, u32[]{:S(2)}) collective-permute-start(f32[64,512]{1,0:T(8,128)S(1)} %slice.48), channel_id=1, source_target_pairs={{0,8},{1,9},{2,10},{3,11},{4,12},{5,13},{6,14},{7,15},{16,24},{17,... | collective-permute-start | bytes 393224 | tf_op jit(solution)/shard_map/ppermute | solution.py:38
  34.6 2.2 %collective-permute-start.7 = (bf16[64,512]{1,0:T(8,128)(2,1)S(1)}, bf16[64,512]{1,0:T(8,128)(2,1)S(1)}, u32[]{:S(2)}, u32[]{:S(2)}) collective-permute-start(bf16[64,512]{1,0:T(8,128)(2,1)S(1)} %pad_maximum_fusion.6), channel_id=1, source_target_pairs={{0,8},{1,9},{2,10},{3,11},{4,12},{5,13},{6,14},{7,15},{16,24},{17,... | collective-permute-start | bytes 196616 | tf_op jit(solution)/shard_map/ppermute | solution.py:38
  37.0 6.4 %collective-permute-start.9 = (f32[64,512]{1,0:T(8,128)S(1)}, f32[64,512]{1,0:T(8,128)S(1)}, u32[]{:S(2)}, u32[]{:S(2)}) collective-permute-start(f32[64,512]{1,0:T(8,128)S(1)} %fusion.24), channel_id=1, source_target_pairs={{0,2},{1,3},{2,0},{3,1},{4,6},{5,7},{6,4},{7,5},{8,10},{9,11},{10,... | collective-permute-start | bytes 393224 | tf_op jit(solution)/shard_map/ppermute | solution.py:38
  41.2 17.1 %collective-permute-start.18 = (f16[416,512]{1,0:T(8,128)(2,1)S(1)}, f16[416,512]{1,0:T(8,128)(2,1)S(1)}, u32[]{:S(2)}, u32[]{:S(2)}) collective-permute-start(f16[416,512]{1,0:T(8,128)(2,1)S(1)} %convolution_convert_fusion), channel_id=1, source_target_pairs={{0,2},{1,3},{2,0},{3,1},{4,6},{5,7},{6,4},{7,5},{8,10},{9,11},{10,... | collective-permute-start | bytes 1277960 | tf_op jit(solution)/shard_map/ppermute | solution.py:38
  43.4 10.9 %collective-permute-start.10 = (f32[64,512]{1,0:T(8,128)S(1)}, f32[64,512]{1,0:T(8,128)S(1)}, u32[]{:S(2)}, u32[]{:S(2)}) collective-permute-start(f32[64,512]{1,0:T(8,128)S(1)} %add.460), channel_id=1, source_target_pairs={{0,4},{1,5},{2,6},{3,7},{4,0},{5,1},{6,2},{7,3},{8,12},{9,13},{10,... | collective-permute-start | bytes 393224 | tf_op jit(solution)/shard_map/ppermute | solution.py:38
  44.0 24.0 %collective-permute-start.16 = (f16[416,512]{1,0:T(8,128)(2,1)S(1)}, f16[416,512]{1,0:T(8,128)(2,1)S(1)}, u32[]{:S(2)}, u32[]{:S(2)}) collective-permute-start(f16[416,512]{1,0:T(8,128)(2,1)S(1)} %convolution_convert_fusion.1), channel_id=1, source_target_pairs={{0,2},{1,3},{2,0},{3,1},{4,6},{5,7},{6,4},{7,5},{8,10},{9,11},{10,... | collective-permute-start | bytes 1277960 | tf_op jit(solution)/shard_map/ppermute | solution.py:38
  54.4 8.5 %collective-permute-start.11 = (f32[64,512]{1,0:T(8,128)S(1)}, f32[64,512]{1,0:T(8,128)S(1)}, u32[]{:S(2)}, u32[]{:S(2)}) collective-permute-start(f32[64,512]{1,0:T(8,128)S(1)} %add.461), channel_id=1, source_target_pairs={{0,16},{1,17},{2,18},{3,19},{4,20},{5,21},{6,22},{7,23},{8,24},{9,... | collective-permute-start | bytes 393224 | tf_op jit(solution)/shard_map/ppermute | solution.py:38
  56.8 6.1 %collective-permute-start.12 = (f32[64,512]{1,0:T(8,128)S(1)}, f32[64,512]{1,0:T(8,128)S(1)}, u32[]{:S(2)}, u32[]{:S(2)}) collective-permute-start(f32[64,512]{1,0:T(8,128)S(1)} %add.461), channel_id=1, source_target_pairs={{0,1},{1,0},{2,3},{3,2},{4,5},{5,4},{6,7},{7,6},{8,9},{9,8},{10,11... | collective-permute-start | bytes 393224 | tf_op jit(solution)/shard_map/ppermute | solution.py:38
  58.3 5.9 %collective-permute-start.13 = (f32[64,512]{1,0:T(8,128)S(1)}, f32[64,512]{1,0:T(8,128)S(1)}, u32[]{:S(2)}, u32[]{:S(2)}) collective-permute-start(f32[64,512]{1,0:T(8,128)S(1)} %add.461), channel_id=1, source_target_pairs={{0,17},{1,16},{2,19},{3,18},{4,21},{5,20},{6,23},{7,22},{8,25},{9,... | collective-permute-start | bytes 393224 | tf_op jit(solution)/shard_map/ppermute | solution.py:38
  58.3 19.1 %copy-start.4 = (bf16[416,256]{1,0:T(8,128)(2,1)S(1)}, bf16[416,256]{1,0:T(8,128)(2,1)}, u32[]{:S(2)}) copy-start(bf16[416,256]{1,0:T(8,128)(2,1)} %get-tuple-element.12) | copy-start | bytes 638980
  59.5 18.0 %collective-permute-start.19 = (f16[416,512]{1,0:T(8,128)(2,1)}, f16[416,512]{1,0:T(8,128)(2,1)}, u32[]{:S(2)}, u32[]{:S(2)}) collective-permute-start(f16[416,512]{1,0:T(8,128)(2,1)} %fusion.3), channel_id=1, source_target_pairs={{0,4},{1,5},{2,6},{3,7},{4,0},{5,1},{6,2},{7,3},{8,12},{9,13},{10,... | collective-permute-start | bytes 1277960 | tf_op jit(solution)/shard_map/ppermute | solution.py:38
  64.2 15.7 %collective-permute-start.14 = (f32[4,64,512]{2,1,0:T(8,128)S(1)}, f32[4,64,512]{2,1,0:T(8,128)S(1)}, u32[]{:S(2)}, u32[]{:S(2)}) collective-permute-start(f32[4,64,512]{2,1,0:T(8,128)S(1)} %pad_maximum_fusion.1), channel_id=1, source_target_pairs={{0,8},{1,9},{2,10},{3,11},{4,12},{5,13},{6,14},{7,15},{8,0},{9,1},... | collective-permute-start | bytes 1572872 | tf_op jit(solution)/shard_map/ppermute | solution.py:38
  (3 other events, 10.4 us)

commit v2 on v0

v2 whole, which is shorter than its diff:
```python
import functools

import jax
import jax.numpy as jnp
from jax import lax
from jax.experimental import pallas as pl
from jax.experimental.pallas import tpu as pltpu
from jax.sharding import PartitionSpec as P

BLK = 128
NS_ITERS = 3
CORES = 2
WIRE = jnp.float16
LANES = 128
ROW_TILE = 16
VMEM = pl.BlockSpec(memory_space=pltpu.VMEM)
SMEM = pl.BlockSpec(memory_space=pltpu.SMEM)
PARAMS = pltpu.CompilerParams(vmem_limit_bytes=40 * 2**20)


def inner_size(n):
    return max(d for d in range(1, n + 1) if n % d == 0 and d * d <= n)


class Grid:
    def __init__(self):
        self.gr = lax.axis_size("gr")
        self.gc = lax.axis_size("gc")
        self.cores = CORES if self.gr % CORES == 0 else 1
        self.xs = self.gr // self.cores
        self.ys = inner_size(self.gc)
        self.zs = self.gc // self.ys
        gr, gc = lax.axis_index("gr"), lax.axis_index("gc")
        self.x, self.core = gr // self.cores, gr % self.cores
        self.z, self.y = gc // self.ys, gc % self.ys
        self.gr_index, self.gc_index = gr, gc
        self.plane = [(a, b) for b in range(self.ys) for a in range(self.xs)]

    def swap(self, value, dx=0, dcore=0, dz=0, dy=0, sources=None):
        pairs = []
        for gr in range(self.gr):
            for gc in range(self.gc):
                if sources is not None and not sources(gr, gc):
                    continue
                to_gr = ((gr // self.cores) ^ dx) * self.cores + ((gr % self.cores) ^ dcore)
                to_gc = ((gc // self.ys) ^ dz) * self.ys + ((gc % self.ys) ^ dy)
                pairs.append((gr * self.gc + gc, to_gr * self.gc + to_gc))
        return lax.ppermute(value, ("gr", "gc"), pairs)


def rows_of(value, start, count):
    return lax.dynamic_slice_in_dim(value, start, count, axis=0)


def shape(rows, columns, dtype):
    return jax.ShapeDtypeStruct((rows, columns), dtype)


def below_skyline(part, first_row, first_of):
    row_ids = first_row + lax.broadcasted_iota(jnp.int32, (part.shape[0], 1), 0)
    kept = []
    for c in range(part.shape[1] // BLK):
        block = part[:, c * BLK : (c + 1) * BLK]
        kept.append(jnp.where(row_ids >= first_of(c) * BLK, block, jnp.zeros_like(block)))
    return jnp.concatenate(kept, axis=1)


def chunks_kernel(indices, base, first, window_ref, out_ref):
    rows = out_ref.shape[0]
    start = base[0] + indices[pl.program_id(0)] * rows
    out_ref[...] = below_skyline(window_ref[...], start, lambda c: first[c])


def masked_chunks(window, first_block, row_base, indices, rows):
    depth = window.shape[1]
    count = indices.shape[0]
    return pl.pallas_call(
        chunks_kernel,
        grid_spec=pltpu.PrefetchScalarGridSpec(
            num_scalar_prefetch=3,
            grid=(count,),
            in_specs=[pl.BlockSpec((rows, depth), lambda i, indices, base, first: (indices[i], 0))],
            out_specs=pl.BlockSpec((rows, depth), lambda i, indices, base, first: (i, 0)),
        ),
        out_shape=shape(count * rows, depth, window.dtype),
        cost_estimate=pl.CostEstimate(flops=0, bytes_accessed=4 * count * rows * depth, transcendentals=0),
        name="masked_chunks",
    )(indices, row_base[None], first_block, window)


def front_kernel(chip_rows, targets, starts, base, first, panel_ref, head_ref, *out_refs):
    depth, width = panel_ref.shape
    for n in range(targets):
        start = pl.multiple_of(starts[n], chip_rows)
        rows = below_skyline(head_ref[pl.ds(start, chip_rows), :], base[0] + start, lambda c: first[c])
        if n == 0:
            out_refs[0][...] = rows
            continue
        out_refs[n][:depth, :] = panel_ref[...]
        for h in range(depth // width):
            out_refs[n][depth + h * chip_rows : depth + (h + 1) * chip_rows, :] = rows[:, h * width : (h + 1) * width]


def front_pack(upper_panel, head, first_block, row_base, starts, chip_rows):
    depth, width = upper_panel.shape
    targets = starts.shape[0]
    packed = shape(depth + chip_rows * depth // width, width, head.dtype)
    return pl.pallas_call(
        functools.partial(front_kernel, chip_rows, targets),
        in_specs=[SMEM, SMEM, SMEM, VMEM, pl.BlockSpec(head.shape, lambda: (0, 0))],
        out_specs=[VMEM] * targets,
        out_shape=[shape(chip_rows, depth, head.dtype)] + [packed] * (targets - 1),
        name="front_pack",
    )(starts, row_base[None], first_block, upper_panel, head)


def chip_kernel(xs, ys, cores, place, panel_ref, rows_ref, *refs):
    arrived, (out_ref, mine_ref) = refs[:-2], refs[-2:]
    depth, width = panel_ref.shape
    chip_rows = rows_ref.shape[0]
    piece = chip_rows // cores
    halves = depth // width
    x = place[0]
    base = xs * ys * depth
    for b in range(ys):
        picked = [jnp.zeros((chip_rows, width), rows_ref.dtype)] * halves
        for a in range(xs):
            n = b * xs + a
            if n == 0:
                out_ref[:depth, :] = panel_ref[...]
                found = [rows_ref[:, h * width : (h + 1) * width] for h in range(halves)]
            else:
                got = arrived[n - 1]
                out_ref[n * depth : (n + 1) * depth, :] = got[:depth, :]
                found = [got[depth + h * chip_rows : depth + (h + 1) * chip_rows, :] for h in range(halves)]
            picked = [jnp.where(x == a, new, old) for new, old in zip(found, picked)]
        for h in range(halves):
            n = b * halves + h
            mine_ref[:, n * width : (n + 1) * width] = picked[h][:piece]
            if cores > 1:
                out_ref[base + n * piece : base + (n + 1) * piece, :] = picked[h][piece:]


def chip_pack(grid, place, upper_panel, own_rows, arrived):
    depth, width = upper_panel.shape
    chip_rows = own_rows.shape[0]
    piece = chip_rows // grid.cores
    span = grid.ys * depth
    rows = len(grid.plane) * depth + span // width * piece
    return pl.pallas_call(
        functools.partial(chip_kernel, grid.xs, grid.ys, grid.cores),
        in_specs=[SMEM] + [VMEM] * (2 + len(arrived)),
        out_specs=[VMEM, VMEM],
        out_shape=[shape(rows, width, upper_panel.dtype), shape(piece, span, upper_panel.dtype)],
        name="chip_pack",
    )(place, upper_panel, own_rows, *arrived)


def panel_kernel(xs, ys, cores, depth, place, rows_ref, *refs):
    packs, (panel_ref, update_ref) = refs[:-2], refs[-2:]
    width = packs[0].shape[1]
    piece = rows_ref.shape[0]
    x, core = place[0], place[1]
    for b in range(ys):
        for a in range(xs):
            n = b * xs + a
            for e in range(cores):
                gr = jnp.bitwise_xor(x, a) * cores + jnp.bitwise_xor(core, e)
                columns = pl.ds(pl.multiple_of(gr * width, width), width)
                panel_ref[b * depth : (b + 1) * depth, columns] = packs[e][n * depth : (n + 1) * depth, :]
    rows = rows_ref[...]
    if cores > 1:
        base = xs * ys * depth
        count = rows.shape[1] // width
        theirs = [packs[1][base + n * piece : base + (n + 1) * piece, :] for n in range(count)]
        rows = jnp.where(core == 0, rows, jnp.concatenate(theirs, axis=1))
    update_ref[...] = jnp.dot(rows, panel_ref[...], preferred_element_type=jnp.float32)


def panel_assemble(grid, place, depth, rows, packs):
    width = packs[0].shape[1]
    total = grid.gr * width
    return pl.pallas_call(
        functools.partial(panel_kernel, grid.xs, grid.ys, grid.cores, depth),
        in_specs=[SMEM] + [VMEM] * (1 + len(packs)),
        out_specs=[VMEM, VMEM],
        out_shape=[shape(grid.ys * depth, total, rows.dtype), shape(rows.shape[0], total, jnp.float32)],
        name="panel_assemble",
    )(place, rows, *packs)


def two_parts(value):
    high = value.astype(jnp.bfloat16)
    return high, (value - high.astype(jnp.float32)).astype(jnp.bfloat16)


def product(left, right):
    dot = functools.partial(jnp.dot, preferred_element_type=jnp.float32)
    return dot(left[0], right[0]) + (dot(left[0], right[1]) + dot(left[1], right[0]))


def inverse_kernel(xs, ys, cores, place, *refs):
    stacks, (high_ref, low_ref, scale_ref, pivot_ref) = refs[:cores], refs[cores:]
    piece = stacks[0].shape[0] // (xs * ys)
    x, core, y = place[0], place[1], place[2]
    for b in range(ys):
        for a in range(xs):
            n = b * xs + a
            chip = jnp.bitwise_xor(y, b) * xs + jnp.bitwise_xor(x, a)
            for e in range(cores):
                start = (chip * cores + jnp.bitwise_xor(core, e)) * piece
                pivot_ref[pl.ds(pl.multiple_of(start, piece), piece), :] = stacks[e][n * piece : (n + 1) * piece, :]
    order = pivot_ref.shape[0]
    square = (order, order)
    diagonal = lax.broadcasted_iota(jnp.int32, square, 0) == lax.broadcasted_iota(jnp.int32, square, 1)
    pivot = pivot_ref[...]
    scale = jnp.sum(jnp.where(diagonal, pivot, 0.0)) / order
    power = jnp.where(diagonal, 1.0, 0.0) - pivot / scale
    rest = power
    parts = two_parts(power)
    for step in range(NS_ITERS - 1):
        power = product(parts, parts)
        parts = two_parts(power)
        rest = rest + power + product(two_parts(rest), parts)
    high_ref[...], low_ref[...] = two_parts(rest)
    scale_ref[0] = scale


def inverse_rest(grid, place, stacks):
    order = stacks[0].shape[1]
    half = shape(order, order, jnp.bfloat16)
    return pl.pallas_call(
        functools.partial(inverse_kernel, grid.xs, grid.ys, grid.cores),
        in_specs=[SMEM] + [VMEM] * len(stacks),
        out_specs=[VMEM, VMEM, SMEM],
        out_shape=[half, half, jax.ShapeDtypeStruct((1,), jnp.float32)],
        scratch_shapes=[pltpu.VMEM((order, order), jnp.float32)],
        compiler_params=PARAMS,
        cost_estimate=pl.CostEstimate(flops=24 * order**3, bytes_accessed=8 * order**2, transcendentals=0),
        name="pivot_inverse",
    )(place, *stacks)


def factor_kernel(start_ref, scale_ref, schur_ref, high_ref, low_ref, out_ref):
    rows, order = out_ref.shape
    schur = schur_ref[...]
    rest = high_ref[...], low_ref[...]
    out_ref[...] = (schur + product(two_parts(schur), rest)) / scale_ref[0]
    start = start_ref[0]

    @pl.when(start < order)
    def _():
        here = start + lax.broadcasted_iota(jnp.int32, (rows, order), 0)
        across = lax.broadcasted_iota(jnp.int32, (rows, order), 1)
        pick = jnp.where(here == across, 1.0, 0.0).astype(jnp.bfloat16)
        dot = functools.partial(jnp.dot, preferred_element_type=jnp.float32)
        inverse = pick.astype(jnp.float32) + (dot(pick, rest[0]) + dot(pick, rest[1]))
        out_ref[...] = jnp.where(here < order, inverse, out_ref[...])


def factor_rows(global_start, scale, schur, high, low):
    rows, order = schur.shape
    return pl.pallas_call(
        factor_kernel,
        in_specs=[SMEM, SMEM, VMEM, VMEM, VMEM],
        out_specs=VMEM,
        out_shape=shape(rows, order, jnp.float32),
        compiler_params=PARAMS,
        name="factor_rows",
    )(global_start[None], scale, schur, high, low)


def masked_rows(window, first_block, row_base, start, count):
    col_first = jnp.repeat(first_block, BLK)
    row_ids = row_base + start + jnp.arange(count, dtype=jnp.int32)
    inside = (row_ids // BLK)[:, None] >= col_first[None, :]
    part = rows_of(window, start, count)
    return jnp.where(inside, part, jnp.zeros_like(part))


def plain_front_pack(upper_panel, head, first_block, row_base, starts, chip_rows):
    depth, width = upper_panel.shape
    out = []
    for n in range(starts.shape[0]):
        rows = masked_rows(head, first_block, row_base, starts[n], chip_rows)
        out.append(rows if n == 0 else jnp.concatenate([upper_panel] + jnp.split(rows, depth // width, axis=1), axis=0))
    return out


def plain_chip_pack(grid, place, upper_panel, own_rows, arrived):
    depth, width = upper_panel.shape
    chip_rows = own_rows.shape[0]
    piece = chip_rows // grid.cores
    halves = depth // width
    rows = [jnp.concatenate(jnp.split(own_rows, halves, axis=1), axis=0)] + [got[depth:] for got in arrived]
    shards = [upper_panel] + [got[:depth] for got in arrived]
    mine, theirs = [], []
    for b in range(grid.ys):
        stack = jnp.stack(rows[b * grid.xs : (b + 1) * grid.xs])
        picked = lax.dynamic_index_in_dim(stack, grid.x, 0, keepdims=False).reshape(halves, chip_rows, width)
        mine += [picked[h, :piece] for h in range(halves)]
        theirs += [picked[h, piece:] for h in range(halves)]
    return jnp.concatenate(shards + theirs, axis=0), jnp.concatenate(mine, axis=1)


def plain_panel_assemble(grid, place, depth, rows, packs):
    width = packs[0].shape[1]
    count = len(grid.plane)
    stack = jnp.stack([pack[: count * depth].reshape(count, depth, width) for pack in packs])
    bands = []
    for b in range(grid.ys):
        bands.append(
            jnp.concatenate(
                [stack[grid.core ^ (gr % grid.cores), b * grid.xs + (grid.x ^ (gr // grid.cores))] for gr in range(grid.gr)], axis=1
            )
        )
    panel = jnp.concatenate(bands, axis=0)
    if grid.cores > 1:
        theirs = packs[1][count * depth :].reshape(-1, rows.shape[0], width)
        rows = jnp.where(grid.core == 0, rows, jnp.concatenate(list(theirs), axis=1))
    return panel, jnp.dot(rows, panel, preferred_element_type=jnp.float32)


def body(factor_window, upper_panel, panel_block, first_block):
    grid = Grid()
    local_rows, depth = factor_window.shape
    own_rows, panel_width = panel_block.shape
    width = upper_panel.shape[1]
    row_base = grid.gr_index * local_rows
    global_start = (grid.gr_index * grid.gc + grid.gc_index) * own_rows
    place = jnp.stack([grid.x, grid.core, grid.y])
    piece = panel_width // (grid.gr * grid.ys)
    chip_rows = piece * grid.cores
    whole_tiles = width % LANES == 0 and piece % ROW_TILE == 0
    whole_chunks = own_rows % ROW_TILE == 0

    def chip_start(a, b):
        return ((grid.y ^ b) * grid.xs + (grid.x ^ a)) * chip_rows

    starts = jnp.stack([chip_start(a, b) for a, b in grid.plane])
    head = factor_window[:panel_width]
    steps = (front_pack, chip_pack, panel_assemble) if whole_tiles else (plain_front_pack, plain_chip_pack, plain_panel_assemble)

    own_pivot, *packed = steps[0](upper_panel, head, first_block, row_base, starts, chip_rows)
    arrived = [grid.swap(pack, dx=a, dy=b) for pack, (a, b) in zip(packed, grid.plane[1:])]

    order = list(range(grid.zs - 1, -1, -1))

    def chunks(ks, j):
        indices = jnp.stack([(grid.z ^ k) * grid.ys + (grid.y ^ j) for k in ks])
        if whole_chunks:
            return masked_chunks(factor_window, first_block, row_base, indices, own_rows)
        parts = [masked_rows(factor_window, first_block, row_base, i * own_rows, own_rows) for i in indices]
        return jnp.concatenate(parts, axis=0)

    columns = {}
    for ks in ([order[0]], order[1:]):
        if not ks:
            continue
        bands = [grid.swap(chunks(ks, j), dy=j) for j in range(1, grid.ys)]
        bands = [chunks(ks, 0)] + bands
        for n, k in enumerate(ks):
            columns[k] = [band[n * own_rows : (n + 1) * own_rows] for band in bands]

    pack, mine = steps[1](grid, place, upper_panel, own_pivot, arrived)
    packs = [pack] + ([grid.swap(pack, dcore=1)] if grid.cores > 1 else [])
    panel, pivot_update = steps[2](grid, place, depth, mine, packs)

    def holds(gr, gc):
        return gr == 0 and gc * own_rows < panel_width

    padded = jnp.zeros((panel_width + own_rows, panel_width), jnp.float32)
    padded = lax.dynamic_update_slice_in_dim(padded, panel_block, jnp.minimum(global_start, panel_width), axis=0)
    before = jnp.where(grid.gr_index == 0, rows_of(padded, starts[0], chip_rows), 0.0)
    for n, (a, b) in enumerate(grid.plane):
        if n:
            before = before + grid.swap(rows_of(padded, starts[n], chip_rows), dx=a, dy=b, sources=holds)
    if grid.cores > 1:
        others = grid.swap(before[piece:], dcore=1, sources=lambda gr, gc: gr % grid.cores == 0)
        before = jnp.where(grid.core == 0, before[:piece], others)

    total = before - pivot_update
    step = 1
    while step < grid.zs:
        total = total + grid.swap(total, dz=step)
        step *= 2
    stack = jnp.concatenate([total] + [grid.swap(total, dx=a, dy=b) for a, b in grid.plane[1:]], axis=0)
    stacks = [stack] + ([grid.swap(stack, dcore=1)] if grid.cores > 1 else [])
    high, low, scale = inverse_rest(grid, place, stacks)

    sums = {}
    for k in order:
        bands = [panel[j * depth : (j + 1) * depth] for j in range(grid.ys)]
        parts = [jnp.dot(part, band, preferred_element_type=jnp.float32) for part, band in zip(columns[k], bands)]
        sums[k] = sum(parts[1:], parts[0])
    step = 1
    while step < grid.zs:
        for k in sorted((k for k in sums if k & step), reverse=True):
            got = grid.swap(sums.pop(k).astype(WIRE), dz=step)
            sums[k ^ step] = sums[k ^ step] + got.astype(jnp.float32)
        step *= 2
    schur_rows = panel_block - sums[0]
    return factor_rows(global_start, scale, schur_rows, high, low)


def solution(mesh):
    return jax.shard_map(
        body,
        mesh=mesh,
        in_specs=(P("gr", "gc"), P("gc", "gr"), P(("gr", "gc"), None), P("gc")),
        out_specs=P(("gr", "gc"), None),
        check_vma=False,
    )
```

time: 311 us -> 96 us (0.31)
  waiting for transfers between devices: 256 us -> 31.6 us
  starting transfers between devices: 0.04 us -> 26.2 us
  Pallas kernels: 0 us -> 25.1 us
  matrix products: 17.3 us -> 3.16 us
  between operations: 14.2 us -> 0.35 us
  local copies, waits for them, and re-layouts: 12 us -> 4.38 us
  blocking collectives: 7.54 us -> 0 us
    psum x1 -> x0, waiting for transfers between devices: 130 us -> none  [body(): pivot_block = lax.psum(pivot_term, ('gr', 'gc'))]
    reduce_scatter x1 -> x0, waiting for transfers between devices: 127 us -> none  [body(): lax.psum_scatter(jnp.dot(masked_rows(factor_window, row_base, col_first),...]
    ppermute x0 -> x19, waiting for transfers between devices: none -> 31.6 us  [swap(): return lax.ppermute(value, ('gr', 'gc'), pairs)]
    ppermute x0 -> x19, starting transfers between devices: none -> 26.2 us  [swap(): return lax.ppermute(value, ('gr', 'gc'), pairs)]
    pallas_call x0 -> x9, Pallas kernels: none -> 25.1 us  [the longest x4 11.9 us: masked_chunks(): pl.pallas_call(chunks_kernel, grid_spec=pltpu.PrefetchScalarGridSpec(num_...]
    dot_general x8, matrix products: 17.3 us -> 3.16 us  [body(): jnp.dot(part, band, preferred_element_type=jnp.float32)]
    gather x3 -> x0, local copies, waits for them, and re-layouts: 11.9 us -> none  [the longest x1 8.61 us: body(): pivot_scale = jnp.mean(jnp.diagonal(pivot_block))]
    all_gather x1 -> x0, blocking collectives: 7.54 us -> none  [body(): whole_panel = lax.all_gather(upper_panel, 'gr', axis=1, tiled=True)]
  transfers between devices with their start and end apart: 2 -> 19, of which waited for: 2 -> 5; matrix products, arithmetic and copies ran while one was open for 0% -> 9% of each run, Pallas kernels for 0% -> 17%
where the time goes in v2:
time: 96 us; the launch traced here: 95.4 us
  waiting for transfers between devices  31.6 us (33%)
  starting transfers between devices  26.2 us (27%)
  Pallas kernels  25.1 us (26%)
  other arithmetic  4.67 us (5%)
  local copies, waits for them, and re-layouts  4.38 us (5%)
  matrix products  3.16 us (3%)
    ppermute x19, waiting for transfers between devices, swap(): return lax.ppermute(value, ('gr', 'gc'), pairs)  31.6 us
    ppermute x19, starting transfers between devices, swap(): return lax.ppermute(value, ('gr', 'gc'), pairs)  26.2 us
    pallas_call x4, Pallas kernels, masked_chunks(): pl.pallas_call(chunks_kernel, grid_spec=pltpu.PrefetchScalarGridSpec(num_...  11.9 us
    pallas_call x1, Pallas kernels, inverse_rest(): pl.pallas_call(functools.partial(inverse_kernel, grid.xs, grid.ys, grid.c...  4.55 us
    dot_general x8, matrix products, body(): jnp.dot(part, band, preferred_element_type=jnp.float32)  3.16 us
    pallas_call x1, Pallas kernels, factor_rows(): pl.pallas_call(factor_kernel, in_specs=[SMEM, SMEM, VMEM, VMEM, VMEM], ou...  2.93 us
    pallas_call x1, Pallas kernels, panel_assemble(): pl.pallas_call(functools.partial(panel_kernel, grid.xs, grid.ys, grid.cor...  2.07 us
  transfers between devices with their start and end apart: 19, of which 5 were waited for; matrix products, arithmetic and copies ran while one was open for 9% of the time, Pallas kernels for 17%

profile of v2, /device:TPU:0, one launch (start us, length us, event | category | flops | bytes accessed | tf_op | source)
XLA Modules:
  0.0 95.4 jit_solution(14137774683537530200)
XLA Ops:
  0.0 1.7 %slice.41.head_ref = bf16[512,256]{1,0:T(8,128)(2,1)} slice(bf16[3328,256]{1,0:T(8,128)(2,1)} %window_ref.7), slice={[0:512], [0:256]} | slice | bytes 524288 | tf_op jit(solution)/shard_map/slice | solution.py:341
  2.4 1.8 %front_pack.1 = (bf16[128,256]{1,0:T(8,128)(2,1)}, bf16[512,128]{1,0:T(8,128)(2,1)}, bf16[512,128]{1,0:T(8,128)(2,1)}, bf16[512,128]{1,0:T(8,128)(2,1)}) custom-call(s32[4]{0:T(128)} %pad_add_fusion.1.starts, s32[1]{0:T(128)} %bitcast.8.base, s32[2]{0:T(128)} %first.9, bf16[256,128]{1,0:T(8,128)(2,1)} %panel_ref.3, bf16[512,256]{1,0:T(8,128)(2,1)} %slice.41.head_ref), custom_call_target="tpu_custom_call" | custom-call | tf_op jit(solution)/shard_map/front_pack/pallas_call | solution.py:108
  4.2 2.9 %collective-permute-start.4 = (bf16[512,128]{1,0:T(8,128)(2,1)}, bf16[512,128]{1,0:T(8,128)(2,1)S(1)}, u32[]{:S(2)}, u32[]{:S(2)}) collective-permute-start(bf16[512,128]{1,0:T(8,128)(2,1)} %get-tuple-element.17), channel_id=1, source_target_pairs={{0,16},{1,17},{2,18},{3,19},{4,20},{5,21},{6,22},{7,23},{8,24},{9,... | collective-permute-start | bytes 393224 | tf_op jit(solution)/shard_map/ppermute | solution.py:48
  9.0 2.6 %collective-permute-start = (f32[128,512]{1,0:T(8,128)}, f32[128,512]{1,0:T(8,128)}, u32[]{:S(2)}, u32[]{:S(2)}) collective-permute-start(f32[128,512]{1,0:T(8,128)} %get-tuple-element.27), channel_id=1, source_target_pairs={{0,16},{1,17}} | collective-permute-start | bytes 786440 | tf_op jit(solution)/shard_map/ppermute | solution.py:48
  11.7 2.8 %collective-permute-start.2 = (f32[128,512]{1,0:T(8,128)}, f32[128,512]{1,0:T(8,128)}, u32[]{:S(2)}, u32[]{:S(2)}) collective-permute-start(f32[128,512]{1,0:T(8,128)} %get-tuple-element.28), channel_id=1, source_target_pairs={{0,17},{1,16}} | collective-permute-start | bytes 786440 | tf_op jit(solution)/shard_map/ppermute | solution.py:48
  14.4 3.2 %collective-permute-start.1 = (f32[128,512]{1,0:T(8,128)S(1)}, f32[128,512]{1,0:T(8,128)}, u32[]{:S(2)}, u32[]{:S(2)}) collective-permute-start(f32[128,512]{1,0:T(8,128)S(1)} %get-tuple-element.29), channel_id=1, source_target_pairs={{0,1},{1,0}} | collective-permute-start | bytes 786440 | tf_op jit(solution)/shard_map/ppermute | solution.py:48
  18.5 2.3 %masked_chunks.7 = bf16[416,256]{1,0:T(8,128)(2,1)} custom-call(s32[1]{0:T(128)} %bitcast.16.indices, s32[1]{0:T(128)} %bitcast.8.base, s32[2]{0:T(128)} %first.9, bf16[3328,256]{1,0:T(8,128)(2,1)} %window_ref.7), custom_call_target="tpu_custom_call" | custom-call | bytes 425984 | tf_op jit(solution)/shard_map/masked_chunks/pallas_call | solution.py:77
  21.4 6.2 %collective-permute-done.5.refs_1_ = bf16[512,128]{1,0:T(8,128)(2,1)S(1)} collective-permute-done((bf16[512,128]{1,0:T(8,128)(2,1)S(1)}, bf16[512,128]{1,0:T(8,128)(2,1)S(1)}, u32[]{:S(2)}, u32[]{:S(2)}) %collective-permute-start.5) | collective-permute-done | bytes 131104 | tf_op jit(solution)/shard_map/ppermute | solution.py:48
  29.1 1.9 %chip_pack.1 = (bf16[1280,128]{1,0:T(8,128)(2,1)}, bf16[64,512]{1,0:T(8,128)(2,1)}) custom-call(s32[3]{0:T(128)} %pad_add_fusion.place, bf16[256,128]{1,0:T(8,128)(2,1)} %panel_ref.3, bf16[128,256]{1,0:T(8,128)(2,1)} %get-tuple-element.16.rows_ref, bf16[512,128]{1,0:T(8,128)(2,1)} %copy-done.6, bf16[512,128]{1,0:T(8,128)(2,1)} %copy-done.7, ...), custom_call_target="tpu_custom_call" | custom-call | tf_op jit(solution)/shard_map/chip_pack/pallas_call | solution.py:150
  32.2 2.4 %collective-permute-start.3 = (f32[64,512]{1,0:T(8,128)S(1)}, f32[64,512]{1,0:T(8,128)S(1)}, u32[]{:S(2)}, u32[]{:S(2)}) collective-permute-start(f32[64,512]{1,0:T(8,128)S(1)} %slice.51), channel_id=1, source_target_pairs={{0,8},{1,9},{2,10},{3,11},{4,12},{5,13},{6,14},{7,15},{16,24},{17,... | collective-permute-start | bytes 393224 | tf_op jit(solution)/shard_map/ppermute | solution.py:48
  35.2 3.5 %masked_chunks.5 = bf16[1248,256]{1,0:T(8,128)(2,1)} custom-call(s32[3]{0:T(128)} %pad_add_fusion.3.indices, s32[1]{0:T(128)} %bitcast.8.base, s32[2]{0:T(128)} %first.9, bf16[3328,256]{1,0:T(8,128)(2,1)} %window_ref.7), custom_call_target="tpu_custom_call" | custom-call | bytes 1277952 | tf_op jit(solution)/shard_map/masked_chunks/pallas_call | solution.py:77
  39.4 2.3 %masked_chunks.6 = bf16[416,256]{1,0:T(8,128)(2,1)} custom-call(s32[1]{0:T(128)} %bitcast.15.indices, s32[1]{0:T(128)} %bitcast.8.base, s32[2]{0:T(128)} %first.9, bf16[3328,256]{1,0:T(8,128)(2,1)} %window_ref.7), custom_call_target="tpu_custom_call" | custom-call | bytes 425984 | tf_op jit(solution)/shard_map/masked_chunks/pallas_call | solution.py:77
  42.3 3.7 %masked_chunks.4 = bf16[1248,256]{1,0:T(8,128)(2,1)} custom-call(s32[3]{0:T(128)} %pad_add_fusion.2.indices, s32[1]{0:T(128)} %bitcast.8.base, s32[2]{0:T(128)} %first.9, bf16[3328,256]{1,0:T(8,128)(2,1)} %window_ref.7), custom_call_target="tpu_custom_call" | custom-call | bytes 1277952 | tf_op jit(solution)/shard_map/masked_chunks/pallas_call | solution.py:77
  46.7 2.1 %panel_assemble.1 = (bf16[512,512]{1,0:T(8,128)(2,1)}, f32[64,512]{1,0:T(8,128)}) custom-call(s32[3]{0:T(128)} %pad_add_fusion.place, bf16[64,512]{1,0:T(8,128)(2,1)} %get-tuple-element.20.rows_ref, bf16[1280,128]{1,0:T(8,128)(2,1)} %get-tuple-element.21.refs_0_, bf16[1280,128]{1,0:T(8,128)(2,1)} %copy-done.5), custom_call_target="tpu_custom_call" | custom-call | tf_op jit(solution)/shard_map/panel_assemble/pallas_call | solution.py:183
  51.4 2.1 %collective-permute-start.17 = (f16[416,512]{1,0:T(8,128)(2,1)S(1)}, f16[416,512]{1,0:T(8,128)(2,1)S(1)}, u32[]{:S(2)}, u32[]{:S(2)}) collective-permute-start(f16[416,512]{1,0:T(8,128)(2,1)S(1)} %fusion.6), channel_id=1, source_target_pairs={{0,2},{1,3},{2,0},{3,1},{4,6},{5,7},{6,4},{7,5},{8,10},{9,11},{10,... | collective-permute-start | bytes 1277960 | tf_op jit(solution)/shard_map/ppermute | solution.py:48
  53.5 2.7 %collective-permute-done.8 = f32[64,512]{1,0:T(8,128)S(1)} collective-permute-done((f32[64,512]{1,0:T(8,128)S(1)}, f32[64,512]{1,0:T(8,128)S(1)}, u32[]{:S(2)}, u32[]{:S(2)}) %collective-permute-start.8) | collective-permute-done | bytes 131104 | tf_op jit(solution)/shard_map/ppermute | solution.py:48
  57.3 9.3 %collective-permute-done.9 = f32[64,512]{1,0:T(8,128)S(1)} collective-permute-done((f32[64,512]{1,0:T(8,128)S(1)}, f32[64,512]{1,0:T(8,128)S(1)}, u32[]{:S(2)}, u32[]{:S(2)}) %collective-permute-start.9) | collective-permute-done | bytes 131104 | tf_op jit(solution)/shard_map/ppermute | solution.py:48
  66.7 1.4 %collective-permute-start.11 = (f32[64,512]{1,0:T(8,128)S(1)}, f32[64,512]{1,0:T(8,128)S(1)}, u32[]{:S(2)}, u32[]{:S(2)}) collective-permute-start(f32[64,512]{1,0:T(8,128)S(1)} %add.115), channel_id=1, source_target_pairs={{0,1},{1,0},{2,3},{3,2},{4,5},{5,4},{6,7},{7,6},{8,9},{9,8},{10,11... | collective-permute-start | bytes 393224 | tf_op jit(solution)/shard_map/ppermute | solution.py:48
  68.1 2.0 %collective-permute-start.10 = (f32[64,512]{1,0:T(8,128)S(1)}, f32[64,512]{1,0:T(8,128)S(1)}, u32[]{:S(2)}, u32[]{:S(2)}) collective-permute-start(f32[64,512]{1,0:T(8,128)S(1)} %add.115), channel_id=1, source_target_pairs={{0,16},{1,17},{2,18},{3,19},{4,20},{5,21},{6,22},{7,23},{8,24},{9,... | collective-permute-start | bytes 393224 | tf_op jit(solution)/shard_map/ppermute | solution.py:48
  70.4 3.4 %collective-permute-start.18 = (f16[416,512]{1,0:T(8,128)(2,1)S(1)}, f16[416,512]{1,0:T(8,128)(2,1)S(1)}, u32[]{:S(2)}, u32[]{:S(2)}) collective-permute-start(f16[416,512]{1,0:T(8,128)(2,1)S(1)} %fusion.4), channel_id=1, source_target_pairs={{0,4},{1,5},{2,6},{3,7},{4,0},{5,1},{6,2},{7,3},{8,12},{9,13},{10,... | collective-permute-start | bytes 1277960 | tf_op jit(solution)/shard_map/ppermute | solution.py:48
  74.3 4.4 %collective-permute-done.15 = f16[416,512]{1,0:T(8,128)(2,1)S(1)} collective-permute-done((f16[416,512]{1,0:T(8,128)(2,1)S(1)}, f16[416,512]{1,0:T(8,128)(2,1)S(1)}, u32[]{:S(2)}, u32[]{:S(2)}) %collective-permute-start.15) | collective-permute-done | bytes 426016 | tf_op jit(solution)/shard_map/ppermute | solution.py:48
  78.7 8.9 %collective-permute-done.18 = f16[416,512]{1,0:T(8,128)(2,1)S(1)} collective-permute-done((f16[416,512]{1,0:T(8,128)(2,1)S(1)}, f16[416,512]{1,0:T(8,128)(2,1)S(1)}, u32[]{:S(2)}, u32[]{:S(2)}) %collective-permute-start.18) | collective-permute-done | bytes 426016 | tf_op jit(solution)/shard_map/ppermute | solution.py:48
  87.9 4.6 %pivot_inverse.1 = (bf16[512,512]{1,0:T(8,128)(2,1)S(1)}, bf16[512,512]{1,0:T(8,128)(2,1)S(1)}, f32[1]{0:T(128)}) custom-call(s32[3]{0:T(128)S(1)} %copy-done, f32[256,512]{1,0:T(8,128)S(1)} %pad_maximum_fusion.refs_0_, f32[256,512]{1,0:T(8,128)S(1)} %collective-permute-done.13.refs_1_), custom_call_target="tpu_custom_call" | custom-call | flops 3221225472 | bytes 2097152 | tf_op jit(solution)/shard_map/pivot_inverse/pallas_call | solution.py:232
  92.5 2.9 %factor_rows.1 = f32[416,512]{1,0:T(8,128)} custom-call(s32[1]{0:T(128)} %bitcast.start_ref, f32[1]{0:T(128)} %get-tuple-element.23.scale_ref, f32[416,512]{1,0:T(8,128)S(1)} %fusion.2.schur_ref, bf16[512,512]{1,0:T(8,128)(2,1)S(1)} %get-tuple-element.25.high_ref, bf16[512,512]{1,0:T(8,128)(2,1)S(1)} %get-tuple-element.26.low_ref), custom_call_target="tpu_custom_call" | custom-call | tf_op jit(solution)/shard_map/factor_rows/pallas_call | solution.py:263
  (63 shorter events, 13.7 us)
Async XLA Ops:
  0.0 7.4 %copy-start.2 = (f32[416,512]{1,0:T(8,128)S(1)}, f32[416,512]{1,0:T(8,128)}, u32[]{:S(2)}) copy-start(f32[416,512]{1,0:T(8,128)} %param.6) | copy-start | bytes 2555908
  4.2 14.2 %collective-permute-start.4 = (bf16[512,128]{1,0:T(8,128)(2,1)}, bf16[512,128]{1,0:T(8,128)(2,1)S(1)}, u32[]{:S(2)}, u32[]{:S(2)}) collective-permute-start(bf16[512,128]{1,0:T(8,128)(2,1)} %get-tuple-element.17), channel_id=1, source_target_pairs={{0,16},{1,17},{2,18},{3,19},{4,20},{5,21},{6,22},{7,23},{8,24},{9,... | collective-permute-start | bytes 393224 | tf_op jit(solution)/shard_map/ppermute | solution.py:48
  7.4 10.2 %copy-start.8 = (bf16[512,128]{1,0:T(8,128)(2,1)S(1)}, bf16[512,128]{1,0:T(8,128)(2,1)}, u32[]{:S(2)}) copy-start(bf16[512,128]{1,0:T(8,128)(2,1)} %get-tuple-element.18) | copy-start | bytes 393220
  9.0 22.0 %collective-permute-start = (f32[128,512]{1,0:T(8,128)}, f32[128,512]{1,0:T(8,128)}, u32[]{:S(2)}, u32[]{:S(2)}) collective-permute-start(f32[128,512]{1,0:T(8,128)} %get-tuple-element.27), channel_id=1, source_target_pairs={{0,16},{1,17}} | collective-permute-start | bytes 786440 | tf_op jit(solution)/shard_map/ppermute | solution.py:48
  11.7 19.3 %collective-permute-start.2 = (f32[128,512]{1,0:T(8,128)}, f32[128,512]{1,0:T(8,128)}, u32[]{:S(2)}, u32[]{:S(2)}) collective-permute-start(f32[128,512]{1,0:T(8,128)} %get-tuple-element.28), channel_id=1, source_target_pairs={{0,17},{1,16}} | collective-permute-start | bytes 786440 | tf_op jit(solution)/shard_map/ppermute | solution.py:48
  14.4 16.6 %collective-permute-start.1 = (f32[128,512]{1,0:T(8,128)S(1)}, f32[128,512]{1,0:T(8,128)}, u32[]{:S(2)}, u32[]{:S(2)}) collective-permute-start(f32[128,512]{1,0:T(8,128)S(1)} %get-tuple-element.29), channel_id=1, source_target_pairs={{0,1},{1,0}} | collective-permute-start | bytes 786440 | tf_op jit(solution)/shard_map/ppermute | solution.py:48
  17.6 10.0 %collective-permute-start.5 = (bf16[512,128]{1,0:T(8,128)(2,1)S(1)}, bf16[512,128]{1,0:T(8,128)(2,1)S(1)}, u32[]{:S(2)}, u32[]{:S(2)}) collective-permute-start(bf16[512,128]{1,0:T(8,128)(2,1)S(1)} %copy-done.8), channel_id=1, source_target_pairs={{0,1},{1,0},{2,3},{3,2},{4,5},{5,4},{6,7},{7,6},{8,9},{9,8},{10,11... | collective-permute-start | bytes 393224 | tf_op jit(solution)/shard_map/ppermute | solution.py:48
  18.4 10.6 %copy-start.6 = (bf16[512,128]{1,0:T(8,128)(2,1)}, bf16[512,128]{1,0:T(8,128)(2,1)S(1)}, u32[]{:S(2)}) copy-start(bf16[512,128]{1,0:T(8,128)(2,1)S(1)} %collective-permute-done.4.refs_0_) | copy-start | bytes 393220
  18.4 10.6 %collective-permute-start.6 = (bf16[512,128]{1,0:T(8,128)(2,1)}, bf16[512,128]{1,0:T(8,128)(2,1)}, u32[]{:S(2)}, u32[]{:S(2)}) collective-permute-start(bf16[512,128]{1,0:T(8,128)(2,1)} %get-tuple-element.19), channel_id=1, source_target_pairs={{0,17},{1,16},{2,19},{3,18},{4,21},{5,20},{6,23},{7,22},{8,25},{9,... | collective-permute-start | bytes 393224 | tf_op jit(solution)/shard_map/ppermute | solution.py:48
  27.6 22.2 %collective-permute-start.16 = (bf16[416,256]{1,0:T(8,128)(2,1)}, bf16[416,256]{1,0:T(8,128)(2,1)S(1)}, u32[]{:S(2)}, u32[]{:S(2)}) collective-permute-start(bf16[416,256]{1,0:T(8,128)(2,1)} %masked_chunks.7), channel_id=1, source_target_pairs={{0,1},{1,0},{2,3},{3,2},{4,5},{5,4},{6,7},{7,6},{8,9},{9,8},{10,11... | collective-permute-start | bytes 638984 | tf_op jit(solution)/shard_map/ppermute | solution.py:48
  31.0 15.0 %collective-permute-start.7 = (bf16[1280,128]{1,0:T(8,128)(2,1)}, bf16[1280,128]{1,0:T(8,128)(2,1)S(1)}, u32[]{:S(2)}, u32[]{:S(2)}) collective-permute-start(bf16[1280,128]{1,0:T(8,128)(2,1)} %get-tuple-element.21.refs_0_), channel_id=1, source_target_pairs={{0,8},{1,9},{2,10},{3,11},{4,12},{5,13},{6,14},{7,15},{8,0},{9,1},... | collective-permute-start | bytes 983048 | tf_op jit(solution)/shard_map/ppermute | solution.py:48
  32.2 16.6 %collective-permute-start.3 = (f32[64,512]{1,0:T(8,128)S(1)}, f32[64,512]{1,0:T(8,128)S(1)}, u32[]{:S(2)}, u32[]{:S(2)}) collective-permute-start(f32[64,512]{1,0:T(8,128)S(1)} %slice.51), channel_id=1, source_target_pairs={{0,8},{1,9},{2,10},{3,11},{4,12},{5,13},{6,14},{7,15},{16,24},{17,... | collective-permute-start | bytes 393224 | tf_op jit(solution)/shard_map/ppermute | solution.py:48
  38.8 17.5 %collective-permute-start.14 = (bf16[1248,256]{1,0:T(8,128)(2,1)}, bf16[1248,256]{1,0:T(8,128)(2,1)S(1)}, u32[]{:S(2)}, u32[]{:S(2)}) collective-permute-start(bf16[1248,256]{1,0:T(8,128)(2,1)} %masked_chunks.5), channel_id=1, source_target_pairs={{0,1},{1,0},{2,3},{3,2},{4,5},{5,4},{6,7},{7,6},{8,9},{9,8},{10,11... | collective-permute-start | bytes 1916936 | tf_op jit(solution)/shard_map/ppermute | solution.py:48
  42.3 8.8 %copy-start.4 = (bf16[416,256]{1,0:T(8,128)(2,1)S(1)}, bf16[416,256]{1,0:T(8,128)(2,1)}, u32[]{:S(2)}) copy-start(bf16[416,256]{1,0:T(8,128)(2,1)} %masked_chunks.6) | copy-start | bytes 638980
  49.8 6.4 %collective-permute-start.8 = (f32[64,512]{1,0:T(8,128)S(1)}, f32[64,512]{1,0:T(8,128)S(1)}, u32[]{:S(2)}, u32[]{:S(2)}) collective-permute-start(f32[64,512]{1,0:T(8,128)S(1)} %fusion.25), channel_id=1, source_target_pairs={{0,2},{1,3},{2,0},{3,1},{4,6},{5,7},{6,4},{7,5},{8,10},{9,11},{10,... | collective-permute-start | bytes 393224 | tf_op jit(solution)/shard_map/ppermute | solution.py:48
  51.4 18.7 %collective-permute-start.17 = (f16[416,512]{1,0:T(8,128)(2,1)S(1)}, f16[416,512]{1,0:T(8,128)(2,1)S(1)}, u32[]{:S(2)}, u32[]{:S(2)}) collective-permute-start(f16[416,512]{1,0:T(8,128)(2,1)S(1)} %fusion.6), channel_id=1, source_target_pairs={{0,2},{1,3},{2,0},{3,1},{4,6},{5,7},{6,4},{7,5},{8,10},{9,11},{10,... | collective-permute-start | bytes 1277960 | tf_op jit(solution)/shard_map/ppermute | solution.py:48
  56.3 10.3 %collective-permute-start.9 = (f32[64,512]{1,0:T(8,128)S(1)}, f32[64,512]{1,0:T(8,128)S(1)}, u32[]{:S(2)}, u32[]{:S(2)}) collective-permute-start(f32[64,512]{1,0:T(8,128)S(1)} %add.114), channel_id=1, source_target_pairs={{0,4},{1,5},{2,6},{3,7},{4,0},{5,1},{6,2},{7,3},{8,12},{9,13},{10,... | collective-permute-start | bytes 393224 | tf_op jit(solution)/shard_map/ppermute | solution.py:48
  56.9 21.8 %collective-permute-start.15 = (f16[416,512]{1,0:T(8,128)(2,1)S(1)}, f16[416,512]{1,0:T(8,128)(2,1)S(1)}, u32[]{:S(2)}, u32[]{:S(2)}) collective-permute-start(f16[416,512]{1,0:T(8,128)(2,1)S(1)} %fusion.5), channel_id=1, source_target_pairs={{0,2},{1,3},{2,0},{3,1},{4,6},{5,7},{6,4},{7,5},{8,10},{9,11},{10,... | collective-permute-start | bytes 1277960 | tf_op jit(solution)/shard_map/ppermute | solution.py:48
  66.6 7.3 %collective-permute-start.12 = (f32[64,512]{1,0:T(8,128)S(1)}, f32[64,512]{1,0:T(8,128)S(1)}, u32[]{:S(2)}, u32[]{:S(2)}) collective-permute-start(f32[64,512]{1,0:T(8,128)S(1)} %add.115), channel_id=1, source_target_pairs={{0,17},{1,16},{2,19},{3,18},{4,21},{5,20},{6,23},{7,22},{8,25},{9,... | collective-permute-start | bytes 393224 | tf_op jit(solution)/shard_map/ppermute | solution.py:48
  66.7 7.2 %collective-permute-start.11 = (f32[64,512]{1,0:T(8,128)S(1)}, f32[64,512]{1,0:T(8,128)S(1)}, u32[]{:S(2)}, u32[]{:S(2)}) collective-permute-start(f32[64,512]{1,0:T(8,128)S(1)} %add.115), channel_id=1, source_target_pairs={{0,1},{1,0},{2,3},{3,2},{4,5},{5,4},{6,7},{7,6},{8,9},{9,8},{10,11... | collective-permute-start | bytes 393224 | tf_op jit(solution)/shard_map/ppermute | solution.py:48
  68.1 5.8 %collective-permute-start.10 = (f32[64,512]{1,0:T(8,128)S(1)}, f32[64,512]{1,0:T(8,128)S(1)}, u32[]{:S(2)}, u32[]{:S(2)}) collective-permute-start(f32[64,512]{1,0:T(8,128)S(1)} %add.115), channel_id=1, source_target_pairs={{0,16},{1,17},{2,18},{3,19},{4,20},{5,21},{6,22},{7,23},{8,24},{9,... | collective-permute-start | bytes 393224 | tf_op jit(solution)/shard_map/ppermute | solution.py:48
  70.4 17.1 %collective-permute-start.18 = (f16[416,512]{1,0:T(8,128)(2,1)S(1)}, f16[416,512]{1,0:T(8,128)(2,1)S(1)}, u32[]{:S(2)}, u32[]{:S(2)}) collective-permute-start(f16[416,512]{1,0:T(8,128)(2,1)S(1)} %fusion.4), channel_id=1, source_target_pairs={{0,4},{1,5},{2,6},{3,7},{4,0},{5,1},{6,2},{7,3},{8,12},{9,13},{10,... | collective-permute-start | bytes 1277960 | tf_op jit(solution)/shard_map/ppermute | solution.py:48
  73.9 14.0 %collective-permute-start.13 = (f32[256,512]{1,0:T(8,128)S(1)}, f32[256,512]{1,0:T(8,128)S(1)}, u32[]{:S(2)}, u32[]{:S(2)}) collective-permute-start(f32[256,512]{1,0:T(8,128)S(1)} %pad_maximum_fusion.refs_0_), channel_id=1, source_target_pairs={{0,8},{1,9},{2,10},{3,11},{4,12},{5,13},{6,14},{7,15},{8,0},{9,1},... | collective-permute-start | bytes 1572872 | tf_op jit(solution)/shard_map/ppermute | solution.py:48
  74.3 13.6 %copy-start = (s32[3]{0:T(128)S(1)}, s32[3]{0:T(128)}, u32[]{:S(2)}) copy-start(s32[3]{0:T(128)} %pad_add_fusion.place) | copy-start | bytes 40
  (4 other events, 10.0 us)

commit v3 on v0

v3 whole, which is shorter than its diff:
```python
import functools

import jax
import jax.numpy as jnp
from jax import lax
from jax.experimental import pallas as pl
from jax.experimental.pallas import tpu as pltpu
from jax.sharding import PartitionSpec as P

BLK = 128
NS_ITERS = 3
CORES = 2
WIRE = jnp.float16
LANES = 128
ROW_TILE = 16
VMEM = pl.BlockSpec(memory_space=pltpu.VMEM)
SMEM = pl.BlockSpec(memory_space=pltpu.SMEM)
HBM = pl.BlockSpec(memory_space=pltpu.HBM)
QUICK = pl.CostEstimate(flops=0, bytes_accessed=0, transcendentals=0)
PARAMS = pltpu.CompilerParams(vmem_limit_bytes=12 * 2**20)


def inner_size(n):
    return max(d for d in range(1, n + 1) if n % d == 0 and d * d <= n)


class Grid:
    def __init__(self):
        self.gr = lax.axis_size("gr")
        self.gc = lax.axis_size("gc")
        self.cores = CORES if self.gr % CORES == 0 else 1
        self.xs = self.gr // self.cores
        self.ys = inner_size(self.gc)
        self.zs = self.gc // self.ys
        gr, gc = lax.axis_index("gr"), lax.axis_index("gc")
        self.x, self.core = gr // self.cores, gr % self.cores
        self.z, self.y = gc // self.ys, gc % self.ys
        self.gr_index, self.gc_index = gr, gc
        self.plane = [(a, b) for b in range(self.ys) for a in range(self.xs)]

    def swap(self, value, dx=0, dcore=0, dz=0, dy=0):
        return self.permute(value, lambda core: (dx, dcore, dz, dy))

    def permute(self, value, moves):
        pairs = []
        for gr in range(self.gr):
            for gc in range(self.gc):
                core = gr % self.cores
                dx, dcore, dz, dy = moves(core)
                to_gr = ((gr // self.cores) ^ dx) * self.cores + (core ^ dcore)
                to_gc = ((gc // self.ys) ^ dz) * self.ys + ((gc % self.ys) ^ dy)
                pairs.append((gr * self.gc + gc, to_gr * self.gc + to_gc))
        return lax.ppermute(value, ("gr", "gc"), pairs)


def rows_of(value, start, count):
    return lax.dynamic_slice_in_dim(value, start, count, axis=0)


def shape(rows, columns, dtype):
    return pltpu.VMEM((rows, columns), dtype)


def placed(space, *values):
    return [pltpu.with_memory_space_constraint(value, space) for value in values]


def below_skyline(part, first_row, first_of):
    row_ids = first_row + lax.broadcasted_iota(jnp.int32, (part.shape[0], 1), 0)
    kept = []
    for c in range(part.shape[1] // BLK):
        block = part[:, c * BLK : (c + 1) * BLK]
        kept.append(jnp.where(row_ids >= first_of(c) * BLK, block, jnp.zeros_like(block)))
    return jnp.concatenate(kept, axis=1)


def chunks_kernel(ys, ks, j, own_rows, first, window_ref, *refs):
    shard_refs, (out_ref, sems) = refs[:-2], refs[-2:]
    gr, gc = lax.axis_index("gr"), lax.axis_index("gc")
    z, y = gc // ys, gc % ys
    base = gr * window_ref.shape[0]
    starts = [(jnp.bitwise_xor(z, k) * ys + jnp.bitwise_xor(y, j)) * own_rows for k in ks]
    places = [pl.ds(n * own_rows, own_rows) for n in range(len(ks))]
    copies = [
        pltpu.make_async_copy(
            window_ref.at[pl.ds(pl.multiple_of(start, ROW_TILE), own_rows), :], out_ref.at[place, :], sems.at[n]
        )
        for n, (start, place) in enumerate(zip(starts, places))
    ]
    for copy in copies:
        copy.start()
    for shard in shard_refs:
        out_ref[len(ks) * own_rows :, :] = across(shard[...], out_ref.shape[1])
    for copy, start, place in zip(copies, starts, places):
        copy.wait()
        out_ref[place, :] = below_skyline(out_ref[place, :], base + start, lambda c: first[c])


def across(shard, columns):
    return jnp.concatenate(jnp.split(shard, columns // shard.shape[1], axis=0), axis=1)


def masked_chunks(grid, window, first_block, ks, j, own_rows, *shard):
    extra = sum(part.size // window.shape[1] for part in shard)
    return pl.pallas_call(
        functools.partial(chunks_kernel, grid.ys, ks, j, own_rows),
        in_specs=[SMEM, HBM] + [VMEM] * len(shard),
        out_specs=VMEM,
        out_shape=shape(len(ks) * own_rows + extra, window.shape[1], window.dtype),
        scratch_shapes=[pltpu.SemaphoreType.DMA((len(ks),))],
        compiler_params=PARAMS,
        cost_estimate=QUICK,
        name="masked_chunks",
    )(first_block, *placed(pltpu.HBM, window), *shard)


def plain_masked_chunks(grid, window, first_block, ks, j, own_rows, *shard):
    parts = []
    for k in ks:
        start = ((grid.z ^ k) * grid.ys + (grid.y ^ j)) * own_rows
        parts.append(masked_rows(rows_of(window, start, own_rows), first_block, grid.gr_index * window.shape[0] + start))
    return jnp.concatenate(parts + [across(part, window.shape[1]) for part in shard], axis=0)


def pivot_pack_kernel(xs, ys, cores, first, window_ref, block_ref, *refs):
    out_refs, (head, padded, head_sem, block_sem) = refs[:-4], refs[-4:]
    chip_rows = out_refs[0].shape[0]
    own_rows, order = block_ref.shape
    depth = head.shape[1]
    gr, gc = lax.axis_index("gr"), lax.axis_index("gc")
    x, y = gr // cores, gc % ys
    begin = gc * own_rows
    head_copy = pltpu.make_async_copy(window_ref.at[pl.ds(0, order), :], head, head_sem)
    block_copy = pltpu.make_async_copy(block_ref, padded.at[pl.ds(chip_rows, own_rows), :], block_sem)
    holds = (gr == 0) & (begin < order)

    def start_of(n):
        return (jnp.bitwise_xor(y, n // xs) * xs + jnp.bitwise_xor(x, n % xs)) * chip_rows

    @pl.when(gr == 0)
    def _():
        head_copy.start()

    @pl.when(holds)
    def _():
        block_copy.start()

    for out_ref in out_refs:
        out_ref[...] = jnp.zeros_like(out_ref)

    @pl.when(gr == 0)
    def _():
        head_copy.wait()
        for n, out_ref in enumerate(out_refs):
            rows = head[pl.ds(pl.multiple_of(start_of(n), chip_rows), chip_rows), :]
            out_ref[:, :depth] = below_skyline(rows, start_of(n), lambda c: first[c])

    @pl.when(holds)
    def _():
        edge = jnp.zeros((chip_rows, order), jnp.float32)
        padded[:chip_rows, :] = edge
        padded[chip_rows + own_rows :, :] = edge
        block_copy.wait()
        for n, out_ref in enumerate(out_refs):
            place = jnp.clip(start_of(n) - begin + chip_rows, 0, chip_rows + own_rows)
            high, low = two_parts(padded[pl.ds(pl.multiple_of(place, 8), chip_rows), :])
            out_ref[:, depth : depth + order] = high
            out_ref[:, depth + order :] = low


def pivot_pack(grid, window, panel_block, first_block, chip_rows):
    own_rows, order = panel_block.shape
    depth = window.shape[1]
    targets = len(grid.plane)
    return pl.pallas_call(
        functools.partial(pivot_pack_kernel, grid.xs, grid.ys, grid.cores),
        in_specs=[SMEM, HBM, HBM],
        out_specs=[VMEM] * targets,
        out_shape=[shape(chip_rows, depth + 2 * order, window.dtype)] * targets,
        scratch_shapes=[
            pltpu.VMEM((order, depth), window.dtype),
            pltpu.VMEM((own_rows + 2 * chip_rows, order), jnp.float32),
            pltpu.SemaphoreType.DMA,
            pltpu.SemaphoreType.DMA,
        ],
        compiler_params=PARAMS,
        cost_estimate=QUICK,
        name="pivot_pack",
    )(first_block, *placed(pltpu.HBM, window, panel_block))


def plain_pivot_pack(grid, window, panel_block, first_block, chip_rows):
    own_rows, order = panel_block.shape
    begin = grid.gc_index * own_rows
    padded = jnp.zeros((order + own_rows, order), jnp.float32)
    padded = lax.dynamic_update_slice_in_dim(padded, panel_block, jnp.minimum(begin, order), axis=0)
    out = []
    for a, b in grid.plane:
        start = ((grid.y ^ b) * grid.xs + (grid.x ^ a)) * chip_rows
        rows = masked_rows(rows_of(window, start, chip_rows), first_block, start)
        entries = rows_of(padded, start, chip_rows)
        high = lax.reduce_precision(entries, 8, 7)
        parts = [rows, high.astype(rows.dtype), (entries - high).astype(rows.dtype)]
        out.append(jnp.concatenate(parts, axis=1))
    return [jnp.where(grid.gr_index == 0, pack, jnp.zeros_like(pack)) for pack in out]


def panel_kernel(xs, ys, cores, *refs):
    count = cores * xs * ys
    shards, packs, (panel_ref, total_ref) = refs[:count], refs[count:-2], refs[-2:]
    depth, width = shards[0].shape
    order = total_ref.shape[1]
    gr = lax.axis_index("gr")
    x, core = gr // cores, gr % cores
    for e in range(cores):
        for b in range(ys):
            for a in range(xs):
                place = jnp.bitwise_xor(x, a) * cores + jnp.bitwise_xor(core, e)
                columns = pl.ds(pl.multiple_of(place * width, width), width)
                panel_ref[b * depth : (b + 1) * depth, columns] = shards[(e * ys + b) * xs + a][...]
    total = jnp.zeros(total_ref.shape, jnp.float32)
    for b in range(ys):
        rows = packs[b * xs][:, :depth]
        for a in range(1, xs):
            rows = rows + packs[b * xs + a][:, :depth]
        total = total - jnp.dot(rows, panel_ref[b * depth : (b + 1) * depth, :], preferred_element_type=jnp.float32)
    for pack in packs:
        total = total + pack[:, depth : depth + order].astype(jnp.float32) + pack[:, depth + order :].astype(jnp.float32)
    total_ref[...] = total


def panel_and_pivot(grid, shards, packs):
    depth, width = shards[0].shape
    order = grid.gr * width
    return pl.pallas_call(
        functools.partial(panel_kernel, grid.xs, grid.ys, grid.cores),
        in_specs=[VMEM] * (len(shards) + len(packs)),
        out_specs=[VMEM, VMEM],
        out_shape=[shape(grid.ys * depth, order, shards[0].dtype), shape(packs[0].shape[0], order, jnp.float32)],
        compiler_params=PARAMS,
        cost_estimate=QUICK,
        name="panel_and_pivot",
    )(*placed(pltpu.VMEM, *shards, *packs))


def plain_panel_and_pivot(grid, shards, packs):
    depth = shards[0].shape[0]
    stack = jnp.stack(shards).reshape((grid.cores, grid.ys, grid.xs) + shards[0].shape)
    total, bands = 0.0, []
    for b in range(grid.ys):
        blocks = [stack[grid.core ^ (gr % grid.cores), b, grid.x ^ (gr // grid.cores)] for gr in range(grid.gr)]
        bands.append(jnp.concatenate(blocks, axis=1))
        rows = sum(pack[:, :depth] for pack in packs[b * grid.xs : (b + 1) * grid.xs])
        total = total - jnp.dot(rows, bands[b], preferred_element_type=jnp.float32)
    for pack in packs:
        high, low = jnp.split(pack[:, depth:].astype(jnp.float32), 2, axis=1)
        total = total + (high + low)
    return jnp.concatenate(bands, axis=0), total


def two_parts(value):
    high = value.astype(jnp.bfloat16)
    return high, (value - high.astype(jnp.float32)).astype(jnp.bfloat16)


def product(left, right):
    dot = functools.partial(jnp.dot, preferred_element_type=jnp.float32)
    return dot(left[0], right[0]) + (dot(left[0], right[1]) + dot(left[1], right[0]))


def inverse_kernel(xs, ys, cores, *refs):
    pieces, (high_ref, low_ref, scale_ref, pivot_ref) = refs[:-4], refs[-4:]
    piece = pieces[0].shape[0]
    gr, y = lax.axis_index("gr"), lax.axis_index("gc") % ys
    x, core = gr // cores, gr % cores
    for i, piece_ref in enumerate(pieces):
        e, n = divmod(i, xs * ys)
        chip = jnp.bitwise_xor(y, n // xs) * xs + jnp.bitwise_xor(x, n % xs)
        start = (chip * cores + jnp.bitwise_xor(core, e)) * piece
        pivot_ref[pl.ds(pl.multiple_of(start, piece), piece), :] = piece_ref[...]
    order = pivot_ref.shape[0]
    square = (order, order)
    diagonal = lax.broadcasted_iota(jnp.int32, square, 0) == lax.broadcasted_iota(jnp.int32, square, 1)
    pivot = pivot_ref[...]
    scale = jnp.sum(jnp.where(diagonal, pivot, 0.0)) / order
    power = jnp.where(diagonal, 1.0, 0.0) - pivot / scale
    rest = power
    parts = two_parts(power)
    for step in range(NS_ITERS - 1):
        power = product(parts, parts)
        parts = two_parts(power)
        rest = rest + power + product(two_parts(rest), parts)
    high_ref[...], low_ref[...] = two_parts(rest)
    scale_ref[0] = scale


def inverse_rest(grid, pieces):
    order = pieces[0].shape[1]
    half = shape(order, order, jnp.bfloat16)
    return pl.pallas_call(
        functools.partial(inverse_kernel, grid.xs, grid.ys, grid.cores),
        in_specs=[VMEM] * len(pieces),
        out_specs=[VMEM, VMEM, SMEM],
        out_shape=[half, half, jax.ShapeDtypeStruct((1,), jnp.float32)],
        scratch_shapes=[pltpu.VMEM((order, order), jnp.float32)],
        compiler_params=PARAMS,
        cost_estimate=QUICK,
        name="pivot_inverse",
    )(*placed(pltpu.VMEM, *pieces))


def factor_kernel(schur_ref, high_ref, low_ref, out_ref):
    rows, order = out_ref.shape
    schur = schur_ref[...]
    rest = high_ref[...], low_ref[...]
    out_ref[...] = schur + product(two_parts(schur), rest)
    start = (lax.axis_index("gr") * lax.axis_size("gc") + lax.axis_index("gc")) * rows

    @pl.when(start < order)
    def _():
        here = start + lax.broadcasted_iota(jnp.int32, (rows, order), 0)
        across = lax.broadcasted_iota(jnp.int32, (rows, order), 1)
        pick = jnp.where(here == across, 1.0, 0.0).astype(jnp.bfloat16)
        dot = functools.partial(jnp.dot, preferred_element_type=jnp.float32)
        inverse = pick.astype(jnp.float32) + (dot(pick, rest[0]) + dot(pick, rest[1]))
        out_ref[...] = jnp.where(here < order, inverse, out_ref[...])


def factor_rows(schur, high, low):
    rows, order = schur.shape
    return pl.pallas_call(
        factor_kernel,
        in_specs=[VMEM, VMEM, VMEM],
        out_specs=VMEM,
        out_shape=jax.ShapeDtypeStruct((rows, order), jnp.float32),
        compiler_params=PARAMS,
        cost_estimate=QUICK,
        name="factor_rows",
    )(*placed(pltpu.VMEM, schur, high, low))


def masked_rows(part, first_block, first_row):
    col_first = jnp.repeat(first_block, BLK)
    row_ids = first_row + jnp.arange(part.shape[0], dtype=jnp.int32)
    inside = (row_ids // BLK)[:, None] >= col_first[None, :]
    return jnp.where(inside, part, jnp.zeros_like(part))


def body(factor_window, upper_panel, panel_block, first_block):
    grid = Grid()
    local_rows, depth = factor_window.shape
    own_rows, panel_width = panel_block.shape
    chip_rows = panel_width // (grid.xs * grid.ys)
    whole_tiles = upper_panel.shape[1] % LANES == 0 and chip_rows % ROW_TILE == 0

    order = list(range(grid.zs - 1, -1, -1))
    chunks = masked_chunks if own_rows % ROW_TILE == 0 else plain_masked_chunks
    chunks = functools.partial(chunks, grid, factor_window, first_block)
    columns = {k: [None] * grid.ys for k in order}
    shards = {(0, 0): upper_panel}
    for b in range(1, grid.ys):
        got = grid.swap(chunks(order[:1], b, own_rows, upper_panel), dy=b)
        columns[order[0]][b] = got[:own_rows]
        shards[0, b] = jnp.concatenate(jnp.split(got[own_rows:], depth // upper_panel.shape[1], axis=1), axis=0)
    columns[order[0]][0] = chunks(order[:1], 0, own_rows)
    for b in range(grid.ys if order[1:] else 0):
        band = chunks(order[1:], b, own_rows)
        band = grid.swap(band, dy=b) if b else band
        for n, k in enumerate(order[1:]):
            columns[k][b] = band[n * own_rows : (n + 1) * own_rows]

    shards.update({(a, b): grid.swap(upper_panel, dx=a, dy=b) for a, b in grid.plane if a})
    shards = [shards[place] for place in grid.plane]
    if grid.cores > 1:
        shards = shards + [grid.swap(shard, dcore=1) for shard in shards]

    packs = (pivot_pack if whole_tiles else plain_pivot_pack)(grid, factor_window, panel_block, first_block, chip_rows)
    packs = [packs[0]] + [
        grid.permute(pack, lambda core: (0, 0, 1, 0) if core and grid.zs > 1 else (a, 0, 0, b))
        for pack, (a, b) in zip(packs[1:], grid.plane[1:])
    ]
    panel, total = (panel_and_pivot if whole_tiles else plain_panel_and_pivot)(grid, shards, packs)

    if grid.cores > 1:
        piece = chip_rows // grid.cores
        total = jnp.where(grid.core == 0, total[:piece], grid.swap(total[piece:], dcore=1))
    step = 1
    while step < grid.zs:
        total = total + grid.swap(total, dz=step)
        step *= 2
    pieces = [total] + [grid.swap(total, dx=a, dy=b) for a, b in grid.plane[1:]]
    if grid.cores > 1:
        pieces = pieces + [grid.swap(piece, dcore=1) for piece in pieces]
    high, low, scale = inverse_rest(grid, pieces)

    sums = {}
    for k in order:
        bands = [panel[j * depth : (j + 1) * depth] for j in range(grid.ys)]
        parts = [jnp.dot(part, band, preferred_element_type=jnp.float32) for part, band in zip(columns[k], bands)]
        sums[k] = sum(parts[1:], parts[0])
    step = 1
    while step < grid.zs:
        for k in sorted((k for k in sums if k & step), reverse=True):
            got = grid.swap(sums.pop(k).astype(WIRE), dz=step)
            sums[k ^ step] = sums[k ^ step] + got.astype(jnp.float32)
        step *= 2
    return factor_rows((panel_block - sums[0]) / scale[0], high, low)


def solution(mesh):
    return jax.shard_map(
        body,
        mesh=mesh,
        in_specs=(P("gr", "gc"), P("gc", "gr"), P(("gr", "gc"), None), P("gc")),
        out_specs=P(("gr", "gc"), None),
        check_vma=False,
    )
```

time: 311 us -> 69.1 us (0.22)
  waiting for transfers between devices: 256 us -> 23 us
  starting transfers between devices: 0.04 us -> 24.7 us
  Pallas kernels: 0 us -> 16.4 us
  matrix products: 17.3 us -> 2.87 us
  between operations: 14.2 us -> 0.26 us
  local copies, waits for them, and re-layouts: 12 us -> 1.53 us
  blocking collectives: 7.54 us -> 0 us
  other arithmetic: 3.25 us -> 0.06 us
    psum x1 -> x0, waiting for transfers between devices: 130 us -> none  [body(): pivot_block = lax.psum(pivot_term, ('gr', 'gc'))]
    reduce_scatter x1 -> x0, waiting for transfers between devices: 127 us -> none  [body(): lax.psum_scatter(jnp.dot(masked_rows(factor_window, row_base, col_first),...]
    ppermute x0 -> x24, starting transfers between devices: none -> 24.7 us  [permute(): return lax.ppermute(value, ('gr', 'gc'), pairs)]
    ppermute x0 -> x24, waiting for transfers between devices: none -> 23 us  [permute(): return lax.ppermute(value, ('gr', 'gc'), pairs)]
    pallas_call x0 -> x8, Pallas kernels: none -> 16.4 us  [the longest x4 6.68 us: masked_chunks(): pl.pallas_call(functools.partial(chunks_kernel, grid.ys, ks, j, own_rows)...]
    dot_general x8, matrix products: 17.3 us -> 2.87 us  [body(): jnp.dot(part, band, preferred_element_type=jnp.float32)]
    gather x3 -> x0, local copies, waits for them, and re-layouts: 11.9 us -> none  [the longest x1 8.61 us: body(): pivot_scale = jnp.mean(jnp.diagonal(pivot_block))]
    all_gather x1 -> x0, blocking collectives: 7.54 us -> none  [body(): whole_panel = lax.all_gather(upper_panel, 'gr', axis=1, tiled=True)]
  transfers between devices with their start and end apart: 2 -> 24, of which waited for: 2 -> 12; matrix products, arithmetic and copies ran while one was open for 0% -> 3% of each run, Pallas kernels for 0% -> 18%
where the time goes in v3:
time: 69.1 us; the launch traced here: 68.8 us
  starting transfers between devices  24.7 us (36%)
  waiting for transfers between devices  23 us (33%)
  Pallas kernels  16.4 us (24%)
  matrix products  2.87 us (4%)
  local copies, waits for them, and re-layouts  1.53 us (2%)
    ppermute x24, starting transfers between devices, permute(): return lax.ppermute(value, ('gr', 'gc'), pairs)  24.7 us
    ppermute x24, waiting for transfers between devices, permute(): return lax.ppermute(value, ('gr', 'gc'), pairs)  23 us
    pallas_call x4, Pallas kernels, masked_chunks(): pl.pallas_call(functools.partial(chunks_kernel, grid.ys, ks, j, own_rows)...  6.68 us
    pallas_call x1, Pallas kernels, inverse_rest(): pl.pallas_call(functools.partial(inverse_kernel, grid.xs, grid.ys, grid.c...  4.02 us
    pallas_call x1, Pallas kernels, pivot_pack(): pl.pallas_call(functools.partial(pivot_pack_kernel, grid.xs, grid.ys, gri...  2.9 us
    dot_general x8, matrix products, body(): jnp.dot(part, band, preferred_element_type=jnp.float32)  2.87 us
    pallas_call x1, Pallas kernels, factor_rows(): pl.pallas_call(factor_kernel, in_specs=[VMEM, VMEM, VMEM], out_specs=VMEM...  2.37 us
    unnamed x12, local copies, waits for them, and re-layouts  1.51 us
  transfers between devices with their start and end apart: 24, of which 12 were waited for; matrix products, arithmetic and copies ran while one was open for 3% of the time, Pallas kernels for 18%

profile of v3, /device:TPU:0, one launch (start us, length us, event | category | flops | bytes accessed | tf_op | source)
XLA Modules:
  0.0 68.8 jit_solution(741766993448641650)
XLA Ops:
  1.5 1.6 %masked_chunks.5 = bf16[544,256]{1,0:T(8,128)(2,1)S(1)} custom-call(s32[2]{0:T(128)S(1)} %copy-done.2, bf16[3328,256]{1,0:T(8,128)(2,1)} %window_ref.9, bf16[256,128]{1,0:T(8,128)(2,1)S(1)} %copy-done), custom_call_target="tpu_custom_call" | custom-call | tf_op jit(solution)/shard_map/masked_chunks/pallas_call | solution.py:105
  3.1 3.0 %collective-permute-start.1 = (bf16[544,256]{1,0:T(8,128)(2,1)S(1)}, bf16[544,256]{1,0:T(8,128)(2,1)S(1)}, u32[]{:S(2)}, u32[]{:S(2)}) collective-permute-start(bf16[544,256]{1,0:T(8,128)(2,1)S(1)} %masked_chunks.5), channel_id=1, source_target_pairs={{0,1},{1,0},{2,3},{3,2},{4,5},{5,4},{6,7},{7,6},{8,9},{9,8},{10,11... | collective-permute-start | bytes 835592 | tf_op jit(solution)/shard_map/ppermute | solution.py:53
  6.1 1.5 %collective-permute-start = (bf16[256,128]{1,0:T(8,128)(2,1)S(1)}, bf16[256,128]{1,0:T(8,128)(2,1)S(1)}, u32[]{:S(2)}, u32[]{:S(2)}) collective-permute-start(bf16[256,128]{1,0:T(8,128)(2,1)S(1)} %copy-done), channel_id=1, source_target_pairs={{0,16},{1,17},{2,18},{3,19},{4,20},{5,21},{6,22},{7,23},{8,24},{9,... | collective-permute-start | bytes 196616 | tf_op jit(solution)/shard_map/ppermute | solution.py:53
  7.6 2.9 %pivot_pack.1 = (bf16[128,1280]{1,0:T(8,128)(2,1)S(1)}, bf16[128,1280]{1,0:T(8,128)(2,1)}, bf16[128,1280]{1,0:T(8,128)(2,1)}, bf16[128,1280]{1,0:T(8,128)(2,1)}) custom-call(s32[2]{0:T(128)S(1)} %copy-done.2, bf16[3328,256]{1,0:T(8,128)(2,1)} %window_ref.9, f32[416,512]{1,0:T(8,128)} %block_ref.1), custom_call_target="tpu_custom_call" | custom-call | tf_op jit(solution)/shard_map/pivot_pack/pallas_call | solution.py:175
  11.2 1.5 %collective-permute-start.8 = (bf16[128,1280]{1,0:T(8,128)(2,1)}, bf16[128,1280]{1,0:T(8,128)(2,1)S(1)}, u32[]{:S(2)}, u32[]{:S(2)}) collective-permute-start(bf16[128,1280]{1,0:T(8,128)(2,1)} %get-tuple-element.16), channel_id=1, source_target_pairs={{0,1},{1,0},{2,3},{3,2},{4,5},{5,4},{6,7},{7,6},{8,10},{9,11},{10,... | collective-permute-start | bytes 983048 | tf_op jit(solution)/shard_map/ppermute | solution.py:53
  12.7 1.4 %collective-permute-done.1 = bf16[544,256]{1,0:T(8,128)(2,1)S(1)} collective-permute-done((bf16[544,256]{1,0:T(8,128)(2,1)S(1)}, bf16[544,256]{1,0:T(8,128)(2,1)S(1)}, u32[]{:S(2)}, u32[]{:S(2)}) %collective-permute-start.1) | collective-permute-done | bytes 278560 | tf_op jit(solution)/shard_map/ppermute | solution.py:53
  14.2 2.7 %collective-permute-start.9 = (bf16[128,1280]{1,0:T(8,128)(2,1)}, bf16[128,1280]{1,0:T(8,128)(2,1)S(1)}, u32[]{:S(2)}, u32[]{:S(2)}) collective-permute-start(bf16[128,1280]{1,0:T(8,128)(2,1)} %get-tuple-element.17), channel_id=1, source_target_pairs={{0,17},{1,16},{2,19},{3,18},{4,21},{5,20},{6,23},{7,22},{8,10},{9,... | collective-permute-start | bytes 983048 | tf_op jit(solution)/shard_map/ppermute | solution.py:53
  18.3 1.6 %masked_chunks.7 = bf16[416,256]{1,0:T(8,128)(2,1)S(1)} custom-call(s32[2]{0:T(128)S(1)} %copy-done.2, bf16[3328,256]{1,0:T(8,128)(2,1)} %window_ref.9), custom_call_target="tpu_custom_call" | custom-call | tf_op jit(solution)/shard_map/masked_chunks/pallas_call | solution.py:105
  19.9 1.8 %masked_chunks.6 = bf16[1248,256]{1,0:T(8,128)(2,1)S(1)} custom-call(s32[2]{0:T(128)S(1)} %copy-done.2, bf16[3328,256]{1,0:T(8,128)(2,1)} %window_ref.9), custom_call_target="tpu_custom_call" | custom-call | tf_op jit(solution)/shard_map/masked_chunks/pallas_call | solution.py:105
  21.7 1.8 %masked_chunks.4 = bf16[1248,256]{1,0:T(8,128)(2,1)S(1)} custom-call(s32[2]{0:T(128)S(1)} %copy-done.2, bf16[3328,256]{1,0:T(8,128)(2,1)} %window_ref.9), custom_call_target="tpu_custom_call" | custom-call | tf_op jit(solution)/shard_map/masked_chunks/pallas_call | solution.py:105
  26.0 1.6 %collective-permute-start.15 = (f32[64,512]{1,0:T(8,128)S(1)}, f32[64,512]{1,0:T(8,128)S(1)}, u32[]{:S(2)}, u32[]{:S(2)}) collective-permute-start(f32[64,512]{1,0:T(8,128)S(1)} %slice_select_fusion), channel_id=1, source_target_pairs={{0,2},{1,3},{2,0},{3,1},{4,6},{5,7},{6,4},{7,5},{8,10},{9,11},{10,... | collective-permute-start | bytes 393224 | tf_op jit(solution)/shard_map/ppermute | solution.py:53
  28.5 4.0 %collective-permute-done.15 = f32[64,512]{1,0:T(8,128)S(1)} collective-permute-done((f32[64,512]{1,0:T(8,128)S(1)}, f32[64,512]{1,0:T(8,128)S(1)}, u32[]{:S(2)}, u32[]{:S(2)}) %collective-permute-start.15) | collective-permute-done | bytes 131104 | tf_op jit(solution)/shard_map/ppermute | solution.py:53
  32.5 2.7 %collective-permute-start.16 = (f32[64,512]{1,0:T(8,128)S(1)}, f32[64,512]{1,0:T(8,128)S(1)}, u32[]{:S(2)}, u32[]{:S(2)}) collective-permute-start(f32[64,512]{1,0:T(8,128)S(1)} %add.39), channel_id=1, source_target_pairs={{0,4},{1,5},{2,6},{3,7},{4,0},{5,1},{6,2},{7,3},{8,12},{9,13},{10,... | collective-permute-start | bytes 393224 | tf_op jit(solution)/shard_map/ppermute | solution.py:53
  35.1 5.1 %collective-permute-done.10 = bf16[1248,256]{1,0:T(8,128)(2,1)S(1)} collective-permute-done((bf16[1248,256]{1,0:T(8,128)(2,1)S(1)}, bf16[1248,256]{1,0:T(8,128)(2,1)S(1)}, u32[]{:S(2)}, u32[]{:S(2)}) %collective-permute-start.10) | collective-permute-done | bytes 639008 | tf_op jit(solution)/shard_map/ppermute | solution.py:53
  40.8 1.6 %collective-permute-start.11 = (f16[416,512]{1,0:T(8,128)(2,1)S(1)}, f16[416,512]{1,0:T(8,128)(2,1)S(1)}, u32[]{:S(2)}, u32[]{:S(2)}) collective-permute-start(f16[416,512]{1,0:T(8,128)(2,1)S(1)} %fusion.5), channel_id=1, source_target_pairs={{0,2},{1,3},{2,0},{3,1},{4,6},{5,7},{6,4},{7,5},{8,10},{9,11},{10,... | collective-permute-start | bytes 1277960 | tf_op jit(solution)/shard_map/ppermute | solution.py:53
  44.5 3.3 %collective-permute-start.13 = (f16[416,512]{1,0:T(8,128)(2,1)S(1)}, f16[416,512]{1,0:T(8,128)(2,1)S(1)}, u32[]{:S(2)}, u32[]{:S(2)}) collective-permute-start(f16[416,512]{1,0:T(8,128)(2,1)S(1)} %fusion.4), channel_id=1, source_target_pairs={{0,4},{1,5},{2,6},{3,7},{4,0},{5,1},{6,2},{7,3},{8,12},{9,13},{10,... | collective-permute-start | bytes 1277960 | tf_op jit(solution)/shard_map/ppermute | solution.py:53
  47.8 1.6 %collective-permute-start.18 = (f32[64,512]{1,0:T(8,128)S(1)}, f32[64,512]{1,0:T(8,128)S(1)}, u32[]{:S(2)}, u32[]{:S(2)}) collective-permute-start(f32[64,512]{1,0:T(8,128)S(1)} %add.40.refs_0_), channel_id=1, source_target_pairs={{0,1},{1,0},{2,3},{3,2},{4,5},{5,4},{6,7},{7,6},{8,9},{9,8},{10,11... | collective-permute-start | bytes 393224 | tf_op jit(solution)/shard_map/ppermute | solution.py:53
  49.4 1.2 %collective-permute-start.19 = (f32[64,512]{1,0:T(8,128)S(1)}, f32[64,512]{1,0:T(8,128)S(1)}, u32[]{:S(2)}, u32[]{:S(2)}) collective-permute-start(f32[64,512]{1,0:T(8,128)S(1)} %add.40.refs_0_), channel_id=1, source_target_pairs={{0,17},{1,16},{2,19},{3,18},{4,21},{5,20},{6,23},{7,22},{8,25},{9,... | collective-permute-start | bytes 393224 | tf_op jit(solution)/shard_map/ppermute | solution.py:53
  50.6 2.9 %collective-permute-done.18.refs_2_ = f32[64,512]{1,0:T(8,128)S(1)} collective-permute-done((f32[64,512]{1,0:T(8,128)S(1)}, f32[64,512]{1,0:T(8,128)S(1)}, u32[]{:S(2)}, u32[]{:S(2)}) %collective-permute-start.18) | collective-permute-done | bytes 131104 | tf_op jit(solution)/shard_map/ppermute | solution.py:53
  53.5 1.7 %collective-permute-done.19.refs_3_ = f32[64,512]{1,0:T(8,128)S(1)} collective-permute-done((f32[64,512]{1,0:T(8,128)S(1)}, f32[64,512]{1,0:T(8,128)S(1)}, u32[]{:S(2)}, u32[]{:S(2)}) %collective-permute-start.19) | collective-permute-done | bytes 131104 | tf_op jit(solution)/shard_map/ppermute | solution.py:53
  56.8 4.0 %pivot_inverse.1 = (bf16[512,512]{1,0:T(8,128)(2,1)S(1)}, bf16[512,512]{1,0:T(8,128)(2,1)S(1)}, f32[1]{0:T(128)}) custom-call(f32[64,512]{1,0:T(8,128)S(1)} %add.40.refs_0_, f32[64,512]{1,0:T(8,128)S(1)} %collective-permute-done.17.refs_1_, f32[64,512]{1,0:T(8,128)S(1)} %collective-permute-done.18.refs_2_, f32[64,512]{1,0:T(8,128)S(1)} %collective-permute-done.19.refs_3_, ...), custom_call_target="tpu_custom_call" | custom-call | tf_op jit(solution)/shard_map/pivot_inverse/pallas_call | solution.py:300
  60.8 4.6 %collective-permute-done.13 = f16[416,512]{1,0:T(8,128)(2,1)S(1)} collective-permute-done((f16[416,512]{1,0:T(8,128)(2,1)S(1)}, f16[416,512]{1,0:T(8,128)(2,1)S(1)}, u32[]{:S(2)}, u32[]{:S(2)}) %collective-permute-start.13) | collective-permute-done | bytes 426016 | tf_op jit(solution)/shard_map/ppermute | solution.py:53
  65.4 1.0 %broadcast_divide_fusion.schur_ref = f32[416,512]{1,0:T(8,128)S(1)} fusion(f32[]{:T(128)} %bitcast, f32[416,512]{1,0:T(8,128)S(1)} %copy-done.3, f16[416,512]{1,0:T(8,128)(2,1)S(1)} %collective-permute-done.13, f16[416,512]{1,0:T(8,128)(2,1)S(1)} %collective-permute-done.11, f32[416,512]{1,0:T(8,128)S(1)} %fusion.15, ...), kind=kOutput, calls=%fused_computation.11 | convolution fusion | flops 110542848 | bytes 3883012 | tf_op jit(solution)/shard_map/dot_general | solution.py:399
  66.4 2.4 %factor_rows.1 = f32[416,512]{1,0:T(8,128)} custom-call(f32[416,512]{1,0:T(8,128)S(1)} %broadcast_divide_fusion.schur_ref, bf16[512,512]{1,0:T(8,128)(2,1)S(1)} %get-tuple-element.21.high_ref, bf16[512,512]{1,0:T(8,128)(2,1)S(1)} %get-tuple-element.22.low_ref), custom_call_target="tpu_custom_call" | custom-call | tf_op jit(solution)/shard_map/factor_rows/pallas_call | solution.py:331
  (58 shorter events, 11.0 us)
Async XLA Ops:
  3.1 11.1 %collective-permute-start.1 = (bf16[544,256]{1,0:T(8,128)(2,1)S(1)}, bf16[544,256]{1,0:T(8,128)(2,1)S(1)}, u32[]{:S(2)}, u32[]{:S(2)}) collective-permute-start(bf16[544,256]{1,0:T(8,128)(2,1)S(1)} %masked_chunks.5), channel_id=1, source_target_pairs={{0,1},{1,0},{2,3},{3,2},{4,5},{5,4},{6,7},{7,6},{8,9},{9,8},{10,11... | collective-permute-start | bytes 835592 | tf_op jit(solution)/shard_map/ppermute | solution.py:53
  6.1 5.1 %collective-permute-start = (bf16[256,128]{1,0:T(8,128)(2,1)S(1)}, bf16[256,128]{1,0:T(8,128)(2,1)S(1)}, u32[]{:S(2)}, u32[]{:S(2)}) collective-permute-start(bf16[256,128]{1,0:T(8,128)(2,1)S(1)} %copy-done), channel_id=1, source_target_pairs={{0,16},{1,17},{2,18},{3,19},{4,20},{5,21},{6,22},{7,23},{8,24},{9,... | collective-permute-start | bytes 196616 | tf_op jit(solution)/shard_map/ppermute | solution.py:53
  7.6 9.2 %collective-permute-start.2 = (bf16[256,128]{1,0:T(8,128)(2,1)S(1)}, bf16[256,128]{1,0:T(8,128)(2,1)S(1)}, u32[]{:S(2)}, u32[]{:S(2)}) collective-permute-start(bf16[256,128]{1,0:T(8,128)(2,1)S(1)} %copy-done), channel_id=1, source_target_pairs={{0,17},{1,16},{2,19},{3,18},{4,21},{5,20},{6,23},{7,22},{8,25},{9,... | collective-permute-start | bytes 196616 | tf_op jit(solution)/shard_map/ppermute | solution.py:53
  7.6 9.3 %collective-permute-start.3 = (bf16[256,128]{1,0:T(8,128)(2,1)S(1)}, bf16[256,128]{1,0:T(8,128)(2,1)S(1)}, u32[]{:S(2)}, u32[]{:S(2)}) collective-permute-start(bf16[256,128]{1,0:T(8,128)(2,1)S(1)} %copy-done), channel_id=1, source_target_pairs={{0,8},{1,9},{2,10},{3,11},{4,12},{5,13},{6,14},{7,15},{8,0},{9,1},... | collective-permute-start | bytes 196616 | tf_op jit(solution)/shard_map/ppermute | solution.py:53
  10.6 13.5 %collective-permute-start.7 = (bf16[128,1280]{1,0:T(8,128)(2,1)}, bf16[128,1280]{1,0:T(8,128)(2,1)S(1)}, u32[]{:S(2)}, u32[]{:S(2)}) collective-permute-start(bf16[128,1280]{1,0:T(8,128)(2,1)} %get-tuple-element.15), channel_id=1, source_target_pairs={{0,16},{1,17},{2,18},{3,19},{4,20},{5,21},{6,22},{7,23},{8,10},{9,... | collective-permute-start | bytes 983048 | tf_op jit(solution)/shard_map/ppermute | solution.py:53
  11.2 12.9 %collective-permute-start.8 = (bf16[128,1280]{1,0:T(8,128)(2,1)}, bf16[128,1280]{1,0:T(8,128)(2,1)S(1)}, u32[]{:S(2)}, u32[]{:S(2)}) collective-permute-start(bf16[128,1280]{1,0:T(8,128)(2,1)} %get-tuple-element.16), channel_id=1, source_target_pairs={{0,1},{1,0},{2,3},{3,2},{4,5},{5,4},{6,7},{7,6},{8,10},{9,11},{10,... | collective-permute-start | bytes 983048 | tf_op jit(solution)/shard_map/ppermute | solution.py:53
  14.2 9.9 %collective-permute-start.9 = (bf16[128,1280]{1,0:T(8,128)(2,1)}, bf16[128,1280]{1,0:T(8,128)(2,1)S(1)}, u32[]{:S(2)}, u32[]{:S(2)}) collective-permute-start(bf16[128,1280]{1,0:T(8,128)(2,1)} %get-tuple-element.17), channel_id=1, source_target_pairs={{0,17},{1,16},{2,19},{3,18},{4,21},{5,20},{6,23},{7,22},{8,10},{9,... | collective-permute-start | bytes 983048 | tf_op jit(solution)/shard_map/ppermute | solution.py:53
  16.8 1.3 %collective-permute-start.4 = (bf16[256,128]{1,0:T(8,128)(2,1)S(1)}, bf16[256,128]{1,0:T(8,128)(2,1)S(1)}, u32[]{:S(2)}, u32[]{:S(2)}) collective-permute-start(bf16[256,128]{1,0:T(8,128)(2,1)S(1)} %collective-permute-done.refs_1_), channel_id=1, source_target_pairs={{0,8},{1,9},{2,10},{3,11},{4,12},{5,13},{6,14},{7,15},{8,0},{9,1},... | collective-permute-start | bytes 196616 | tf_op jit(solution)/shard_map/ppermute | solution.py:53
  16.9 6.6 %collective-permute-start.6 = (bf16[256,128]{1,0:T(8,128)(2,1)S(1)}, bf16[256,128]{1,0:T(8,128)(2,1)S(1)}, u32[]{:S(2)}, u32[]{:S(2)}) collective-permute-start(bf16[256,128]{1,0:T(8,128)(2,1)S(1)} %collective-permute-done.2.refs_3_), channel_id=1, source_target_pairs={{0,8},{1,9},{2,10},{3,11},{4,12},{5,13},{6,14},{7,15},{8,0},{9,1},... | collective-permute-start | bytes 196616 | tf_op jit(solution)/shard_map/ppermute | solution.py:53
  18.2 5.9 %collective-permute-start.5 = (bf16[256,128]{1,0:T(8,128)(2,1)S(1)}, bf16[256,128]{1,0:T(8,128)(2,1)S(1)}, u32[]{:S(2)}, u32[]{:S(2)}) collective-permute-start(bf16[256,128]{1,0:T(8,128)(2,1)S(1)} %pad_maximum_fusion.refs_2_), channel_id=1, source_target_pairs={{0,8},{1,9},{2,10},{3,11},{4,12},{5,13},{6,14},{7,15},{8,0},{9,1},... | collective-permute-start | bytes 196616 | tf_op jit(solution)/shard_map/ppermute | solution.py:53
  23.5 16.7 %collective-permute-start.10 = (bf16[1248,256]{1,0:T(8,128)(2,1)S(1)}, bf16[1248,256]{1,0:T(8,128)(2,1)S(1)}, u32[]{:S(2)}, u32[]{:S(2)}) collective-permute-start(bf16[1248,256]{1,0:T(8,128)(2,1)S(1)} %masked_chunks.6), channel_id=1, source_target_pairs={{0,1},{1,0},{2,3},{3,2},{4,5},{5,4},{6,7},{7,6},{8,9},{9,8},{10,11... | collective-permute-start | bytes 1916936 | tf_op jit(solution)/shard_map/ppermute | solution.py:53
  24.6 1.4 %collective-permute-start.14 = (f32[64,512]{1,0:T(8,128)S(1)}, f32[64,512]{1,0:T(8,128)S(1)}, u32[]{:S(2)}, u32[]{:S(2)}) collective-permute-start(f32[64,512]{1,0:T(8,128)S(1)} %slice.52), channel_id=1, source_target_pairs={{0,8},{1,9},{2,10},{3,11},{4,12},{5,13},{6,14},{7,15},{8,0},{9,1},... | collective-permute-start | bytes 393224 | tf_op jit(solution)/shard_map/ppermute | solution.py:53
  26.0 6.4 %collective-permute-start.15 = (f32[64,512]{1,0:T(8,128)S(1)}, f32[64,512]{1,0:T(8,128)S(1)}, u32[]{:S(2)}, u32[]{:S(2)}) collective-permute-start(f32[64,512]{1,0:T(8,128)S(1)} %slice_select_fusion), channel_id=1, source_target_pairs={{0,2},{1,3},{2,0},{3,1},{4,6},{5,7},{6,4},{7,5},{8,10},{9,11},{10,... | collective-permute-start | bytes 393224 | tf_op jit(solution)/shard_map/ppermute | solution.py:53
  28.0 16.2 %collective-permute-start.12 = (f16[416,512]{1,0:T(8,128)(2,1)S(1)}, f16[416,512]{1,0:T(8,128)(2,1)S(1)}, u32[]{:S(2)}, u32[]{:S(2)}) collective-permute-start(f16[416,512]{1,0:T(8,128)(2,1)S(1)} %fusion.6), channel_id=1, source_target_pairs={{0,2},{1,3},{2,0},{3,1},{4,6},{5,7},{6,4},{7,5},{8,10},{9,11},{10,... | collective-permute-start | bytes 1277960 | tf_op jit(solution)/shard_map/ppermute | solution.py:53
  32.5 10.8 %collective-permute-start.16 = (f32[64,512]{1,0:T(8,128)S(1)}, f32[64,512]{1,0:T(8,128)S(1)}, u32[]{:S(2)}, u32[]{:S(2)}) collective-permute-start(f32[64,512]{1,0:T(8,128)S(1)} %add.39), channel_id=1, source_target_pairs={{0,4},{1,5},{2,6},{3,7},{4,0},{5,1},{6,2},{7,3},{8,12},{9,13},{10,... | collective-permute-start | bytes 393224 | tf_op jit(solution)/shard_map/ppermute | solution.py:53
  40.8 20.0 %collective-permute-start.11 = (f16[416,512]{1,0:T(8,128)(2,1)S(1)}, f16[416,512]{1,0:T(8,128)(2,1)S(1)}, u32[]{:S(2)}, u32[]{:S(2)}) collective-permute-start(f16[416,512]{1,0:T(8,128)(2,1)S(1)} %fusion.5), channel_id=1, source_target_pairs={{0,2},{1,3},{2,0},{3,1},{4,6},{5,7},{6,4},{7,5},{8,10},{9,11},{10,... | collective-permute-start | bytes 1277960 | tf_op jit(solution)/shard_map/ppermute | solution.py:53
  43.3 7.3 %collective-permute-start.17 = (f32[64,512]{1,0:T(8,128)S(1)}, f32[64,512]{1,0:T(8,128)S(1)}, u32[]{:S(2)}, u32[]{:S(2)}) collective-permute-start(f32[64,512]{1,0:T(8,128)S(1)} %add.40.refs_0_), channel_id=1, source_target_pairs={{0,16},{1,17},{2,18},{3,19},{4,20},{5,21},{6,22},{7,23},{8,24},{9,... | collective-permute-start | bytes 393224 | tf_op jit(solution)/shard_map/ppermute | solution.py:53
  44.5 21.0 %collective-permute-start.13 = (f16[416,512]{1,0:T(8,128)(2,1)S(1)}, f16[416,512]{1,0:T(8,128)(2,1)S(1)}, u32[]{:S(2)}, u32[]{:S(2)}) collective-permute-start(f16[416,512]{1,0:T(8,128)(2,1)S(1)} %fusion.4), channel_id=1, source_target_pairs={{0,4},{1,5},{2,6},{3,7},{4,0},{5,1},{6,2},{7,3},{8,12},{9,13},{10,... | collective-permute-start | bytes 1277960 | tf_op jit(solution)/shard_map/ppermute | solution.py:53
  47.8 5.8 %collective-permute-start.18 = (f32[64,512]{1,0:T(8,128)S(1)}, f32[64,512]{1,0:T(8,128)S(1)}, u32[]{:S(2)}, u32[]{:S(2)}) collective-permute-start(f32[64,512]{1,0:T(8,128)S(1)} %add.40.refs_0_), channel_id=1, source_target_pairs={{0,1},{1,0},{2,3},{3,2},{4,5},{5,4},{6,7},{7,6},{8,9},{9,8},{10,11... | collective-permute-start | bytes 393224 | tf_op jit(solution)/shard_map/ppermute | solution.py:53
  49.4 5.9 %collective-permute-start.19 = (f32[64,512]{1,0:T(8,128)S(1)}, f32[64,512]{1,0:T(8,128)S(1)}, u32[]{:S(2)}, u32[]{:S(2)}) collective-permute-start(f32[64,512]{1,0:T(8,128)S(1)} %add.40.refs_0_), channel_id=1, source_target_pairs={{0,17},{1,16},{2,19},{3,18},{4,21},{5,20},{6,23},{7,22},{8,25},{9,... | collective-permute-start | bytes 393224 | tf_op jit(solution)/shard_map/ppermute | solution.py:53
  50.6 4.7 %collective-permute-start.20 = (f32[64,512]{1,0:T(8,128)S(1)}, f32[64,512]{1,0:T(8,128)S(1)}, u32[]{:S(2)}, u32[]{:S(2)}) collective-permute-start(f32[64,512]{1,0:T(8,128)S(1)} %add.40.refs_0_), channel_id=1, source_target_pairs={{0,8},{1,9},{2,10},{3,11},{4,12},{5,13},{6,14},{7,15},{8,0},{9,1},... | collective-permute-start | bytes 393224 | tf_op jit(solution)/shard_map/ppermute | solution.py:53
  53.5 2.5 %collective-permute-start.21 = (f32[64,512]{1,0:T(8,128)S(1)}, f32[64,512]{1,0:T(8,128)S(1)}, u32[]{:S(2)}, u32[]{:S(2)}) collective-permute-start(f32[64,512]{1,0:T(8,128)S(1)} %collective-permute-done.17.refs_1_), channel_id=1, source_target_pairs={{0,8},{1,9},{2,10},{3,11},{4,12},{5,13},{6,14},{7,15},{8,0},{9,1},... | collective-permute-start | bytes 393224 | tf_op jit(solution)/shard_map/ppermute | solution.py:53
  55.2 1.3 %collective-permute-start.22 = (f32[64,512]{1,0:T(8,128)S(1)}, f32[64,512]{1,0:T(8,128)S(1)}, u32[]{:S(2)}, u32[]{:S(2)}) collective-permute-start(f32[64,512]{1,0:T(8,128)S(1)} %collective-permute-done.18.refs_2_), channel_id=1, source_target_pairs={{0,8},{1,9},{2,10},{3,11},{4,12},{5,13},{6,14},{7,15},{8,0},{9,1},... | collective-permute-start | bytes 393224 | tf_op jit(solution)/shard_map/ppermute | solution.py:53
  55.3 1.5 %collective-permute-start.23 = (f32[64,512]{1,0:T(8,128)S(1)}, f32[64,512]{1,0:T(8,128)S(1)}, u32[]{:S(2)}, u32[]{:S(2)}) collective-permute-start(f32[64,512]{1,0:T(8,128)S(1)} %collective-permute-done.19.refs_3_), channel_id=1, source_target_pairs={{0,8},{1,9},{2,10},{3,11},{4,12},{5,13},{6,14},{7,15},{8,0},{9,1},... | collective-permute-start | bytes 393224 | tf_op jit(solution)/shard_map/ppermute | solution.py:53
  (6 other events, 33.7 us)

commit v4 on v3

v4 whole, which is shorter than its diff:
```python
import functools

import jax
import jax.numpy as jnp
from jax import lax
from jax.experimental import pallas as pl
from jax.experimental.pallas import tpu as pltpu
from jax.sharding import PartitionSpec as P

BLK = 128
NS_ITERS = 3
CORES = 2
WIRE = jnp.float16
LANES = 128
ROW_TILE = 16
VMEM = pl.BlockSpec(memory_space=pltpu.VMEM)
SMEM = pl.BlockSpec(memory_space=pltpu.SMEM)
HBM = pl.BlockSpec(memory_space=pltpu.HBM)
ANY = pl.BlockSpec(memory_space=pl.ANY)
QUICK = pl.CostEstimate(flops=0, bytes_accessed=0, transcendentals=0)
PARAMS = pltpu.CompilerParams(vmem_limit_bytes=12 * 2**20)


def inner_size(n):
    return max(d for d in range(1, n + 1) if n % d == 0 and d * d <= n)


class Grid:
    def __init__(self):
        self.gr = lax.axis_size("gr")
        self.gc = lax.axis_size("gc")
        self.cores = CORES if self.gr % CORES == 0 else 1
        self.xs = self.gr // self.cores
        self.ys = inner_size(self.gc)
        self.ps = 2 if self.gc // self.ys % 2 == 0 else 1
        self.qs = self.gc // self.ps
        self.gr_index, self.gc_index = lax.axis_index("gr"), lax.axis_index("gc")
        self.x, self.core = self.gr_index // self.cores, self.gr_index % self.cores
        self.p = pair_place(self.gc_index, self.ys, self.ps)
        self.plane = [(a, b) for b in range(self.ps) for a in range(self.xs)]

    def swap(self, value, dx=0, dcore=0, dp=0, dq=0):
        return self.permute(value, lambda core: (dx, dcore, dp, dq))

    def permute(self, value, moves):
        pairs = []
        for gr in range(self.gr):
            for gc in range(self.gc):
                core = gr % self.cores
                dx, dcore, dp, dq = moves(core)
                to_gr = ((gr // self.cores) ^ dx) * self.cores + (core ^ dcore)
                pairs.append((gr * self.gc + gc, to_gr * self.gc + partner(gc, self.ys, self.ps, dq, dp)))
        return lax.ppermute(value, ("gr", "gc"), pairs)


def pair_place(gc, ys, ps):
    return gc // ys % ps


def partner(gc, ys, ps, dq, dp):
    return (gc // ys ^ (dq // ys * ps) ^ dp) * ys + (gc % ys ^ dq % ys)


def rows_of(value, start, count):
    return lax.dynamic_slice_in_dim(value, start, count, axis=0)


def shape(rows, columns, dtype):
    return pltpu.VMEM((rows, columns), dtype)


def after(value, *others):
    return pl.pallas_call(
        lambda *refs: None,
        in_specs=[ANY] * (1 + len(others)),
        out_specs=ANY,
        out_shape=jax.ShapeDtypeStruct(value.shape, value.dtype),
        input_output_aliases={0: 0},
        compiler_params=PARAMS,
        cost_estimate=QUICK,
        name="after",
    )(value, *others)


def placed(space, *values):
    return [pltpu.with_memory_space_constraint(value, space) for value in values]


def below_skyline(part, first_row, first_of):
    row_ids = first_row + lax.broadcasted_iota(jnp.int32, (part.shape[0], 1), 0)
    kept = []
    for c in range(part.shape[1] // BLK):
        block = part[:, c * BLK : (c + 1) * BLK]
        kept.append(jnp.where(row_ids >= first_of(c) * BLK, block, jnp.zeros_like(block)))
    return jnp.concatenate(kept, axis=1)


def across(shard, columns):
    return jnp.concatenate(jnp.split(shard, columns // shard.shape[1], axis=0), axis=1)


def chunks_kernel(ys, ps, wanted, own_rows, shards, first_ref, window_ref, *refs):
    shard_refs, refs = refs[:shards], refs[shards:]
    out_refs, (first, first_sem, sems) = refs[: len(wanted)], refs[len(wanted) : len(wanted) + 3]
    gr, gc = lax.axis_index("gr"), lax.axis_index("gc")
    first_copy = pltpu.make_async_copy(first_ref, first, first_sem)
    first_copy.start()
    copies = []
    for out_ref, chunks in zip(out_refs, wanted):
        for n, (k, j) in enumerate(chunks):
            start = partner(gc, ys, ps, k, j) * own_rows
            source = window_ref.at[pl.ds(pl.multiple_of(start, ROW_TILE), own_rows), :]
            place = out_ref.at[n * own_rows : (n + 1) * own_rows, :]
            copies.append((pltpu.make_async_copy(source, place, sems.at[len(copies)]), place, start))
            copies[-1][0].start()
    if shards:
        held, held_sem = refs[-2:]
        held_copy = pltpu.make_async_copy(shard_refs[0], held, held_sem)
        held_copy.start()
        held_copy.wait()
        out_refs[0][len(wanted[0]) * own_rows :, :] = across(held[...], out_refs[0].shape[1])
    first_copy.wait()
    for copy, place, start in copies:
        copy.wait()
        place[...] = below_skyline(place[...], gr * window_ref.shape[0] + start, lambda c: first[c])


def masked_chunks(grid, window, first_block, wanted, own_rows, *shard):
    extra = sum(part.size // window.shape[1] for part in shard)
    rows = [len(chunks) * own_rows for chunks in wanted]
    rows[0] += extra
    scratch = [
        pltpu.SMEM(first_block.shape, first_block.dtype),
        pltpu.SemaphoreType.DMA,
        pltpu.SemaphoreType.DMA((sum(len(chunks) for chunks in wanted),)),
    ]
    for part in shard:
        scratch += [pltpu.VMEM(part.shape, part.dtype), pltpu.SemaphoreType.DMA]
    return pl.pallas_call(
        functools.partial(chunks_kernel, grid.ys, grid.ps, wanted, own_rows, len(shard)),
        in_specs=[HBM] * (2 + len(shard)),
        out_specs=[VMEM] * len(wanted),
        out_shape=[shape(count, window.shape[1], window.dtype) for count in rows],
        scratch_shapes=scratch,
        compiler_params=PARAMS,
        cost_estimate=QUICK,
        name="masked_chunks",
    )(*placed(pltpu.HBM, first_block, window, *shard))


def plain_masked_chunks(grid, window, first_block, wanted, own_rows, *shard):
    out = []
    for chunks in wanted:
        parts = []
        for k, j in chunks:
            start = partner(grid.gc_index, grid.ys, grid.ps, k, j) * own_rows
            part = rows_of(window, start, own_rows)
            parts.append(masked_rows(part, first_block, grid.gr_index * window.shape[0] + start))
        if not out:
            parts += [across(part, window.shape[1]) for part in shard]
        out.append(jnp.concatenate(parts, axis=0))
    return out


def pivot_pack_kernel(xs, ys, ps, cores, first, window_ref, block_ref, *refs):
    out_refs, (head, padded, head_sem, block_sem) = refs[:-4], refs[-4:]
    chip_rows = out_refs[0].shape[0]
    own_rows, order = block_ref.shape
    depth = head.shape[1]
    gr, gc = lax.axis_index("gr"), lax.axis_index("gc")
    x, p = gr // cores, pair_place(gc, ys, ps)
    begin = gc * own_rows
    head_copy = pltpu.make_async_copy(window_ref.at[pl.ds(0, order), :], head, head_sem)
    block_copy = pltpu.make_async_copy(block_ref, padded.at[pl.ds(chip_rows, own_rows), :], block_sem)
    holds = (gr == 0) & (begin < order)

    def start_of(n):
        return ((p ^ n // xs) * xs + (x ^ n % xs)) * chip_rows

    @pl.when(gr == 0)
    def _():
        head_copy.start()

    @pl.when(holds)
    def _():
        block_copy.start()

    for out_ref in out_refs:
        out_ref[...] = jnp.zeros_like(out_ref)

    @pl.when(gr == 0)
    def _():
        head_copy.wait()
        for n, out_ref in enumerate(out_refs):
            rows = head[pl.ds(pl.multiple_of(start_of(n), chip_rows), chip_rows), :]
            out_ref[:, :depth] = below_skyline(rows, start_of(n), lambda c: first[c])

    @pl.when(holds)
    def _():
        edge = jnp.zeros((chip_rows, order), jnp.float32)
        padded[:chip_rows, :] = edge
        padded[chip_rows + own_rows :, :] = edge
        block_copy.wait()
        for n, out_ref in enumerate(out_refs):
            place = jnp.clip(start_of(n) - begin + chip_rows, 0, chip_rows + own_rows)
            high, low = two_parts(padded[pl.ds(pl.multiple_of(place, 8), chip_rows), :])
            out_ref[:, depth : depth + order] = high
            out_ref[:, depth + order :] = low


def pivot_pack(grid, window, panel_block, first_block, chip_rows):
    own_rows, order = panel_block.shape
    depth = window.shape[1]
    targets = len(grid.plane)
    return pl.pallas_call(
        functools.partial(pivot_pack_kernel, grid.xs, grid.ys, grid.ps, grid.cores),
        in_specs=[SMEM, HBM, HBM],
        out_specs=[VMEM] * targets,
        out_shape=[shape(chip_rows, depth + 2 * order, window.dtype)] * targets,
        scratch_shapes=[
            pltpu.VMEM((order, depth), window.dtype),
            pltpu.VMEM((own_rows + 2 * chip_rows, order), jnp.float32),
            pltpu.SemaphoreType.DMA,
            pltpu.SemaphoreType.DMA,
        ],
        compiler_params=PARAMS,
        cost_estimate=pl.CostEstimate(flops=0, bytes_accessed=36 * 2**20, transcendentals=0),
        name="pivot_pack",
    )(first_block, *placed(pltpu.HBM, window, panel_block))


def plain_pivot_pack(grid, window, panel_block, first_block, chip_rows):
    own_rows, order = panel_block.shape
    begin = grid.gc_index * own_rows
    padded = jnp.zeros((order + own_rows, order), jnp.float32)
    padded = lax.dynamic_update_slice_in_dim(padded, panel_block, jnp.minimum(begin, order), axis=0)
    out = []
    for a, b in grid.plane:
        start = ((grid.p ^ b) * grid.xs + (grid.x ^ a)) * chip_rows
        rows = masked_rows(rows_of(window, start, chip_rows), first_block, start)
        entries = rows_of(padded, start, chip_rows)
        high = lax.reduce_precision(entries, 8, 7)
        parts = [rows, high.astype(rows.dtype), (entries - high).astype(rows.dtype)]
        out.append(jnp.concatenate(parts, axis=1))
    return [jnp.where(grid.gr_index == 0, pack, jnp.zeros_like(pack)) for pack in out]


def panel_kernel(xs, ps, cores, *refs):
    shards, (panel_ref, sem) = refs[:-2], refs[-2:]
    depth, width = shards[0].shape
    gr = lax.axis_index("gr")
    x, core = gr // cores, gr % cores

    def place(i):
        (e, b), a = divmod(i // xs, ps), i % xs
        column = ((x ^ a) * cores + (core ^ e)) * width
        return panel_ref.at[b * depth : (b + 1) * depth, pl.ds(pl.multiple_of(column, width), width)]

    copy = pltpu.make_async_copy(shards[0], place(0), sem)
    copy.start()
    for i, shard in enumerate(shards):
        if i:
            place(i)[...] = shard[...]
    copy.wait()


def panel_assemble(grid, shards):
    depth, width = shards[0].shape
    return pl.pallas_call(
        functools.partial(panel_kernel, grid.xs, grid.ps, grid.cores),
        in_specs=[HBM] + [VMEM] * (len(shards) - 1),
        out_specs=VMEM,
        out_shape=shape(grid.ps * depth, grid.gr * width, shards[0].dtype),
        scratch_shapes=[pltpu.SemaphoreType.DMA],
        compiler_params=PARAMS,
        cost_estimate=QUICK,
        name="panel_assemble",
    )(*placed(pltpu.HBM, shards[0]), *placed(pltpu.VMEM, *shards[1:]))


def plain_panel_assemble(grid, shards):
    stack = jnp.stack(shards).reshape((grid.cores, grid.ps, grid.xs) + shards[0].shape)
    bands = []
    for b in range(grid.ps):
        blocks = [stack[grid.core ^ (gr % grid.cores), b, grid.x ^ (gr // grid.cores)] for gr in range(grid.gr)]
        bands.append(jnp.concatenate(blocks, axis=1))
    return jnp.concatenate(bands, axis=0)


def pivot_kernel(xs, ps, panel_ref, *refs):
    packs, total_ref = refs[:-1], refs[-1]
    order = total_ref.shape[1]
    depth = panel_ref.shape[0] // ps
    total = jnp.zeros(total_ref.shape, jnp.float32)
    for b in range(ps):
        rows = packs[b * xs][:, :depth]
        for a in range(1, xs):
            rows = rows + packs[b * xs + a][:, :depth]
        total = total - jnp.dot(rows, panel_ref[b * depth : (b + 1) * depth, :], preferred_element_type=jnp.float32)
    for pack in packs:
        total = total + pack[:, depth : depth + order].astype(jnp.float32) + pack[:, depth + order :].astype(jnp.float32)
    total_ref[...] = total


def pivot_part(grid, panel, packs):
    return pl.pallas_call(
        functools.partial(pivot_kernel, grid.xs, grid.ps),
        in_specs=[VMEM] * (1 + len(packs)),
        out_specs=VMEM,
        out_shape=shape(packs[0].shape[0], panel.shape[1], jnp.float32),
        compiler_params=PARAMS,
        cost_estimate=QUICK,
        name="pivot_part",
    )(*placed(pltpu.VMEM, panel, *packs))


def two_parts(value):
    high = value.astype(jnp.bfloat16)
    return high, (value - high.astype(jnp.float32)).astype(jnp.bfloat16)


def product(left, right):
    dot = functools.partial(jnp.dot, preferred_element_type=jnp.float32)
    return dot(left[0], right[0]) + (dot(left[0], right[1]) + dot(left[1], right[0]))


def inverse_kernel(xs, ys, ps, cores, *refs):
    pieces, (high_ref, low_ref, scale_ref, pivot_ref) = refs[:-4], refs[-4:]
    piece = pieces[0].shape[0]
    gr, p = lax.axis_index("gr"), pair_place(lax.axis_index("gc"), ys, ps)
    x, core = gr // cores, gr % cores
    for i, piece_ref in enumerate(pieces):
        e, n = divmod(i, xs * ps)
        chip = (p ^ n // xs) * xs + (x ^ n % xs)
        start = (chip * cores + (core ^ e)) * piece
        pivot_ref[pl.ds(pl.multiple_of(start, piece), piece), :] = piece_ref[...]
    order = pivot_ref.shape[0]
    square = (order, order)
    diagonal = lax.broadcasted_iota(jnp.int32, square, 0) == lax.broadcasted_iota(jnp.int32, square, 1)
    pivot = pivot_ref[...]
    scale = jnp.sum(jnp.where(diagonal, pivot, 0.0)) / order
    power = jnp.where(diagonal, 1.0, 0.0) - pivot / scale
    rest = power
    parts = two_parts(power)
    for step in range(NS_ITERS - 1):
        power = product(parts, parts)
        parts = two_parts(power)
        rest = rest + power + product(two_parts(rest), parts)
    high_ref[:order, :], low_ref[:order, :] = two_parts(rest)
    scale_ref[0] = scale


def inverse_rest(grid, pieces, spare):
    order = pieces[0].shape[1]
    half = shape(order + spare, order, jnp.bfloat16)
    return pl.pallas_call(
        functools.partial(inverse_kernel, grid.xs, grid.ys, grid.ps, grid.cores),
        in_specs=[VMEM] * len(pieces),
        out_specs=[VMEM, VMEM, SMEM],
        out_shape=[half, half, jax.ShapeDtypeStruct((1,), jnp.float32)],
        scratch_shapes=[pltpu.VMEM((order, order), jnp.float32)],
        compiler_params=PARAMS,
        cost_estimate=QUICK,
        name="pivot_inverse",
    )(*placed(pltpu.VMEM, *pieces))


def factor_kernel(schur_ref, high_ref, low_ref, out_ref):
    rows, order = out_ref.shape
    schur = schur_ref[...]
    rest = high_ref[:order, :], low_ref[:order, :]
    out_ref[...] = schur + product(two_parts(schur), rest)
    start = (lax.axis_index("gr") * lax.axis_size("gc") + lax.axis_index("gc")) * rows

    @pl.when(start < order)
    def _():
        here = start + lax.broadcasted_iota(jnp.int32, (rows, order), 0)
        across = lax.broadcasted_iota(jnp.int32, (rows, order), 1)
        place = pl.ds(pl.multiple_of(start, ROW_TILE), rows)
        inverse = jnp.where(here == across, 1.0, 0.0) + high_ref[place, :].astype(jnp.float32)
        inverse = inverse + low_ref[place, :].astype(jnp.float32)
        out_ref[...] = jnp.where(here < order, inverse, out_ref[...])


def factor_rows(schur, high, low):
    rows, order = schur.shape
    return pl.pallas_call(
        factor_kernel,
        in_specs=[VMEM, VMEM, VMEM],
        out_specs=VMEM,
        out_shape=jax.ShapeDtypeStruct((rows, order), jnp.float32),
        compiler_params=PARAMS,
        cost_estimate=QUICK,
        name="factor_rows",
    )(*placed(pltpu.VMEM, schur, high, low))


def masked_rows(part, first_block, first_row):
    col_first = jnp.repeat(first_block, BLK)
    row_ids = first_row + jnp.arange(part.shape[0], dtype=jnp.int32)
    inside = (row_ids // BLK)[:, None] >= col_first[None, :]
    return jnp.where(inside, part, jnp.zeros_like(part))


def body(factor_window, upper_panel, panel_block, first_block):
    grid = Grid()
    local_rows, depth = factor_window.shape
    own_rows, panel_width = panel_block.shape
    chip_rows = panel_width // (grid.xs * grid.ps)
    whole_tiles = upper_panel.shape[1] % LANES == 0 and chip_rows % ROW_TILE == 0

    order = list(range(grid.qs - 1, -1, -1))
    chunks = masked_chunks if own_rows % ROW_TILE == 0 else plain_masked_chunks
    chunks = functools.partial(chunks, grid, factor_window, first_block)
    others = range(1, grid.ps)
    columns = {k: [None] * grid.ps for k in order}

    packs = list((pivot_pack if whole_tiles else plain_pivot_pack)(grid, factor_window, panel_block, first_block, chip_rows))
    token = packs[0]
    shards = {(0, 0): upper_panel}
    first = [[(order[0], b)] for b in others]
    first = chunks(first, own_rows, upper_panel)
    for b in others:
        got = grid.swap(first[b - 1], dp=b)
        columns[order[0]][b] = got[:own_rows]
        shards[0, b] = jnp.concatenate(jnp.split(got[own_rows:], depth // upper_panel.shape[1], axis=1), axis=0)
    shards.update({(a, b): grid.swap(upper_panel, dx=a, dp=b) for a, b in grid.plane if a})
    shards[0, 1 % grid.ps] = after(shards[0, 1 % grid.ps], token)
    shards = [shards[place] for place in grid.plane]
    if grid.cores > 1:
        shards = shards + [grid.swap(shard, dcore=1) for shard in shards]
    panel = (panel_assemble if whole_tiles else plain_panel_assemble)(grid, shards)
    groups = [order[1:]]
    wanted = [([(k, b) for k in ks], ks, b) for ks in groups for b in others]
    own = order
    bands = chunks([names for names, _, _ in wanted] + [[(k, 0) for k in own]], own_rows)
    for n, k in enumerate(own):
        columns[k][0] = bands[-1][n * own_rows : (n + 1) * own_rows]

    def update(k):
        halves = [panel[j * depth : (j + 1) * depth] for j in range(grid.ps)]
        parts = [jnp.dot(part, half, preferred_element_type=jnp.float32) for part, half in zip(columns[k], halves)]
        return sum(parts[1:], parts[0])

    leading = update(order[0]).astype(WIRE)

    if grid.cores > 1:
        piece = chip_rows // grid.cores
    packs = [packs[0]] + [
        grid.permute(pack, lambda core: (0, 0, 0, 1) if core and grid.qs > 1 else (a, 0, b, 0))
        for pack, (a, b) in zip(packs[1:], grid.plane[1:])
    ]
    total = pivot_part(grid, panel, packs)
    if grid.cores > 1:
        total = jnp.where(grid.core == 0, total[:piece], grid.swap(total[piece:], dcore=1))
    bands = [grid.swap(band, dp=b) for band, (_, _, b) in zip(bands, wanted)]

    def arrive(lists, total):
        for band, (_, ks, b) in lists:
            band = after(band, total) if total is not None else band
            for n, k in enumerate(ks):
                columns[k][b] = band[n * own_rows : (n + 1) * own_rows]

    step, sums, last = 1, {}, {}
    while step < grid.qs:
        got = grid.swap(total, dq=step)
        if step == 1:
            sending = {order[0]: grid.swap(leading, dq=1)}
            total = total + got
            arrive(zip(bands, wanted), total)
            sums = {k: update(k) for k in order[1:]}
            sending.update({k: grid.swap(sums.pop(k).astype(WIRE), dq=1) for k in order[1:] if k & 1 and k > 1})
            last = {k: sums.pop(k).astype(WIRE) for k in order[1:] if k == 1 and k in sums}
        else:
            ready = {k: sums.pop(k).astype(WIRE) for k in list(sums) if k & step}
            got = after(got, *(value[:8, :LANES].astype(jnp.float32) for value in (*ready.values(), *last.values())))
            total = total + got
            for k, value in last.items():
                sums[0] = sums[0] + grid.swap(value, dq=1).astype(jnp.float32)
            last = {}
            sending = {k: grid.swap(value, dq=step) for k, value in ready.items()}
        for k, value in sending.items():
            sums[k ^ step] = sums[k ^ step] + value.astype(jnp.float32)
        step *= 2

    pieces = [total] + [grid.swap(total, dx=a, dp=b) for a, b in grid.plane[1:]]
    if grid.cores > 1:
        pieces = pieces + [grid.swap(piece, dcore=1) for piece in pieces]
    high, low, scale = inverse_rest(grid, pieces, own_rows)
    return factor_rows((panel_block - sums[0]) / scale[0], high, low)


def solution(mesh):
    return jax.shard_map(
        body,
        mesh=mesh,
        in_specs=(P("gr", "gc"), P("gc", "gr"), P(("gr", "gc"), None), P("gc")),
        out_specs=P(("gr", "gc"), None),
        check_vma=False,
    )
```

time: 69.1 us -> 65.2 us (0.944)
  Pallas kernels: 16.4 us -> 12.8 us
  local copies, waits for them, and re-layouts: 1.53 us -> 0.03 us
  waiting for transfers between devices: 23 us -> 24.1 us
    pallas_call x6 -> x8, Pallas kernels: 11.2 us -> 7.9 us  [the longest x1 4.02 us: inverse_rest(): pl.pallas_call(functools.partial(inverse_kernel, grid.xs, grid.ys, grid.p...]
    unnamed x12 -> x6, local copies, waits for them, and re-layouts: 1.51 us -> 0.01 us
    ppermute x24, waiting for transfers between devices: 23 us -> 24.1 us  [permute(): return lax.ppermute(value, ('gr', 'gc'), pairs)]
  transfers between devices with their start and end apart: 24 -> 24, of which waited for: 12 -> 10; matrix products, arithmetic and copies ran while one was open for 3% -> 3% of each run, Pallas kernels for 18% -> 15%
where the time goes in v4:
time: 65.2 us; the launch traced here: 64.8 us
  starting transfers between devices  24.5 us (38%)
  waiting for transfers between devices  24.1 us (37%)
  Pallas kernels  12.8 us (20%)
  matrix products  2.93 us (4%)
    ppermute x24, starting transfers between devices, permute(): return lax.ppermute(value, ('gr', 'gc'), pairs)  24.5 us
    ppermute x24, waiting for transfers between devices, permute(): return lax.ppermute(value, ('gr', 'gc'), pairs)  24.1 us
    pallas_call x1, Pallas kernels, inverse_rest(): pl.pallas_call(functools.partial(inverse_kernel, grid.xs, grid.ys, grid.p...  4.02 us
    dot_general x8, matrix products, update(): jnp.dot(part, half, preferred_element_type=jnp.float32)  2.93 us
    pallas_call x1, Pallas kernels, pivot_pack(): pl.pallas_call(functools.partial(pivot_pack_kernel, grid.xs, grid.ys, gri...  2.92 us
    pallas_call x2, Pallas kernels, masked_chunks(): pl.pallas_call(functools.partial(chunks_kernel, grid.ys, grid.ps, wanted,...  2.65 us
    pallas_call x1, Pallas kernels, factor_rows(): pl.pallas_call(factor_kernel, in_specs=[VMEM, VMEM, VMEM], out_specs=VMEM...  1.97 us
  transfers between devices with their start and end apart: 24, of which 10 were waited for; matrix products, arithmetic and copies ran while one was open for 3% of the time, Pallas kernels for 15%

profile of v4, /device:TPU:0, one launch (start us, length us, event | category | flops | bytes accessed | tf_op | source)
XLA Modules:
  0.0 64.8 jit_solution(4982033317150267336)
XLA Ops:
  0.0 1.1 %masked_chunks.3 = bf16[544,256]{1,0:T(8,128)(2,1)S(1)} custom-call(s32[2]{0:T(128)} %first.1, bf16[3328,256]{1,0:T(8,128)(2,1)} %window_ref.5, bf16[256,128]{1,0:T(8,128)(2,1)} %refs_0_.3), custom_call_target="tpu_custom_call" | custom-call | tf_op jit(solution)/shard_map/masked_chunks/pallas_call | solution.py:139
  1.1 3.1 %collective-permute-start.1 = (bf16[544,256]{1,0:T(8,128)(2,1)S(1)}, bf16[544,256]{1,0:T(8,128)(2,1)S(1)}, u32[]{:S(2)}, u32[]{:S(2)}) collective-permute-start(bf16[544,256]{1,0:T(8,128)(2,1)S(1)} %masked_chunks.3), channel_id=1, source_target_pairs={{0,2},{1,3},{2,0},{3,1},{4,6},{5,7},{6,4},{7,5},{8,10},{9,11},{10,... | collective-permute-start | bytes 835592 | tf_op jit(solution)/shard_map/ppermute | solution.py:53
  4.2 1.5 %collective-permute-start = (bf16[256,128]{1,0:T(8,128)(2,1)S(1)}, bf16[256,128]{1,0:T(8,128)(2,1)S(1)}, u32[]{:S(2)}, u32[]{:S(2)}) collective-permute-start(bf16[256,128]{1,0:T(8,128)(2,1)S(1)} %copy-done.2), channel_id=1, source_target_pairs={{0,16},{1,17},{2,18},{3,19},{4,20},{5,21},{6,22},{7,23},{8,24},{9,... | collective-permute-start | bytes 196616 | tf_op jit(solution)/shard_map/ppermute | solution.py:53
  5.7 2.9 %pivot_pack.1 = (bf16[128,1280]{1,0:T(8,128)(2,1)S(1)}, bf16[128,1280]{1,0:T(8,128)(2,1)}, bf16[128,1280]{1,0:T(8,128)(2,1)}, bf16[128,1280]{1,0:T(8,128)(2,1)}) custom-call(s32[2]{0:T(128)S(1)} %copy-done, bf16[3328,256]{1,0:T(8,128)(2,1)} %window_ref.5, f32[416,512]{1,0:T(8,128)} %block_ref.1), custom_call_target="tpu_custom_call" | custom-call | bytes 37748736 | tf_op jit(solution)/shard_map/pivot_pack/pallas_call | solution.py:215
  8.7 1.6 %collective-permute-start.10 = (bf16[128,1280]{1,0:T(8,128)(2,1)}, bf16[128,1280]{1,0:T(8,128)(2,1)S(1)}, u32[]{:S(2)}, u32[]{:S(2)}) collective-permute-start(bf16[128,1280]{1,0:T(8,128)(2,1)} %get-tuple-element.19), channel_id=1, source_target_pairs={{0,18},{1,19},{2,16},{3,17},{4,22},{5,23},{6,20},{7,21},{8,9},{9,8... | collective-permute-start | bytes 983048 | tf_op jit(solution)/shard_map/ppermute | solution.py:53
  10.3 1.5 %collective-permute-start.8 = (bf16[128,1280]{1,0:T(8,128)(2,1)}, bf16[128,1280]{1,0:T(8,128)(2,1)S(1)}, u32[]{:S(2)}, u32[]{:S(2)}) collective-permute-start(bf16[128,1280]{1,0:T(8,128)(2,1)} %get-tuple-element.17), channel_id=1, source_target_pairs={{0,16},{1,17},{2,18},{3,19},{4,20},{5,21},{6,22},{7,23},{8,9},{9,8... | collective-permute-start | bytes 983048 | tf_op jit(solution)/shard_map/ppermute | solution.py:53
  11.8 1.5 %collective-permute-start.9 = (bf16[128,1280]{1,0:T(8,128)(2,1)}, bf16[128,1280]{1,0:T(8,128)(2,1)S(1)}, u32[]{:S(2)}, u32[]{:S(2)}) collective-permute-start(bf16[128,1280]{1,0:T(8,128)(2,1)} %get-tuple-element.18), channel_id=1, source_target_pairs={{0,2},{1,3},{2,0},{3,1},{4,6},{5,7},{6,4},{7,5},{8,9},{9,8},{10,11... | collective-permute-start | bytes 983048 | tf_op jit(solution)/shard_map/ppermute | solution.py:53
  15.1 1.6 %masked_chunks.2 = (bf16[1248,256]{1,0:T(8,128)(2,1)S(1)}, bf16[1664,256]{1,0:T(8,128)(2,1)S(1)}) custom-call(s32[2]{0:T(128)} %first.1, bf16[3328,256]{1,0:T(8,128)(2,1)} %window_ref.5), custom_call_target="tpu_custom_call" | custom-call | tf_op jit(solution)/shard_map/masked_chunks/pallas_call | solution.py:139
  16.7 1.3 %collective-permute-start.7 = (bf16[1248,256]{1,0:T(8,128)(2,1)S(1)}, bf16[1248,256]{1,0:T(8,128)(2,1)S(1)}, u32[]{:S(2)}, u32[]{:S(2)}) collective-permute-start(bf16[1248,256]{1,0:T(8,128)(2,1)S(1)} %get-tuple-element.16), channel_id=1, source_target_pairs={{0,2},{1,3},{2,0},{3,1},{4,6},{5,7},{6,4},{7,5},{8,10},{9,11},{10,... | collective-permute-start | bytes 1916936 | tf_op jit(solution)/shard_map/ppermute | solution.py:53
  18.9 1.5 %collective-permute-done.8.refs_1_ = bf16[128,1280]{1,0:T(8,128)(2,1)S(1)} collective-permute-done((bf16[128,1280]{1,0:T(8,128)(2,1)}, bf16[128,1280]{1,0:T(8,128)(2,1)S(1)}, u32[]{:S(2)}, u32[]{:S(2)}) %collective-permute-start.8) | collective-permute-done | bytes 327712 | tf_op jit(solution)/shard_map/ppermute | solution.py:53
  21.2 1.1 %collective-permute-done.11 = f32[64,512]{1,0:T(8,128)S(1)} collective-permute-done((f32[64,512]{1,0:T(8,128)S(1)}, f32[64,512]{1,0:T(8,128)S(1)}, u32[]{:S(2)}, u32[]{:S(2)}) %collective-permute-start.11) | collective-permute-done | bytes 131104 | tf_op jit(solution)/shard_map/ppermute | solution.py:53
  22.3 1.9 %collective-permute-start.12 = (f32[64,512]{1,0:T(8,128)S(1)}, f32[64,512]{1,0:T(8,128)S(1)}, u32[]{:S(2)}, u32[]{:S(2)}) collective-permute-start(f32[64,512]{1,0:T(8,128)S(1)} %slice_select_fusion), channel_id=1, source_target_pairs={{0,1},{1,0},{2,3},{3,2},{4,5},{5,4},{6,7},{7,6},{8,9},{9,8},{10,11... | collective-permute-start | bytes 393224 | tf_op jit(solution)/shard_map/ppermute | solution.py:53
  24.7 4.0 %collective-permute-done.12 = f32[64,512]{1,0:T(8,128)S(1)} collective-permute-done((f32[64,512]{1,0:T(8,128)S(1)}, f32[64,512]{1,0:T(8,128)S(1)}, u32[]{:S(2)}, u32[]{:S(2)}) %collective-permute-start.12) | collective-permute-done | bytes 131104 | tf_op jit(solution)/shard_map/ppermute | solution.py:53
  28.7 2.7 %collective-permute-start.16 = (f32[64,512]{1,0:T(8,128)S(1)}, f32[64,512]{1,0:T(8,128)S(1)}, u32[]{:S(2)}, u32[]{:S(2)}) collective-permute-start(f32[64,512]{1,0:T(8,128)S(1)} %add.32.refs_1_), channel_id=1, source_target_pairs={{0,4},{1,5},{2,6},{3,7},{4,0},{5,1},{6,2},{7,3},{8,12},{9,13},{10,... | collective-permute-start | bytes 393224 | tf_op jit(solution)/shard_map/ppermute | solution.py:53
  31.3 4.7 %collective-permute-done.7.refs_0_ = bf16[1248,256]{1,0:T(8,128)(2,1)S(1)} collective-permute-done((bf16[1248,256]{1,0:T(8,128)(2,1)S(1)}, bf16[1248,256]{1,0:T(8,128)(2,1)S(1)}, u32[]{:S(2)}, u32[]{:S(2)}) %collective-permute-start.7) | collective-permute-done | bytes 639008 | tf_op jit(solution)/shard_map/ppermute | solution.py:53
  37.5 1.3 %collective-permute-start.17 = (f32[64,512]{1,0:T(8,128)S(1)}, f32[64,512]{1,0:T(8,128)S(1)}, u32[]{:S(2)}, u32[]{:S(2)}) collective-permute-start(f32[64,512]{1,0:T(8,128)S(1)} %add.40.refs_0_), channel_id=1, source_target_pairs={{0,16},{1,17},{2,18},{3,19},{4,20},{5,21},{6,22},{7,23},{8,24},{9,... | collective-permute-start | bytes 393224 | tf_op jit(solution)/shard_map/ppermute | solution.py:53
  38.8 1.9 %collective-permute-start.13 = (f16[416,512]{1,0:T(8,128)(2,1)S(1)}, f16[416,512]{1,0:T(8,128)(2,1)S(1)}, u32[]{:S(2)}, u32[]{:S(2)}) collective-permute-start(f16[416,512]{1,0:T(8,128)(2,1)S(1)} %fusion.5), channel_id=1, source_target_pairs={{0,1},{1,0},{2,3},{3,2},{4,5},{5,4},{6,7},{7,6},{8,9},{9,8},{10,11... | collective-permute-start | bytes 1277960 | tf_op jit(solution)/shard_map/ppermute | solution.py:53
  40.7 1.7 %collective-permute-start.15 = (f16[416,512]{1,0:T(8,128)(2,1)S(1)}, f16[416,512]{1,0:T(8,128)(2,1)S(1)}, u32[]{:S(2)}, u32[]{:S(2)}) collective-permute-start(f16[416,512]{1,0:T(8,128)(2,1)S(1)} %fusion.4), channel_id=1, source_target_pairs={{0,4},{1,5},{2,6},{3,7},{4,0},{5,1},{6,2},{7,3},{8,12},{9,13},{10,... | collective-permute-start | bytes 1277960 | tf_op jit(solution)/shard_map/ppermute | solution.py:53
  42.4 2.3 %collective-permute-start.18 = (f32[64,512]{1,0:T(8,128)S(1)}, f32[64,512]{1,0:T(8,128)S(1)}, u32[]{:S(2)}, u32[]{:S(2)}) collective-permute-start(f32[64,512]{1,0:T(8,128)S(1)} %add.40.refs_0_), channel_id=1, source_target_pairs={{0,2},{1,3},{2,0},{3,1},{4,6},{5,7},{6,4},{7,5},{8,10},{9,11},{10,... | collective-permute-start | bytes 393224 | tf_op jit(solution)/shard_map/ppermute | solution.py:53
  45.0 9.7 %collective-permute-done.18.refs_2_ = f32[64,512]{1,0:T(8,128)S(1)} collective-permute-done((f32[64,512]{1,0:T(8,128)S(1)}, f32[64,512]{1,0:T(8,128)S(1)}, u32[]{:S(2)}, u32[]{:S(2)}) %collective-permute-start.18) | collective-permute-done | bytes 131104 | tf_op jit(solution)/shard_map/ppermute | solution.py:53
  54.8 1.4 %collective-permute-done.19.refs_3_ = f32[64,512]{1,0:T(8,128)S(1)} collective-permute-done((f32[64,512]{1,0:T(8,128)S(1)}, f32[64,512]{1,0:T(8,128)S(1)}, u32[]{:S(2)}, u32[]{:S(2)}) %collective-permute-start.19) | collective-permute-done | bytes 131104 | tf_op jit(solution)/shard_map/ppermute | solution.py:53
  57.7 4.0 %pivot_inverse.1 = (bf16[928,512]{1,0:T(8,128)(2,1)S(1)}, bf16[928,512]{1,0:T(8,128)(2,1)S(1)}, f32[1]{0:T(128)}) custom-call(f32[64,512]{1,0:T(8,128)S(1)} %add.40.refs_0_, f32[64,512]{1,0:T(8,128)S(1)} %collective-permute-done.17.refs_1_, f32[64,512]{1,0:T(8,128)S(1)} %collective-permute-done.18.refs_2_, f32[64,512]{1,0:T(8,128)S(1)} %collective-permute-done.19.refs_3_, ...), custom_call_target="tpu_custom_call" | custom-call | tf_op jit(solution)/shard_map/pivot_inverse/pallas_call | solution.py:356
  61.7 1.0 %broadcast_divide_fusion.schur_ref = f32[416,512]{1,0:T(8,128)S(1)} fusion(f32[]{:T(128)} %bitcast, f32[416,512]{1,0:T(8,128)S(1)} %copy-done.1, f16[416,512]{1,0:T(8,128)(2,1)S(1)} %collective-permute-done.15, f16[416,512]{1,0:T(8,128)(2,1)S(1)} %collective-permute-done.13, f32[416,512]{1,0:T(8,128)S(1)} %fusion.13, ...), kind=kOutput, calls=%fused_computation.11 | convolution fusion | flops 110542848 | bytes 3883012 | tf_op jit(solution)/shard_map/dot_general | solution.py:442
  62.8 2.0 %factor_rows.1 = f32[416,512]{1,0:T(8,128)} custom-call(f32[416,512]{1,0:T(8,128)S(1)} %broadcast_divide_fusion.schur_ref, bf16[928,512]{1,0:T(8,128)(2,1)S(1)} %get-tuple-element.21.high_ref, bf16[928,512]{1,0:T(8,128)(2,1)S(1)} %get-tuple-element.22.low_ref), custom_call_target="tpu_custom_call" | custom-call | tf_op jit(solution)/shard_map/factor_rows/pallas_call | solution.py:387
  (56 shorter events, 7.3 us)
Async XLA Ops:
  1.1 10.7 %collective-permute-start.1 = (bf16[544,256]{1,0:T(8,128)(2,1)S(1)}, bf16[544,256]{1,0:T(8,128)(2,1)S(1)}, u32[]{:S(2)}, u32[]{:S(2)}) collective-permute-start(bf16[544,256]{1,0:T(8,128)(2,1)S(1)} %masked_chunks.3), channel_id=1, source_target_pairs={{0,2},{1,3},{2,0},{3,1},{4,6},{5,7},{6,4},{7,5},{8,10},{9,11},{10,... | collective-permute-start | bytes 835592 | tf_op jit(solution)/shard_map/ppermute | solution.py:53
  4.2 9.1 %collective-permute-start = (bf16[256,128]{1,0:T(8,128)(2,1)S(1)}, bf16[256,128]{1,0:T(8,128)(2,1)S(1)}, u32[]{:S(2)}, u32[]{:S(2)}) collective-permute-start(bf16[256,128]{1,0:T(8,128)(2,1)S(1)} %copy-done.2), channel_id=1, source_target_pairs={{0,16},{1,17},{2,18},{3,19},{4,20},{5,21},{6,22},{7,23},{8,24},{9,... | collective-permute-start | bytes 196616 | tf_op jit(solution)/shard_map/ppermute | solution.py:53
  5.7 7.7 %collective-permute-start.2 = (bf16[256,128]{1,0:T(8,128)(2,1)S(1)}, bf16[256,128]{1,0:T(8,128)(2,1)S(1)}, u32[]{:S(2)}, u32[]{:S(2)}) collective-permute-start(bf16[256,128]{1,0:T(8,128)(2,1)S(1)} %copy-done.2), channel_id=1, source_target_pairs={{0,18},{1,19},{2,16},{3,17},{4,22},{5,23},{6,20},{7,21},{8,26},{9,... | collective-permute-start | bytes 196616 | tf_op jit(solution)/shard_map/ppermute | solution.py:53
  8.7 10.3 %collective-permute-start.10 = (bf16[128,1280]{1,0:T(8,128)(2,1)}, bf16[128,1280]{1,0:T(8,128)(2,1)S(1)}, u32[]{:S(2)}, u32[]{:S(2)}) collective-permute-start(bf16[128,1280]{1,0:T(8,128)(2,1)} %get-tuple-element.19), channel_id=1, source_target_pairs={{0,18},{1,19},{2,16},{3,17},{4,22},{5,23},{6,20},{7,21},{8,9},{9,8... | collective-permute-start | bytes 983048 | tf_op jit(solution)/shard_map/ppermute | solution.py:53
  10.3 10.2 %collective-permute-start.8 = (bf16[128,1280]{1,0:T(8,128)(2,1)}, bf16[128,1280]{1,0:T(8,128)(2,1)S(1)}, u32[]{:S(2)}, u32[]{:S(2)}) collective-permute-start(bf16[128,1280]{1,0:T(8,128)(2,1)} %get-tuple-element.17), channel_id=1, source_target_pairs={{0,16},{1,17},{2,18},{3,19},{4,20},{5,21},{6,22},{7,23},{8,9},{9,8... | collective-permute-start | bytes 983048 | tf_op jit(solution)/shard_map/ppermute | solution.py:53
  11.8 8.7 %collective-permute-start.9 = (bf16[128,1280]{1,0:T(8,128)(2,1)}, bf16[128,1280]{1,0:T(8,128)(2,1)S(1)}, u32[]{:S(2)}, u32[]{:S(2)}) collective-permute-start(bf16[128,1280]{1,0:T(8,128)(2,1)} %get-tuple-element.18), channel_id=1, source_target_pairs={{0,2},{1,3},{2,0},{3,1},{4,6},{5,7},{6,4},{7,5},{8,9},{9,8},{10,11... | collective-permute-start | bytes 983048 | tf_op jit(solution)/shard_map/ppermute | solution.py:53
  13.3 1.3 %collective-permute-start.3 = (bf16[256,128]{1,0:T(8,128)(2,1)S(1)}, bf16[256,128]{1,0:T(8,128)(2,1)S(1)}, u32[]{:S(2)}, u32[]{:S(2)}) collective-permute-start(bf16[256,128]{1,0:T(8,128)(2,1)S(1)} %copy-done.2), channel_id=1, source_target_pairs={{0,8},{1,9},{2,10},{3,11},{4,12},{5,13},{6,14},{7,15},{8,0},{9,1},... | collective-permute-start | bytes 196616 | tf_op jit(solution)/shard_map/ppermute | solution.py:53
  13.4 1.4 %collective-permute-start.4 = (bf16[256,128]{1,0:T(8,128)(2,1)S(1)}, bf16[256,128]{1,0:T(8,128)(2,1)S(1)}, u32[]{:S(2)}, u32[]{:S(2)}) collective-permute-start(bf16[256,128]{1,0:T(8,128)(2,1)S(1)} %collective-permute-done.refs_1_), channel_id=1, source_target_pairs={{0,8},{1,9},{2,10},{3,11},{4,12},{5,13},{6,14},{7,15},{8,0},{9,1},... | collective-permute-start | bytes 196616 | tf_op jit(solution)/shard_map/ppermute | solution.py:53
  14.6 2.1 %collective-permute-start.6 = (bf16[256,128]{1,0:T(8,128)(2,1)S(1)}, bf16[256,128]{1,0:T(8,128)(2,1)S(1)}, u32[]{:S(2)}, u32[]{:S(2)}) collective-permute-start(bf16[256,128]{1,0:T(8,128)(2,1)S(1)} %collective-permute-done.2.refs_3_), channel_id=1, source_target_pairs={{0,8},{1,9},{2,10},{3,11},{4,12},{5,13},{6,14},{7,15},{8,0},{9,1},... | collective-permute-start | bytes 196616 | tf_op jit(solution)/shard_map/ppermute | solution.py:53
  14.8 3.3 %collective-permute-start.5 = (bf16[256,128]{1,0:T(8,128)(2,1)S(1)}, bf16[256,128]{1,0:T(8,128)(2,1)S(1)}, u32[]{:S(2)}, u32[]{:S(2)}) collective-permute-start(bf16[256,128]{1,0:T(8,128)(2,1)S(1)} %after.3.refs_2_), channel_id=1, source_target_pairs={{0,8},{1,9},{2,10},{3,11},{4,12},{5,13},{6,14},{7,15},{8,0},{9,1},... | collective-permute-start | bytes 196616 | tf_op jit(solution)/shard_map/ppermute | solution.py:53
  16.7 19.3 %collective-permute-start.7 = (bf16[1248,256]{1,0:T(8,128)(2,1)S(1)}, bf16[1248,256]{1,0:T(8,128)(2,1)S(1)}, u32[]{:S(2)}, u32[]{:S(2)}) collective-permute-start(bf16[1248,256]{1,0:T(8,128)(2,1)S(1)} %get-tuple-element.16), channel_id=1, source_target_pairs={{0,2},{1,3},{2,0},{3,1},{4,6},{5,7},{6,4},{7,5},{8,10},{9,11},{10,... | collective-permute-start | bytes 1916936 | tf_op jit(solution)/shard_map/ppermute | solution.py:53
  20.8 1.4 %collective-permute-start.11 = (f32[64,512]{1,0:T(8,128)S(1)}, f32[64,512]{1,0:T(8,128)S(1)}, u32[]{:S(2)}, u32[]{:S(2)}) collective-permute-start(f32[64,512]{1,0:T(8,128)S(1)} %slice.67), channel_id=1, source_target_pairs={{0,8},{1,9},{2,10},{3,11},{4,12},{5,13},{6,14},{7,15},{8,0},{9,1},... | collective-permute-start | bytes 393224 | tf_op jit(solution)/shard_map/ppermute | solution.py:53
  22.3 6.4 %collective-permute-start.12 = (f32[64,512]{1,0:T(8,128)S(1)}, f32[64,512]{1,0:T(8,128)S(1)}, u32[]{:S(2)}, u32[]{:S(2)}) collective-permute-start(f32[64,512]{1,0:T(8,128)S(1)} %slice_select_fusion), channel_id=1, source_target_pairs={{0,1},{1,0},{2,3},{3,2},{4,5},{5,4},{6,7},{7,6},{8,9},{9,8},{10,11... | collective-permute-start | bytes 393224 | tf_op jit(solution)/shard_map/ppermute | solution.py:53
  24.5 12.7 %collective-permute-start.14 = (f16[416,512]{1,0:T(8,128)(2,1)S(1)}, f16[416,512]{1,0:T(8,128)(2,1)S(1)}, u32[]{:S(2)}, u32[]{:S(2)}) collective-permute-start(f16[416,512]{1,0:T(8,128)(2,1)S(1)} %fusion.6), channel_id=1, source_target_pairs={{0,1},{1,0},{2,3},{3,2},{4,5},{5,4},{6,7},{7,6},{8,9},{9,8},{10,11... | collective-permute-start | bytes 1277960 | tf_op jit(solution)/shard_map/ppermute | solution.py:53
  28.7 8.8 %collective-permute-start.16 = (f32[64,512]{1,0:T(8,128)S(1)}, f32[64,512]{1,0:T(8,128)S(1)}, u32[]{:S(2)}, u32[]{:S(2)}) collective-permute-start(f32[64,512]{1,0:T(8,128)S(1)} %add.32.refs_1_), channel_id=1, source_target_pairs={{0,4},{1,5},{2,6},{3,7},{4,0},{5,1},{6,2},{7,3},{8,12},{9,13},{10,... | collective-permute-start | bytes 393224 | tf_op jit(solution)/shard_map/ppermute | solution.py:53
  37.5 7.5 %collective-permute-start.17 = (f32[64,512]{1,0:T(8,128)S(1)}, f32[64,512]{1,0:T(8,128)S(1)}, u32[]{:S(2)}, u32[]{:S(2)}) collective-permute-start(f32[64,512]{1,0:T(8,128)S(1)} %add.40.refs_0_), channel_id=1, source_target_pairs={{0,16},{1,17},{2,18},{3,19},{4,20},{5,21},{6,22},{7,23},{8,24},{9,... | collective-permute-start | bytes 393224 | tf_op jit(solution)/shard_map/ppermute | solution.py:53
  38.8 22.9 %collective-permute-start.13 = (f16[416,512]{1,0:T(8,128)(2,1)S(1)}, f16[416,512]{1,0:T(8,128)(2,1)S(1)}, u32[]{:S(2)}, u32[]{:S(2)}) collective-permute-start(f16[416,512]{1,0:T(8,128)(2,1)S(1)} %fusion.5), channel_id=1, source_target_pairs={{0,1},{1,0},{2,3},{3,2},{4,5},{5,4},{6,7},{7,6},{8,9},{9,8},{10,11... | collective-permute-start | bytes 1277960 | tf_op jit(solution)/shard_map/ppermute | solution.py:53
  40.7 21.0 %collective-permute-start.15 = (f16[416,512]{1,0:T(8,128)(2,1)S(1)}, f16[416,512]{1,0:T(8,128)(2,1)S(1)}, u32[]{:S(2)}, u32[]{:S(2)}) collective-permute-start(f16[416,512]{1,0:T(8,128)(2,1)S(1)} %fusion.4), channel_id=1, source_target_pairs={{0,4},{1,5},{2,6},{3,7},{4,0},{5,1},{6,2},{7,3},{8,12},{9,13},{10,... | collective-permute-start | bytes 1277960 | tf_op jit(solution)/shard_map/ppermute | solution.py:53
  42.4 12.4 %collective-permute-start.18 = (f32[64,512]{1,0:T(8,128)S(1)}, f32[64,512]{1,0:T(8,128)S(1)}, u32[]{:S(2)}, u32[]{:S(2)}) collective-permute-start(f32[64,512]{1,0:T(8,128)S(1)} %add.40.refs_0_), channel_id=1, source_target_pairs={{0,2},{1,3},{2,0},{3,1},{4,6},{5,7},{6,4},{7,5},{8,10},{9,11},{10,... | collective-permute-start | bytes 393224 | tf_op jit(solution)/shard_map/ppermute | solution.py:53
  44.7 11.5 %collective-permute-start.19 = (f32[64,512]{1,0:T(8,128)S(1)}, f32[64,512]{1,0:T(8,128)S(1)}, u32[]{:S(2)}, u32[]{:S(2)}) collective-permute-start(f32[64,512]{1,0:T(8,128)S(1)} %add.40.refs_0_), channel_id=1, source_target_pairs={{0,18},{1,19},{2,16},{3,17},{4,22},{5,23},{6,20},{7,21},{8,26},{9,... | collective-permute-start | bytes 393224 | tf_op jit(solution)/shard_map/ppermute | solution.py:53
  45.0 11.1 %collective-permute-start.20 = (f32[64,512]{1,0:T(8,128)S(1)}, f32[64,512]{1,0:T(8,128)S(1)}, u32[]{:S(2)}, u32[]{:S(2)}) collective-permute-start(f32[64,512]{1,0:T(8,128)S(1)} %add.40.refs_0_), channel_id=1, source_target_pairs={{0,8},{1,9},{2,10},{3,11},{4,12},{5,13},{6,14},{7,15},{8,0},{9,1},... | collective-permute-start | bytes 393224 | tf_op jit(solution)/shard_map/ppermute | solution.py:53
  54.8 2.2 %collective-permute-start.21 = (f32[64,512]{1,0:T(8,128)S(1)}, f32[64,512]{1,0:T(8,128)S(1)}, u32[]{:S(2)}, u32[]{:S(2)}) collective-permute-start(f32[64,512]{1,0:T(8,128)S(1)} %collective-permute-done.17.refs_1_), channel_id=1, source_target_pairs={{0,8},{1,9},{2,10},{3,11},{4,12},{5,13},{6,14},{7,15},{8,0},{9,1},... | collective-permute-start | bytes 393224 | tf_op jit(solution)/shard_map/ppermute | solution.py:53
  56.2 1.3 %collective-permute-start.22 = (f32[64,512]{1,0:T(8,128)S(1)}, f32[64,512]{1,0:T(8,128)S(1)}, u32[]{:S(2)}, u32[]{:S(2)}) collective-permute-start(f32[64,512]{1,0:T(8,128)S(1)} %collective-permute-done.18.refs_2_), channel_id=1, source_target_pairs={{0,8},{1,9},{2,10},{3,11},{4,12},{5,13},{6,14},{7,15},{8,0},{9,1},... | collective-permute-start | bytes 393224 | tf_op jit(solution)/shard_map/ppermute | solution.py:53
  56.2 1.5 %collective-permute-start.23 = (f32[64,512]{1,0:T(8,128)S(1)}, f32[64,512]{1,0:T(8,128)S(1)}, u32[]{:S(2)}, u32[]{:S(2)}) collective-permute-start(f32[64,512]{1,0:T(8,128)S(1)} %collective-permute-done.19.refs_3_), channel_id=1, source_target_pairs={{0,8},{1,9},{2,10},{3,11},{4,12},{5,13},{6,14},{7,15},{8,0},{9,1},... | collective-permute-start | bytes 393224 | tf_op jit(solution)/shard_map/ppermute | solution.py:53
  (3 other events, 34.2 us)

commit v5 on v4

--- a/solution.py
+++ b/solution.py
@@ -143,7 +143,7 @@
         out_shape=[shape(count, window.shape[1], window.dtype) for count in rows],
         scratch_shapes=scratch,
         compiler_params=PARAMS,
-        cost_estimate=QUICK,
+        cost_estimate=pl.CostEstimate(flops=0, bytes_accessed=36 * 2**20, transcendentals=0),
         name="masked_chunks",
     )(*placed(pltpu.HBM, first_block, window, *shard))
 
@@ -224,7 +224,7 @@
             pltpu.SemaphoreType.DMA,
         ],
         compiler_params=PARAMS,
-        cost_estimate=pl.CostEstimate(flops=0, bytes_accessed=36 * 2**20, transcendentals=0),
+        cost_estimate=QUICK,
         name="pivot_pack",
     )(first_block, *placed(pltpu.HBM, window, panel_block))
 
@@ -479,15 +479,22 @@
                 sums[0] = sums[0] + grid.swap(value, dq=1).astype(jnp.float32)
             last = {}
             sending = {k: grid.swap(value, dq=step) for k, value in ready.items()}
+        if step * 2 >= grid.qs:
+            break
         for k, value in sending.items():
             sums[k ^ step] = sums[k ^ step] + value.astype(jnp.float32)
         step *= 2
-
-    pieces = [total] + [grid.swap(total, dx=a, dp=b) for a, b in grid.plane[1:]]
+    base = after(panel_block - sums[0], total)
+
+    pieces = [total] + [grid.swap(total, dx=a) for a in range(1, grid.xs)]
+    later = after(total, pieces[-1])
+    pieces = pieces + [grid.swap(later, dx=a, dp=b) for a, b in grid.plane if b]
     if grid.cores > 1:
         pieces = pieces + [grid.swap(piece, dcore=1) for piece in pieces]
+    pieces[0] = after(pieces[0], base)
     high, low, scale = inverse_rest(grid, pieces, own_rows)
-    return factor_rows((panel_block - sums[0]) / scale[0], high, low)
+    schur_rows = base - sum(value.astype(jnp.float32) for value in sending.values())
+    return factor_rows(schur_rows / scale[0], high, low)
 
 
 def solution(mesh):

time: 65.2 us -> 63.8 us (0.979)
  waiting for transfers between devices: 24.1 us -> 23 us
  matrix products: 2.93 us -> 2.15 us
  other arithmetic: 0.07 us -> 0.84 us
    ppermute x24, waiting for transfers between devices: 24.1 us -> 23 us  [permute(): return lax.ppermute(value, ('gr', 'gc'), pairs)]
    div x0 -> x1, other arithmetic: none -> 0.77 us  [body(): return factor_rows(schur_rows / scale[0], high, low)]
    dot_general x8, matrix products: 2.93 us -> 2.15 us  [update(): jnp.dot(part, half, preferred_element_type=jnp.float32)]
  transfers between devices with their start and end apart: 24 -> 24, of which waited for: 10 -> 11; matrix products, arithmetic and copies ran while one was open for 3% -> 4% of each run, Pallas kernels for 15% -> 15%
where the time goes in v5:
time: 63.8 us; the launch traced here: 63.6 us
  starting transfers between devices  24.5 us (38%)
  waiting for transfers between devices  23 us (36%)
  Pallas kernels  12.8 us (20%)
  matrix products  2.15 us (3%)
  other arithmetic  0.84 us (1%)
    ppermute x24, starting transfers between devices, permute(): return lax.ppermute(value, ('gr', 'gc'), pairs)  24.5 us
    ppermute x24, waiting for transfers between devices, permute(): return lax.ppermute(value, ('gr', 'gc'), pairs)  23 us
    pallas_call x1, Pallas kernels, inverse_rest(): pl.pallas_call(functools.partial(inverse_kernel, grid.xs, grid.ys, grid.p...  4.02 us
    pallas_call x1, Pallas kernels, pivot_pack(): pl.pallas_call(functools.partial(pivot_pack_kernel, grid.xs, grid.ys, gri...  2.92 us
    pallas_call x2, Pallas kernels, masked_chunks(): pl.pallas_call(functools.partial(chunks_kernel, grid.ys, grid.ps, wanted,...  2.65 us
    dot_general x8, matrix products, update(): jnp.dot(part, half, preferred_element_type=jnp.float32)  2.15 us
    pallas_call x1, Pallas kernels, factor_rows(): pl.pallas_call(factor_kernel, in_specs=[VMEM, VMEM, VMEM], out_specs=VMEM...  1.97 us
  transfers between devices with their start and end apart: 24, of which 11 were waited for; matrix products, arithmetic and copies ran while one was open for 4% of the time, Pallas kernels for 15%

profile of v5, /device:TPU:0, one launch (start us, length us, event | category | flops | bytes accessed | tf_op | source)
XLA Modules:
  0.0 63.6 jit_solution(12864507401129737840)
XLA Ops:
  0.0 1.1 %masked_chunks.3 = bf16[544,256]{1,0:T(8,128)(2,1)S(1)} custom-call(s32[2]{0:T(128)} %first.1, bf16[3328,256]{1,0:T(8,128)(2,1)} %window_ref.5, bf16[256,128]{1,0:T(8,128)(2,1)} %refs_0_.3), custom_call_target="tpu_custom_call" | custom-call | bytes 37748736 | tf_op jit(solution)/shard_map/masked_chunks/pallas_call | solution.py:139
  1.1 3.1 %collective-permute-start.1 = (bf16[544,256]{1,0:T(8,128)(2,1)S(1)}, bf16[544,256]{1,0:T(8,128)(2,1)S(1)}, u32[]{:S(2)}, u32[]{:S(2)}) collective-permute-start(bf16[544,256]{1,0:T(8,128)(2,1)S(1)} %masked_chunks.3), channel_id=1, source_target_pairs={{0,2},{1,3},{2,0},{3,1},{4,6},{5,7},{6,4},{7,5},{8,10},{9,11},{10,... | collective-permute-start | bytes 835592 | tf_op jit(solution)/shard_map/ppermute | solution.py:53
  4.2 1.5 %collective-permute-start = (bf16[256,128]{1,0:T(8,128)(2,1)S(1)}, bf16[256,128]{1,0:T(8,128)(2,1)S(1)}, u32[]{:S(2)}, u32[]{:S(2)}) collective-permute-start(bf16[256,128]{1,0:T(8,128)(2,1)S(1)} %copy-done.2), channel_id=1, source_target_pairs={{0,16},{1,17},{2,18},{3,19},{4,20},{5,21},{6,22},{7,23},{8,24},{9,... | collective-permute-start | bytes 196616 | tf_op jit(solution)/shard_map/ppermute | solution.py:53
  5.7 2.9 %pivot_pack.1 = (bf16[128,1280]{1,0:T(8,128)(2,1)S(1)}, bf16[128,1280]{1,0:T(8,128)(2,1)}, bf16[128,1280]{1,0:T(8,128)(2,1)}, bf16[128,1280]{1,0:T(8,128)(2,1)}) custom-call(s32[2]{0:T(128)S(1)} %copy-done, bf16[3328,256]{1,0:T(8,128)(2,1)} %window_ref.5, f32[416,512]{1,0:T(8,128)} %block_ref.1), custom_call_target="tpu_custom_call" | custom-call | tf_op jit(solution)/shard_map/pivot_pack/pallas_call | solution.py:215
  8.7 1.6 %collective-permute-start.10 = (bf16[128,1280]{1,0:T(8,128)(2,1)}, bf16[128,1280]{1,0:T(8,128)(2,1)S(1)}, u32[]{:S(2)}, u32[]{:S(2)}) collective-permute-start(bf16[128,1280]{1,0:T(8,128)(2,1)} %get-tuple-element.19), channel_id=1, source_target_pairs={{0,18},{1,19},{2,16},{3,17},{4,22},{5,23},{6,20},{7,21},{8,9},{9,8... | collective-permute-start | bytes 983048 | tf_op jit(solution)/shard_map/ppermute | solution.py:53
  10.3 1.5 %collective-permute-start.8 = (bf16[128,1280]{1,0:T(8,128)(2,1)}, bf16[128,1280]{1,0:T(8,128)(2,1)S(1)}, u32[]{:S(2)}, u32[]{:S(2)}) collective-permute-start(bf16[128,1280]{1,0:T(8,128)(2,1)} %get-tuple-element.17), channel_id=1, source_target_pairs={{0,16},{1,17},{2,18},{3,19},{4,20},{5,21},{6,22},{7,23},{8,9},{9,8... | collective-permute-start | bytes 983048 | tf_op jit(solution)/shard_map/ppermute | solution.py:53
  11.8 1.5 %collective-permute-start.9 = (bf16[128,1280]{1,0:T(8,128)(2,1)}, bf16[128,1280]{1,0:T(8,128)(2,1)S(1)}, u32[]{:S(2)}, u32[]{:S(2)}) collective-permute-start(bf16[128,1280]{1,0:T(8,128)(2,1)} %get-tuple-element.18), channel_id=1, source_target_pairs={{0,2},{1,3},{2,0},{3,1},{4,6},{5,7},{6,4},{7,5},{8,9},{9,8},{10,11... | collective-permute-start | bytes 983048 | tf_op jit(solution)/shard_map/ppermute | solution.py:53
  15.1 1.6 %masked_chunks.2 = (bf16[1248,256]{1,0:T(8,128)(2,1)S(1)}, bf16[1664,256]{1,0:T(8,128)(2,1)S(1)}) custom-call(s32[2]{0:T(128)} %first.1, bf16[3328,256]{1,0:T(8,128)(2,1)} %window_ref.5), custom_call_target="tpu_custom_call" | custom-call | bytes 37748736 | tf_op jit(solution)/shard_map/masked_chunks/pallas_call | solution.py:139
  16.7 1.3 %collective-permute-start.7 = (bf16[1248,256]{1,0:T(8,128)(2,1)S(1)}, bf16[1248,256]{1,0:T(8,128)(2,1)S(1)}, u32[]{:S(2)}, u32[]{:S(2)}) collective-permute-start(bf16[1248,256]{1,0:T(8,128)(2,1)S(1)} %get-tuple-element.16), channel_id=1, source_target_pairs={{0,2},{1,3},{2,0},{3,1},{4,6},{5,7},{6,4},{7,5},{8,10},{9,11},{10,... | collective-permute-start | bytes 1916936 | tf_op jit(solution)/shard_map/ppermute | solution.py:53
  18.0 0.9 %panel_assemble.1.panel_ref = bf16[512,512]{1,0:T(8,128)(2,1)S(1)} custom-call(bf16[256,128]{1,0:T(8,128)(2,1)} %refs_0_.3, bf16[256,128]{1,0:T(8,128)(2,1)S(1)} %collective-permute-done.refs_1_, bf16[256,128]{1,0:T(8,128)(2,1)S(1)} %after.6.refs_2_, bf16[256,128]{1,0:T(8,128)(2,1)S(1)} %collective-permute-done.2.refs_3_, ...), custom_call_target="tpu_custom_call" | custom-call | tf_op jit(solution)/shard_map/panel_assemble/pallas_call | solution.py:269
  18.9 1.5 %collective-permute-done.8.refs_1_ = bf16[128,1280]{1,0:T(8,128)(2,1)S(1)} collective-permute-done((bf16[128,1280]{1,0:T(8,128)(2,1)}, bf16[128,1280]{1,0:T(8,128)(2,1)S(1)}, u32[]{:S(2)}, u32[]{:S(2)}) %collective-permute-start.8) | collective-permute-done | bytes 327712 | tf_op jit(solution)/shard_map/ppermute | solution.py:53
  21.2 1.1 %collective-permute-done.11 = f32[64,512]{1,0:T(8,128)S(1)} collective-permute-done((f32[64,512]{1,0:T(8,128)S(1)}, f32[64,512]{1,0:T(8,128)S(1)}, u32[]{:S(2)}, u32[]{:S(2)}) %collective-permute-start.11) | collective-permute-done | bytes 131104 | tf_op jit(solution)/shard_map/ppermute | solution.py:53
  22.2 1.9 %collective-permute-start.12 = (f32[64,512]{1,0:T(8,128)S(1)}, f32[64,512]{1,0:T(8,128)S(1)}, u32[]{:S(2)}, u32[]{:S(2)}) collective-permute-start(f32[64,512]{1,0:T(8,128)S(1)} %slice_select_fusion), channel_id=1, source_target_pairs={{0,1},{1,0},{2,3},{3,2},{4,5},{5,4},{6,7},{7,6},{8,9},{9,8},{10,11... | collective-permute-start | bytes 393224 | tf_op jit(solution)/shard_map/ppermute | solution.py:53
  24.7 4.0 %collective-permute-done.12 = f32[64,512]{1,0:T(8,128)S(1)} collective-permute-done((f32[64,512]{1,0:T(8,128)S(1)}, f32[64,512]{1,0:T(8,128)S(1)}, u32[]{:S(2)}, u32[]{:S(2)}) %collective-permute-start.12) | collective-permute-done | bytes 131104 | tf_op jit(solution)/shard_map/ppermute | solution.py:53
  28.7 2.7 %collective-permute-start.14 = (f32[64,512]{1,0:T(8,128)S(1)}, f32[64,512]{1,0:T(8,128)S(1)}, u32[]{:S(2)}, u32[]{:S(2)}) collective-permute-start(f32[64,512]{1,0:T(8,128)S(1)} %add.29.refs_1_), channel_id=1, source_target_pairs={{0,4},{1,5},{2,6},{3,7},{4,0},{5,1},{6,2},{7,3},{8,12},{9,13},{10,... | collective-permute-start | bytes 393224 | tf_op jit(solution)/shard_map/ppermute | solution.py:53
  31.3 4.7 %collective-permute-done.7.refs_0_ = bf16[1248,256]{1,0:T(8,128)(2,1)S(1)} collective-permute-done((bf16[1248,256]{1,0:T(8,128)(2,1)S(1)}, bf16[1248,256]{1,0:T(8,128)(2,1)S(1)}, u32[]{:S(2)}, u32[]{:S(2)}) %collective-permute-start.7) | collective-permute-done | bytes 639008 | tf_op jit(solution)/shard_map/ppermute | solution.py:53
  36.6 1.6 %collective-permute-start.13 = (f16[416,512]{1,0:T(8,128)(2,1)S(1)}, f16[416,512]{1,0:T(8,128)(2,1)S(1)}, u32[]{:S(2)}, u32[]{:S(2)}) collective-permute-start(f16[416,512]{1,0:T(8,128)(2,1)S(1)} %fusion.4), channel_id=1, source_target_pairs={{0,1},{1,0},{2,3},{3,2},{4,5},{5,4},{6,7},{7,6},{8,9},{9,8},{10,11... | collective-permute-start | bytes 1277960 | tf_op jit(solution)/shard_map/ppermute | solution.py:53
  38.8 1.9 %collective-permute-start.17 = (f32[64,512]{1,0:T(8,128)S(1)}, f32[64,512]{1,0:T(8,128)S(1)}, u32[]{:S(2)}, u32[]{:S(2)}) collective-permute-start(f32[64,512]{1,0:T(8,128)S(1)} %add.36.refs_1_.refs_0_), channel_id=1, source_target_pairs={{0,16},{1,17},{2,18},{3,19},{4,20},{5,21},{6,22},{7,23},{8,24},{9,... | collective-permute-start | bytes 393224 | tf_op jit(solution)/shard_map/ppermute | solution.py:53
  41.3 2.6 %collective-permute-done.17.refs_1_ = f32[64,512]{1,0:T(8,128)S(1)} collective-permute-done((f32[64,512]{1,0:T(8,128)S(1)}, f32[64,512]{1,0:T(8,128)S(1)}, u32[]{:S(2)}, u32[]{:S(2)}) %collective-permute-start.17) | collective-permute-done | bytes 131104 | tf_op jit(solution)/shard_map/ppermute | solution.py:53
  44.4 2.8 %collective-permute-start.19 = (f32[64,512]{1,0:T(8,128)S(1)}, f32[64,512]{1,0:T(8,128)S(1)}, u32[]{:S(2)}, u32[]{:S(2)}) collective-permute-start(f32[64,512]{1,0:T(8,128)S(1)} %after.11), channel_id=1, source_target_pairs={{0,18},{1,19},{2,16},{3,17},{4,22},{5,23},{6,20},{7,21},{8,26},{9,... | collective-permute-start | bytes 393224 | tf_op jit(solution)/shard_map/ppermute | solution.py:53
  47.5 6.2 %collective-permute-done.18.refs_2_ = f32[64,512]{1,0:T(8,128)S(1)} collective-permute-done((f32[64,512]{1,0:T(8,128)S(1)}, f32[64,512]{1,0:T(8,128)S(1)}, u32[]{:S(2)}, u32[]{:S(2)}) %collective-permute-start.18) | collective-permute-done | bytes 131104 | tf_op jit(solution)/shard_map/ppermute | solution.py:53
  53.7 1.4 %collective-permute-done.19.refs_3_ = f32[64,512]{1,0:T(8,128)S(1)} collective-permute-done((f32[64,512]{1,0:T(8,128)S(1)}, f32[64,512]{1,0:T(8,128)S(1)}, u32[]{:S(2)}, u32[]{:S(2)}) %collective-permute-start.19) | collective-permute-done | bytes 131104 | tf_op jit(solution)/shard_map/ppermute | solution.py:53
  56.7 4.0 %pivot_inverse.1 = (bf16[928,512]{1,0:T(8,128)(2,1)S(1)}, bf16[928,512]{1,0:T(8,128)(2,1)S(1)}, f32[1]{0:T(128)}) custom-call(f32[64,512]{1,0:T(8,128)S(1)} %after.10.refs_0_, f32[64,512]{1,0:T(8,128)S(1)} %collective-permute-done.17.refs_1_, f32[64,512]{1,0:T(8,128)S(1)} %collective-permute-done.18.refs_2_, f32[64,512]{1,0:T(8,128)S(1)} %collective-permute-done.19.refs_3_, ...), custom_call_target="tpu_custom_call" | custom-call | tf_op jit(solution)/shard_map/pivot_inverse/pallas_call | solution.py:356
  61.6 2.0 %factor_rows.1 = f32[416,512]{1,0:T(8,128)} custom-call(f32[416,512]{1,0:T(8,128)S(1)} %subtract_divide_fusion.schur_ref, bf16[928,512]{1,0:T(8,128)(2,1)S(1)} %get-tuple-element.21.high_ref, bf16[928,512]{1,0:T(8,128)(2,1)S(1)} %get-tuple-element.22.low_ref), custom_call_target="tpu_custom_call" | custom-call | tf_op jit(solution)/shard_map/factor_rows/pallas_call | solution.py:387
  (61 shorter events, 8.0 us)
Async XLA Ops:
  1.1 10.7 %collective-permute-start.1 = (bf16[544,256]{1,0:T(8,128)(2,1)S(1)}, bf16[544,256]{1,0:T(8,128)(2,1)S(1)}, u32[]{:S(2)}, u32[]{:S(2)}) collective-permute-start(bf16[544,256]{1,0:T(8,128)(2,1)S(1)} %masked_chunks.3), channel_id=1, source_target_pairs={{0,2},{1,3},{2,0},{3,1},{4,6},{5,7},{6,4},{7,5},{8,10},{9,11},{10,... | collective-permute-start | bytes 835592 | tf_op jit(solution)/shard_map/ppermute | solution.py:53
  4.2 9.1 %collective-permute-start = (bf16[256,128]{1,0:T(8,128)(2,1)S(1)}, bf16[256,128]{1,0:T(8,128)(2,1)S(1)}, u32[]{:S(2)}, u32[]{:S(2)}) collective-permute-start(bf16[256,128]{1,0:T(8,128)(2,1)S(1)} %copy-done.2), channel_id=1, source_target_pairs={{0,16},{1,17},{2,18},{3,19},{4,20},{5,21},{6,22},{7,23},{8,24},{9,... | collective-permute-start | bytes 196616 | tf_op jit(solution)/shard_map/ppermute | solution.py:53
  5.7 7.7 %collective-permute-start.2 = (bf16[256,128]{1,0:T(8,128)(2,1)S(1)}, bf16[256,128]{1,0:T(8,128)(2,1)S(1)}, u32[]{:S(2)}, u32[]{:S(2)}) collective-permute-start(bf16[256,128]{1,0:T(8,128)(2,1)S(1)} %copy-done.2), channel_id=1, source_target_pairs={{0,18},{1,19},{2,16},{3,17},{4,22},{5,23},{6,20},{7,21},{8,26},{9,... | collective-permute-start | bytes 196616 | tf_op jit(solution)/shard_map/ppermute | solution.py:53
  8.7 10.3 %collective-permute-start.10 = (bf16[128,1280]{1,0:T(8,128)(2,1)}, bf16[128,1280]{1,0:T(8,128)(2,1)S(1)}, u32[]{:S(2)}, u32[]{:S(2)}) collective-permute-start(bf16[128,1280]{1,0:T(8,128)(2,1)} %get-tuple-element.19), channel_id=1, source_target_pairs={{0,18},{1,19},{2,16},{3,17},{4,22},{5,23},{6,20},{7,21},{8,9},{9,8... | collective-permute-start | bytes 983048 | tf_op jit(solution)/shard_map/ppermute | solution.py:53
  10.3 10.2 %collective-permute-start.8 = (bf16[128,1280]{1,0:T(8,128)(2,1)}, bf16[128,1280]{1,0:T(8,128)(2,1)S(1)}, u32[]{:S(2)}, u32[]{:S(2)}) collective-permute-start(bf16[128,1280]{1,0:T(8,128)(2,1)} %get-tuple-element.17), channel_id=1, source_target_pairs={{0,16},{1,17},{2,18},{3,19},{4,20},{5,21},{6,22},{7,23},{8,9},{9,8... | collective-permute-start | bytes 983048 | tf_op jit(solution)/shard_map/ppermute | solution.py:53
  11.8 8.7 %collective-permute-start.9 = (bf16[128,1280]{1,0:T(8,128)(2,1)}, bf16[128,1280]{1,0:T(8,128)(2,1)S(1)}, u32[]{:S(2)}, u32[]{:S(2)}) collective-permute-start(bf16[128,1280]{1,0:T(8,128)(2,1)} %get-tuple-element.18), channel_id=1, source_target_pairs={{0,2},{1,3},{2,0},{3,1},{4,6},{5,7},{6,4},{7,5},{8,9},{9,8},{10,11... | collective-permute-start | bytes 983048 | tf_op jit(solution)/shard_map/ppermute | solution.py:53
  13.3 1.3 %collective-permute-start.3 = (bf16[256,128]{1,0:T(8,128)(2,1)S(1)}, bf16[256,128]{1,0:T(8,128)(2,1)S(1)}, u32[]{:S(2)}, u32[]{:S(2)}) collective-permute-start(bf16[256,128]{1,0:T(8,128)(2,1)S(1)} %copy-done.2), channel_id=1, source_target_pairs={{0,8},{1,9},{2,10},{3,11},{4,12},{5,13},{6,14},{7,15},{8,0},{9,1},... | collective-permute-start | bytes 196616 | tf_op jit(solution)/shard_map/ppermute | solution.py:53
  13.4 1.4 %collective-permute-start.4 = (bf16[256,128]{1,0:T(8,128)(2,1)S(1)}, bf16[256,128]{1,0:T(8,128)(2,1)S(1)}, u32[]{:S(2)}, u32[]{:S(2)}) collective-permute-start(bf16[256,128]{1,0:T(8,128)(2,1)S(1)} %collective-permute-done.refs_1_), channel_id=1, source_target_pairs={{0,8},{1,9},{2,10},{3,11},{4,12},{5,13},{6,14},{7,15},{8,0},{9,1},... | collective-permute-start | bytes 196616 | tf_op jit(solution)/shard_map/ppermute | solution.py:53
  14.6 2.1 %collective-permute-start.6 = (bf16[256,128]{1,0:T(8,128)(2,1)S(1)}, bf16[256,128]{1,0:T(8,128)(2,1)S(1)}, u32[]{:S(2)}, u32[]{:S(2)}) collective-permute-start(bf16[256,128]{1,0:T(8,128)(2,1)S(1)} %collective-permute-done.2.refs_3_), channel_id=1, source_target_pairs={{0,8},{1,9},{2,10},{3,11},{4,12},{5,13},{6,14},{7,15},{8,0},{9,1},... | collective-permute-start | bytes 196616 | tf_op jit(solution)/shard_map/ppermute | solution.py:53
  14.8 3.3 %collective-permute-start.5 = (bf16[256,128]{1,0:T(8,128)(2,1)S(1)}, bf16[256,128]{1,0:T(8,128)(2,1)S(1)}, u32[]{:S(2)}, u32[]{:S(2)}) collective-permute-start(bf16[256,128]{1,0:T(8,128)(2,1)S(1)} %after.6.refs_2_), channel_id=1, source_target_pairs={{0,8},{1,9},{2,10},{3,11},{4,12},{5,13},{6,14},{7,15},{8,0},{9,1},... | collective-permute-start | bytes 196616 | tf_op jit(solution)/shard_map/ppermute | solution.py:53
  16.7 19.3 %collective-permute-start.7 = (bf16[1248,256]{1,0:T(8,128)(2,1)S(1)}, bf16[1248,256]{1,0:T(8,128)(2,1)S(1)}, u32[]{:S(2)}, u32[]{:S(2)}) collective-permute-start(bf16[1248,256]{1,0:T(8,128)(2,1)S(1)} %get-tuple-element.16), channel_id=1, source_target_pairs={{0,2},{1,3},{2,0},{3,1},{4,6},{5,7},{6,4},{7,5},{8,10},{9,11},{10,... | collective-permute-start | bytes 1916936 | tf_op jit(solution)/shard_map/ppermute | solution.py:53
  20.8 1.4 %collective-permute-start.11 = (f32[64,512]{1,0:T(8,128)S(1)}, f32[64,512]{1,0:T(8,128)S(1)}, u32[]{:S(2)}, u32[]{:S(2)}) collective-permute-start(f32[64,512]{1,0:T(8,128)S(1)} %slice.67), channel_id=1, source_target_pairs={{0,8},{1,9},{2,10},{3,11},{4,12},{5,13},{6,14},{7,15},{8,0},{9,1},... | collective-permute-start | bytes 393224 | tf_op jit(solution)/shard_map/ppermute | solution.py:53
  22.2 6.4 %collective-permute-start.12 = (f32[64,512]{1,0:T(8,128)S(1)}, f32[64,512]{1,0:T(8,128)S(1)}, u32[]{:S(2)}, u32[]{:S(2)}) collective-permute-start(f32[64,512]{1,0:T(8,128)S(1)} %slice_select_fusion), channel_id=1, source_target_pairs={{0,1},{1,0},{2,3},{3,2},{4,5},{5,4},{6,7},{7,6},{8,9},{9,8},{10,11... | collective-permute-start | bytes 393224 | tf_op jit(solution)/shard_map/ppermute | solution.py:53
  24.5 14.0 %collective-permute-start.15 = (f16[416,512]{1,0:T(8,128)(2,1)S(1)}, f16[416,512]{1,0:T(8,128)(2,1)S(1)}, u32[]{:S(2)}, u32[]{:S(2)}) collective-permute-start(f16[416,512]{1,0:T(8,128)(2,1)S(1)} %fusion.5), channel_id=1, source_target_pairs={{0,1},{1,0},{2,3},{3,2},{4,5},{5,4},{6,7},{7,6},{8,9},{9,8},{10,11... | collective-permute-start | bytes 1277960 | tf_op jit(solution)/shard_map/ppermute | solution.py:53
  28.7 10.1 %collective-permute-start.14 = (f32[64,512]{1,0:T(8,128)S(1)}, f32[64,512]{1,0:T(8,128)S(1)}, u32[]{:S(2)}, u32[]{:S(2)}) collective-permute-start(f32[64,512]{1,0:T(8,128)S(1)} %add.29.refs_1_), channel_id=1, source_target_pairs={{0,4},{1,5},{2,6},{3,7},{4,0},{5,1},{6,2},{7,3},{8,12},{9,13},{10,... | collective-permute-start | bytes 393224 | tf_op jit(solution)/shard_map/ppermute | solution.py:53
  36.6 18.5 %collective-permute-start.13 = (f16[416,512]{1,0:T(8,128)(2,1)S(1)}, f16[416,512]{1,0:T(8,128)(2,1)S(1)}, u32[]{:S(2)}, u32[]{:S(2)}) collective-permute-start(f16[416,512]{1,0:T(8,128)(2,1)S(1)} %fusion.4), channel_id=1, source_target_pairs={{0,1},{1,0},{2,3},{3,2},{4,5},{5,4},{6,7},{7,6},{8,9},{9,8},{10,11... | collective-permute-start | bytes 1277960 | tf_op jit(solution)/shard_map/ppermute | solution.py:53
  38.8 5.0 %collective-permute-start.17 = (f32[64,512]{1,0:T(8,128)S(1)}, f32[64,512]{1,0:T(8,128)S(1)}, u32[]{:S(2)}, u32[]{:S(2)}) collective-permute-start(f32[64,512]{1,0:T(8,128)S(1)} %add.36.refs_1_.refs_0_), channel_id=1, source_target_pairs={{0,16},{1,17},{2,18},{3,19},{4,20},{5,21},{6,22},{7,23},{8,24},{9,... | collective-permute-start | bytes 393224 | tf_op jit(solution)/shard_map/ppermute | solution.py:53
  40.8 20.1 %collective-permute-start.16 = (f16[416,512]{1,0:T(8,128)(2,1)S(1)}, f16[416,512]{1,0:T(8,128)(2,1)S(1)}, u32[]{:S(2)}, u32[]{:S(2)}) collective-permute-start(f16[416,512]{1,0:T(8,128)(2,1)S(1)} %fusion.3), channel_id=1, source_target_pairs={{0,4},{1,5},{2,6},{3,7},{4,0},{5,1},{6,2},{7,3},{8,12},{9,13},{10,... | collective-permute-start | bytes 1277960 | tf_op jit(solution)/shard_map/ppermute | solution.py:53
  43.9 9.9 %collective-permute-start.18 = (f32[64,512]{1,0:T(8,128)S(1)}, f32[64,512]{1,0:T(8,128)S(1)}, u32[]{:S(2)}, u32[]{:S(2)}) collective-permute-start(f32[64,512]{1,0:T(8,128)S(1)} %after.11), channel_id=1, source_target_pairs={{0,2},{1,3},{2,0},{3,1},{4,6},{5,7},{6,4},{7,5},{8,10},{9,11},{10,... | collective-permute-start | bytes 393224 | tf_op jit(solution)/shard_map/ppermute | solution.py:53
  44.4 10.8 %collective-permute-start.19 = (f32[64,512]{1,0:T(8,128)S(1)}, f32[64,512]{1,0:T(8,128)S(1)}, u32[]{:S(2)}, u32[]{:S(2)}) collective-permute-start(f32[64,512]{1,0:T(8,128)S(1)} %after.11), channel_id=1, source_target_pairs={{0,18},{1,19},{2,16},{3,17},{4,22},{5,23},{6,20},{7,21},{8,26},{9,... | collective-permute-start | bytes 393224 | tf_op jit(solution)/shard_map/ppermute | solution.py:53
  47.4 8.5 %collective-permute-start.20 = (f32[64,512]{1,0:T(8,128)S(1)}, f32[64,512]{1,0:T(8,128)S(1)}, u32[]{:S(2)}, u32[]{:S(2)}) collective-permute-start(f32[64,512]{1,0:T(8,128)S(1)} %add.36.refs_1_.refs_0_), channel_id=1, source_target_pairs={{0,8},{1,9},{2,10},{3,11},{4,12},{5,13},{6,14},{7,15},{8,0},{9,1},... | collective-permute-start | bytes 393224 | tf_op jit(solution)/shard_map/ppermute | solution.py:53
  53.7 2.2 %collective-permute-start.21 = (f32[64,512]{1,0:T(8,128)S(1)}, f32[64,512]{1,0:T(8,128)S(1)}, u32[]{:S(2)}, u32[]{:S(2)}) collective-permute-start(f32[64,512]{1,0:T(8,128)S(1)} %collective-permute-done.17.refs_1_), channel_id=1, source_target_pairs={{0,8},{1,9},{2,10},{3,11},{4,12},{5,13},{6,14},{7,15},{8,0},{9,1},... | collective-permute-start | bytes 393224 | tf_op jit(solution)/shard_map/ppermute | solution.py:53
  55.1 1.3 %collective-permute-start.22 = (f32[64,512]{1,0:T(8,128)S(1)}, f32[64,512]{1,0:T(8,128)S(1)}, u32[]{:S(2)}, u32[]{:S(2)}) collective-permute-start(f32[64,512]{1,0:T(8,128)S(1)} %collective-permute-done.18.refs_2_), channel_id=1, source_target_pairs={{0,8},{1,9},{2,10},{3,11},{4,12},{5,13},{6,14},{7,15},{8,0},{9,1},... | collective-permute-start | bytes 393224 | tf_op jit(solution)/shard_map/ppermute | solution.py:53
  55.1 1.5 %collective-permute-start.23 = (f32[64,512]{1,0:T(8,128)S(1)}, f32[64,512]{1,0:T(8,128)S(1)}, u32[]{:S(2)}, u32[]{:S(2)}) collective-permute-start(f32[64,512]{1,0:T(8,128)S(1)} %collective-permute-done.19.refs_3_), channel_id=1, source_target_pairs={{0,8},{1,9},{2,10},{3,11},{4,12},{5,13},{6,14},{7,15},{8,0},{9,1},... | collective-permute-start | bytes 393224 | tf_op jit(solution)/shard_map/ppermute | solution.py:53
  (3 other events, 26.8 us)

commit v6 on v5

--- a/solution.py
+++ b/solution.py
@@ -338,8 +338,8 @@
     square = (order, order)
     diagonal = lax.broadcasted_iota(jnp.int32, square, 0) == lax.broadcasted_iota(jnp.int32, square, 1)
     pivot = pivot_ref[...]
-    scale = jnp.sum(jnp.where(diagonal, pivot, 0.0)) / order
-    power = jnp.where(diagonal, 1.0, 0.0) - pivot / scale
+    share = order / jnp.sum(jnp.where(diagonal, pivot, 0.0), keepdims=True)
+    power = jnp.where(diagonal, 1.0, 0.0) - pivot * share
     rest = power
     parts = two_parts(power)
     for step in range(NS_ITERS - 1):
@@ -347,7 +347,7 @@
         parts = two_parts(power)
         rest = rest + power + product(two_parts(rest), parts)
     high_ref[:order, :], low_ref[:order, :] = two_parts(rest)
-    scale_ref[0] = scale
+    scale_ref[0] = share[0, 0]
 
 
 def inverse_rest(grid, pieces, spare):
@@ -492,9 +492,9 @@
     if grid.cores > 1:
         pieces = pieces + [grid.swap(piece, dcore=1) for piece in pieces]
     pieces[0] = after(pieces[0], base)
-    high, low, scale = inverse_rest(grid, pieces, own_rows)
+    high, low, share = inverse_rest(grid, pieces, own_rows)
     schur_rows = base - sum(value.astype(jnp.float32) for value in sending.values())
-    return factor_rows(schur_rows / scale[0], high, low)
+    return factor_rows(schur_rows * share[0], high, low)
 
 
 def solution(mesh):

time: 63.8 us -> 63.8 us (level)
    mul x0 -> x1, other arithmetic: none -> 0.78 us  [body(): return factor_rows(schur_rows * share[0], high, low)]
    div x1 -> x0, other arithmetic: 0.77 us -> none  [body(): return factor_rows(schur_rows / scale[0], high, low)]
where the time goes in v6:
time: 63.8 us; the launch traced here: 63.6 us
  starting transfers between devices  24.5 us (38%)
  waiting for transfers between devices  23 us (36%)
  Pallas kernels  12.8 us (20%)
  matrix products  2.15 us (3%)
  other arithmetic  0.84 us (1%)
    ppermute x24, starting transfers between devices, permute(): return lax.ppermute(value, ('gr', 'gc'), pairs)  24.5 us
    ppermute x24, waiting for transfers between devices, permute(): return lax.ppermute(value, ('gr', 'gc'), pairs)  23 us
    pallas_call x1, Pallas kernels, inverse_rest(): pl.pallas_call(functools.partial(inverse_kernel, grid.xs, grid.ys, grid.p...  4.04 us
    pallas_call x1, Pallas kernels, pivot_pack(): pl.pallas_call(functools.partial(pivot_pack_kernel, grid.xs, grid.ys, gri...  2.92 us
    pallas_call x2, Pallas kernels, masked_chunks(): pl.pallas_call(functools.partial(chunks_kernel, grid.ys, grid.ps, wanted,...  2.65 us
    dot_general x8, matrix products, update(): jnp.dot(part, half, preferred_element_type=jnp.float32)  2.15 us
    pallas_call x1, Pallas kernels, factor_rows(): pl.pallas_call(factor_kernel, in_specs=[VMEM, VMEM, VMEM], out_specs=VMEM...  1.97 us
  transfers between devices with their start and end apart: 24, of which 11 were waited for; matrix products, arithmetic and copies ran while one was open for 4% of the time, Pallas kernels for 15%

profile of v6, /device:TPU:0, one launch (start us, length us, event | category | flops | bytes accessed | tf_op | source)
XLA Modules:
  0.0 63.6 jit_solution(12642606072134567686)
XLA Ops:
  0.0 1.1 %masked_chunks.3 = bf16[544,256]{1,0:T(8,128)(2,1)S(1)} custom-call(s32[2]{0:T(128)} %first.1, bf16[3328,256]{1,0:T(8,128)(2,1)} %window_ref.5, bf16[256,128]{1,0:T(8,128)(2,1)} %refs_0_.3), custom_call_target="tpu_custom_call" | custom-call | bytes 37748736 | tf_op jit(solution)/shard_map/masked_chunks/pallas_call | solution.py:139
  1.1 3.1 %collective-permute-start.1 = (bf16[544,256]{1,0:T(8,128)(2,1)S(1)}, bf16[544,256]{1,0:T(8,128)(2,1)S(1)}, u32[]{:S(2)}, u32[]{:S(2)}) collective-permute-start(bf16[544,256]{1,0:T(8,128)(2,1)S(1)} %masked_chunks.3), channel_id=1, source_target_pairs={{0,2},{1,3},{2,0},{3,1},{4,6},{5,7},{6,4},{7,5},{8,10},{9,11},{10,... | collective-permute-start | bytes 835592 | tf_op jit(solution)/shard_map/ppermute | solution.py:53
  4.2 1.5 %collective-permute-start = (bf16[256,128]{1,0:T(8,128)(2,1)S(1)}, bf16[256,128]{1,0:T(8,128)(2,1)S(1)}, u32[]{:S(2)}, u32[]{:S(2)}) collective-permute-start(bf16[256,128]{1,0:T(8,128)(2,1)S(1)} %copy-done.2), channel_id=1, source_target_pairs={{0,16},{1,17},{2,18},{3,19},{4,20},{5,21},{6,22},{7,23},{8,24},{9,... | collective-permute-start | bytes 196616 | tf_op jit(solution)/shard_map/ppermute | solution.py:53
  5.7 2.9 %pivot_pack.1 = (bf16[128,1280]{1,0:T(8,128)(2,1)S(1)}, bf16[128,1280]{1,0:T(8,128)(2,1)}, bf16[128,1280]{1,0:T(8,128)(2,1)}, bf16[128,1280]{1,0:T(8,128)(2,1)}) custom-call(s32[2]{0:T(128)S(1)} %copy-done, bf16[3328,256]{1,0:T(8,128)(2,1)} %window_ref.5, f32[416,512]{1,0:T(8,128)} %block_ref.1), custom_call_target="tpu_custom_call" | custom-call | tf_op jit(solution)/shard_map/pivot_pack/pallas_call | solution.py:215
  8.7 1.6 %collective-permute-start.10 = (bf16[128,1280]{1,0:T(8,128)(2,1)}, bf16[128,1280]{1,0:T(8,128)(2,1)S(1)}, u32[]{:S(2)}, u32[]{:S(2)}) collective-permute-start(bf16[128,1280]{1,0:T(8,128)(2,1)} %get-tuple-element.19), channel_id=1, source_target_pairs={{0,18},{1,19},{2,16},{3,17},{4,22},{5,23},{6,20},{7,21},{8,9},{9,8... | collective-permute-start | bytes 983048 | tf_op jit(solution)/shard_map/ppermute | solution.py:53
  10.3 1.5 %collective-permute-start.8 = (bf16[128,1280]{1,0:T(8,128)(2,1)}, bf16[128,1280]{1,0:T(8,128)(2,1)S(1)}, u32[]{:S(2)}, u32[]{:S(2)}) collective-permute-start(bf16[128,1280]{1,0:T(8,128)(2,1)} %get-tuple-element.17), channel_id=1, source_target_pairs={{0,16},{1,17},{2,18},{3,19},{4,20},{5,21},{6,22},{7,23},{8,9},{9,8... | collective-permute-start | bytes 983048 | tf_op jit(solution)/shard_map/ppermute | solution.py:53
  11.8 1.5 %collective-permute-start.9 = (bf16[128,1280]{1,0:T(8,128)(2,1)}, bf16[128,1280]{1,0:T(8,128)(2,1)S(1)}, u32[]{:S(2)}, u32[]{:S(2)}) collective-permute-start(bf16[128,1280]{1,0:T(8,128)(2,1)} %get-tuple-element.18), channel_id=1, source_target_pairs={{0,2},{1,3},{2,0},{3,1},{4,6},{5,7},{6,4},{7,5},{8,9},{9,8},{10,11... | collective-permute-start | bytes 983048 | tf_op jit(solution)/shard_map/ppermute | solution.py:53
  15.1 1.6 %masked_chunks.2 = (bf16[1248,256]{1,0:T(8,128)(2,1)S(1)}, bf16[1664,256]{1,0:T(8,128)(2,1)S(1)}) custom-call(s32[2]{0:T(128)} %first.1, bf16[3328,256]{1,0:T(8,128)(2,1)} %window_ref.5), custom_call_target="tpu_custom_call" | custom-call | bytes 37748736 | tf_op jit(solution)/shard_map/masked_chunks/pallas_call | solution.py:139
  16.7 1.3 %collective-permute-start.7 = (bf16[1248,256]{1,0:T(8,128)(2,1)S(1)}, bf16[1248,256]{1,0:T(8,128)(2,1)S(1)}, u32[]{:S(2)}, u32[]{:S(2)}) collective-permute-start(bf16[1248,256]{1,0:T(8,128)(2,1)S(1)} %get-tuple-element.16), channel_id=1, source_target_pairs={{0,2},{1,3},{2,0},{3,1},{4,6},{5,7},{6,4},{7,5},{8,10},{9,11},{10,... | collective-permute-start | bytes 1916936 | tf_op jit(solution)/shard_map/ppermute | solution.py:53
  18.0 0.9 %panel_assemble.1.panel_ref = bf16[512,512]{1,0:T(8,128)(2,1)S(1)} custom-call(bf16[256,128]{1,0:T(8,128)(2,1)} %refs_0_.3, bf16[256,128]{1,0:T(8,128)(2,1)S(1)} %collective-permute-done.refs_1_, bf16[256,128]{1,0:T(8,128)(2,1)S(1)} %after.6.refs_2_, bf16[256,128]{1,0:T(8,128)(2,1)S(1)} %collective-permute-done.2.refs_3_, ...), custom_call_target="tpu_custom_call" | custom-call | tf_op jit(solution)/shard_map/panel_assemble/pallas_call | solution.py:269
  18.9 1.5 %collective-permute-done.8.refs_1_ = bf16[128,1280]{1,0:T(8,128)(2,1)S(1)} collective-permute-done((bf16[128,1280]{1,0:T(8,128)(2,1)}, bf16[128,1280]{1,0:T(8,128)(2,1)S(1)}, u32[]{:S(2)}, u32[]{:S(2)}) %collective-permute-start.8) | collective-permute-done | bytes 327712 | tf_op jit(solution)/shard_map/ppermute | solution.py:53
  21.2 1.1 %collective-permute-done.11 = f32[64,512]{1,0:T(8,128)S(1)} collective-permute-done((f32[64,512]{1,0:T(8,128)S(1)}, f32[64,512]{1,0:T(8,128)S(1)}, u32[]{:S(2)}, u32[]{:S(2)}) %collective-permute-start.11) | collective-permute-done | bytes 131104 | tf_op jit(solution)/shard_map/ppermute | solution.py:53
  22.2 1.9 %collective-permute-start.12 = (f32[64,512]{1,0:T(8,128)S(1)}, f32[64,512]{1,0:T(8,128)S(1)}, u32[]{:S(2)}, u32[]{:S(2)}) collective-permute-start(f32[64,512]{1,0:T(8,128)S(1)} %slice_select_fusion), channel_id=1, source_target_pairs={{0,1},{1,0},{2,3},{3,2},{4,5},{5,4},{6,7},{7,6},{8,9},{9,8},{10,11... | collective-permute-start | bytes 393224 | tf_op jit(solution)/shard_map/ppermute | solution.py:53
  24.7 4.0 %collective-permute-done.12 = f32[64,512]{1,0:T(8,128)S(1)} collective-permute-done((f32[64,512]{1,0:T(8,128)S(1)}, f32[64,512]{1,0:T(8,128)S(1)}, u32[]{:S(2)}, u32[]{:S(2)}) %collective-permute-start.12) | collective-permute-done | bytes 131104 | tf_op jit(solution)/shard_map/ppermute | solution.py:53
  28.7 2.7 %collective-permute-start.14 = (f32[64,512]{1,0:T(8,128)S(1)}, f32[64,512]{1,0:T(8,128)S(1)}, u32[]{:S(2)}, u32[]{:S(2)}) collective-permute-start(f32[64,512]{1,0:T(8,128)S(1)} %add.29.refs_1_), channel_id=1, source_target_pairs={{0,4},{1,5},{2,6},{3,7},{4,0},{5,1},{6,2},{7,3},{8,12},{9,13},{10,... | collective-permute-start | bytes 393224 | tf_op jit(solution)/shard_map/ppermute | solution.py:53
  31.3 4.7 %collective-permute-done.7.refs_0_ = bf16[1248,256]{1,0:T(8,128)(2,1)S(1)} collective-permute-done((bf16[1248,256]{1,0:T(8,128)(2,1)S(1)}, bf16[1248,256]{1,0:T(8,128)(2,1)S(1)}, u32[]{:S(2)}, u32[]{:S(2)}) %collective-permute-start.7) | collective-permute-done | bytes 639008 | tf_op jit(solution)/shard_map/ppermute | solution.py:53
  36.6 1.6 %collective-permute-start.13 = (f16[416,512]{1,0:T(8,128)(2,1)S(1)}, f16[416,512]{1,0:T(8,128)(2,1)S(1)}, u32[]{:S(2)}, u32[]{:S(2)}) collective-permute-start(f16[416,512]{1,0:T(8,128)(2,1)S(1)} %fusion.4), channel_id=1, source_target_pairs={{0,1},{1,0},{2,3},{3,2},{4,5},{5,4},{6,7},{7,6},{8,9},{9,8},{10,11... | collective-permute-start | bytes 1277960 | tf_op jit(solution)/shard_map/ppermute | solution.py:53
  38.8 1.9 %collective-permute-start.17 = (f32[64,512]{1,0:T(8,128)S(1)}, f32[64,512]{1,0:T(8,128)S(1)}, u32[]{:S(2)}, u32[]{:S(2)}) collective-permute-start(f32[64,512]{1,0:T(8,128)S(1)} %add.36.refs_1_.refs_0_), channel_id=1, source_target_pairs={{0,16},{1,17},{2,18},{3,19},{4,20},{5,21},{6,22},{7,23},{8,24},{9,... | collective-permute-start | bytes 393224 | tf_op jit(solution)/shard_map/ppermute | solution.py:53
  41.3 2.6 %collective-permute-done.17.refs_1_ = f32[64,512]{1,0:T(8,128)S(1)} collective-permute-done((f32[64,512]{1,0:T(8,128)S(1)}, f32[64,512]{1,0:T(8,128)S(1)}, u32[]{:S(2)}, u32[]{:S(2)}) %collective-permute-start.17) | collective-permute-done | bytes 131104 | tf_op jit(solution)/shard_map/ppermute | solution.py:53
  44.4 2.8 %collective-permute-start.19 = (f32[64,512]{1,0:T(8,128)S(1)}, f32[64,512]{1,0:T(8,128)S(1)}, u32[]{:S(2)}, u32[]{:S(2)}) collective-permute-start(f32[64,512]{1,0:T(8,128)S(1)} %after.11), channel_id=1, source_target_pairs={{0,18},{1,19},{2,16},{3,17},{4,22},{5,23},{6,20},{7,21},{8,26},{9,... | collective-permute-start | bytes 393224 | tf_op jit(solution)/shard_map/ppermute | solution.py:53
  47.5 6.2 %collective-permute-done.18.refs_2_ = f32[64,512]{1,0:T(8,128)S(1)} collective-permute-done((f32[64,512]{1,0:T(8,128)S(1)}, f32[64,512]{1,0:T(8,128)S(1)}, u32[]{:S(2)}, u32[]{:S(2)}) %collective-permute-start.18) | collective-permute-done | bytes 131104 | tf_op jit(solution)/shard_map/ppermute | solution.py:53
  53.7 1.4 %collective-permute-done.19.refs_3_ = f32[64,512]{1,0:T(8,128)S(1)} collective-permute-done((f32[64,512]{1,0:T(8,128)S(1)}, f32[64,512]{1,0:T(8,128)S(1)}, u32[]{:S(2)}, u32[]{:S(2)}) %collective-permute-start.19) | collective-permute-done | bytes 131104 | tf_op jit(solution)/shard_map/ppermute | solution.py:53
  56.7 4.0 %pivot_inverse.1 = (bf16[928,512]{1,0:T(8,128)(2,1)S(1)}, bf16[928,512]{1,0:T(8,128)(2,1)S(1)}, f32[1]{0:T(128)}) custom-call(f32[64,512]{1,0:T(8,128)S(1)} %after.10.refs_0_, f32[64,512]{1,0:T(8,128)S(1)} %collective-permute-done.17.refs_1_, f32[64,512]{1,0:T(8,128)S(1)} %collective-permute-done.18.refs_2_, f32[64,512]{1,0:T(8,128)S(1)} %collective-permute-done.19.refs_3_, ...), custom_call_target="tpu_custom_call" | custom-call | tf_op jit(solution)/shard_map/pivot_inverse/pallas_call | solution.py:356
  61.6 2.0 %factor_rows.1 = f32[416,512]{1,0:T(8,128)} custom-call(f32[416,512]{1,0:T(8,128)S(1)} %subtract_multiply_fusion.schur_ref, bf16[928,512]{1,0:T(8,128)(2,1)S(1)} %get-tuple-element.21.high_ref, bf16[928,512]{1,0:T(8,128)(2,1)S(1)} %get-tuple-element.22.low_ref), custom_call_target="tpu_custom_call" | custom-call | tf_op jit(solution)/shard_map/factor_rows/pallas_call | solution.py:387
  (61 shorter events, 8.0 us)
Async XLA Ops:
  1.1 10.7 %collective-permute-start.1 = (bf16[544,256]{1,0:T(8,128)(2,1)S(1)}, bf16[544,256]{1,0:T(8,128)(2,1)S(1)}, u32[]{:S(2)}, u32[]{:S(2)}) collective-permute-start(bf16[544,256]{1,0:T(8,128)(2,1)S(1)} %masked_chunks.3), channel_id=1, source_target_pairs={{0,2},{1,3},{2,0},{3,1},{4,6},{5,7},{6,4},{7,5},{8,10},{9,11},{10,... | collective-permute-start | bytes 835592 | tf_op jit(solution)/shard_map/ppermute | solution.py:53
  4.2 9.1 %collective-permute-start = (bf16[256,128]{1,0:T(8,128)(2,1)S(1)}, bf16[256,128]{1,0:T(8,128)(2,1)S(1)}, u32[]{:S(2)}, u32[]{:S(2)}) collective-permute-start(bf16[256,128]{1,0:T(8,128)(2,1)S(1)} %copy-done.2), channel_id=1, source_target_pairs={{0,16},{1,17},{2,18},{3,19},{4,20},{5,21},{6,22},{7,23},{8,24},{9,... | collective-permute-start | bytes 196616 | tf_op jit(solution)/shard_map/ppermute | solution.py:53
  5.7 7.7 %collective-permute-start.2 = (bf16[256,128]{1,0:T(8,128)(2,1)S(1)}, bf16[256,128]{1,0:T(8,128)(2,1)S(1)}, u32[]{:S(2)}, u32[]{:S(2)}) collective-permute-start(bf16[256,128]{1,0:T(8,128)(2,1)S(1)} %copy-done.2), channel_id=1, source_target_pairs={{0,18},{1,19},{2,16},{3,17},{4,22},{5,23},{6,20},{7,21},{8,26},{9,... | collective-permute-start | bytes 196616 | tf_op jit(solution)/shard_map/ppermute | solution.py:53
  8.7 10.3 %collective-permute-start.10 = (bf16[128,1280]{1,0:T(8,128)(2,1)}, bf16[128,1280]{1,0:T(8,128)(2,1)S(1)}, u32[]{:S(2)}, u32[]{:S(2)}) collective-permute-start(bf16[128,1280]{1,0:T(8,128)(2,1)} %get-tuple-element.19), channel_id=1, source_target_pairs={{0,18},{1,19},{2,16},{3,17},{4,22},{5,23},{6,20},{7,21},{8,9},{9,8... | collective-permute-start | bytes 983048 | tf_op jit(solution)/shard_map/ppermute | solution.py:53
  10.3 10.2 %collective-permute-start.8 = (bf16[128,1280]{1,0:T(8,128)(2,1)}, bf16[128,1280]{1,0:T(8,128)(2,1)S(1)}, u32[]{:S(2)}, u32[]{:S(2)}) collective-permute-start(bf16[128,1280]{1,0:T(8,128)(2,1)} %get-tuple-element.17), channel_id=1, source_target_pairs={{0,16},{1,17},{2,18},{3,19},{4,20},{5,21},{6,22},{7,23},{8,9},{9,8... | collective-permute-start | bytes 983048 | tf_op jit(solution)/shard_map/ppermute | solution.py:53
  11.8 8.7 %collective-permute-start.9 = (bf16[128,1280]{1,0:T(8,128)(2,1)}, bf16[128,1280]{1,0:T(8,128)(2,1)S(1)}, u32[]{:S(2)}, u32[]{:S(2)}) collective-permute-start(bf16[128,1280]{1,0:T(8,128)(2,1)} %get-tuple-element.18), channel_id=1, source_target_pairs={{0,2},{1,3},{2,0},{3,1},{4,6},{5,7},{6,4},{7,5},{8,9},{9,8},{10,11... | collective-permute-start | bytes 983048 | tf_op jit(solution)/shard_map/ppermute | solution.py:53
  13.3 1.3 %collective-permute-start.3 = (bf16[256,128]{1,0:T(8,128)(2,1)S(1)}, bf16[256,128]{1,0:T(8,128)(2,1)S(1)}, u32[]{:S(2)}, u32[]{:S(2)}) collective-permute-start(bf16[256,128]{1,0:T(8,128)(2,1)S(1)} %copy-done.2), channel_id=1, source_target_pairs={{0,8},{1,9},{2,10},{3,11},{4,12},{5,13},{6,14},{7,15},{8,0},{9,1},... | collective-permute-start | bytes 196616 | tf_op jit(solution)/shard_map/ppermute | solution.py:53
  13.4 1.4 %collective-permute-start.4 = (bf16[256,128]{1,0:T(8,128)(2,1)S(1)}, bf16[256,128]{1,0:T(8,128)(2,1)S(1)}, u32[]{:S(2)}, u32[]{:S(2)}) collective-permute-start(bf16[256,128]{1,0:T(8,128)(2,1)S(1)} %collective-permute-done.refs_1_), channel_id=1, source_target_pairs={{0,8},{1,9},{2,10},{3,11},{4,12},{5,13},{6,14},{7,15},{8,0},{9,1},... | collective-permute-start | bytes 196616 | tf_op jit(solution)/shard_map/ppermute | solution.py:53
  14.6 2.1 %collective-permute-start.6 = (bf16[256,128]{1,0:T(8,128)(2,1)S(1)}, bf16[256,128]{1,0:T(8,128)(2,1)S(1)}, u32[]{:S(2)}, u32[]{:S(2)}) collective-permute-start(bf16[256,128]{1,0:T(8,128)(2,1)S(1)} %collective-permute-done.2.refs_3_), channel_id=1, source_target_pairs={{0,8},{1,9},{2,10},{3,11},{4,12},{5,13},{6,14},{7,15},{8,0},{9,1},... | collective-permute-start | bytes 196616 | tf_op jit(solution)/shard_map/ppermute | solution.py:53
  14.8 3.3 %collective-permute-start.5 = (bf16[256,128]{1,0:T(8,128)(2,1)S(1)}, bf16[256,128]{1,0:T(8,128)(2,1)S(1)}, u32[]{:S(2)}, u32[]{:S(2)}) collective-permute-start(bf16[256,128]{1,0:T(8,128)(2,1)S(1)} %after.6.refs_2_), channel_id=1, source_target_pairs={{0,8},{1,9},{2,10},{3,11},{4,12},{5,13},{6,14},{7,15},{8,0},{9,1},... | collective-permute-start | bytes 196616 | tf_op jit(solution)/shard_map/ppermute | solution.py:53
  16.7 19.3 %collective-permute-start.7 = (bf16[1248,256]{1,0:T(8,128)(2,1)S(1)}, bf16[1248,256]{1,0:T(8,128)(2,1)S(1)}, u32[]{:S(2)}, u32[]{:S(2)}) collective-permute-start(bf16[1248,256]{1,0:T(8,128)(2,1)S(1)} %get-tuple-element.16), channel_id=1, source_target_pairs={{0,2},{1,3},{2,0},{3,1},{4,6},{5,7},{6,4},{7,5},{8,10},{9,11},{10,... | collective-permute-start | bytes 1916936 | tf_op jit(solution)/shard_map/ppermute | solution.py:53
  20.8 1.4 %collective-permute-start.11 = (f32[64,512]{1,0:T(8,128)S(1)}, f32[64,512]{1,0:T(8,128)S(1)}, u32[]{:S(2)}, u32[]{:S(2)}) collective-permute-start(f32[64,512]{1,0:T(8,128)S(1)} %slice.67), channel_id=1, source_target_pairs={{0,8},{1,9},{2,10},{3,11},{4,12},{5,13},{6,14},{7,15},{8,0},{9,1},... | collective-permute-start | bytes 393224 | tf_op jit(solution)/shard_map/ppermute | solution.py:53
  22.2 6.4 %collective-permute-start.12 = (f32[64,512]{1,0:T(8,128)S(1)}, f32[64,512]{1,0:T(8,128)S(1)}, u32[]{:S(2)}, u32[]{:S(2)}) collective-permute-start(f32[64,512]{1,0:T(8,128)S(1)} %slice_select_fusion), channel_id=1, source_target_pairs={{0,1},{1,0},{2,3},{3,2},{4,5},{5,4},{6,7},{7,6},{8,9},{9,8},{10,11... | collective-permute-start | bytes 393224 | tf_op jit(solution)/shard_map/ppermute | solution.py:53
  24.5 14.0 %collective-permute-start.15 = (f16[416,512]{1,0:T(8,128)(2,1)S(1)}, f16[416,512]{1,0:T(8,128)(2,1)S(1)}, u32[]{:S(2)}, u32[]{:S(2)}) collective-permute-start(f16[416,512]{1,0:T(8,128)(2,1)S(1)} %fusion.5), channel_id=1, source_target_pairs={{0,1},{1,0},{2,3},{3,2},{4,5},{5,4},{6,7},{7,6},{8,9},{9,8},{10,11... | collective-permute-start | bytes 1277960 | tf_op jit(solution)/shard_map/ppermute | solution.py:53
  28.7 10.1 %collective-permute-start.14 = (f32[64,512]{1,0:T(8,128)S(1)}, f32[64,512]{1,0:T(8,128)S(1)}, u32[]{:S(2)}, u32[]{:S(2)}) collective-permute-start(f32[64,512]{1,0:T(8,128)S(1)} %add.29.refs_1_), channel_id=1, source_target_pairs={{0,4},{1,5},{2,6},{3,7},{4,0},{5,1},{6,2},{7,3},{8,12},{9,13},{10,... | collective-permute-start | bytes 393224 | tf_op jit(solution)/shard_map/ppermute | solution.py:53
  36.6 18.5 %collective-permute-start.13 = (f16[416,512]{1,0:T(8,128)(2,1)S(1)}, f16[416,512]{1,0:T(8,128)(2,1)S(1)}, u32[]{:S(2)}, u32[]{:S(2)}) collective-permute-start(f16[416,512]{1,0:T(8,128)(2,1)S(1)} %fusion.4), channel_id=1, source_target_pairs={{0,1},{1,0},{2,3},{3,2},{4,5},{5,4},{6,7},{7,6},{8,9},{9,8},{10,11... | collective-permute-start | bytes 1277960 | tf_op jit(solution)/shard_map/ppermute | solution.py:53
  38.8 5.0 %collective-permute-start.17 = (f32[64,512]{1,0:T(8,128)S(1)}, f32[64,512]{1,0:T(8,128)S(1)}, u32[]{:S(2)}, u32[]{:S(2)}) collective-permute-start(f32[64,512]{1,0:T(8,128)S(1)} %add.36.refs_1_.refs_0_), channel_id=1, source_target_pairs={{0,16},{1,17},{2,18},{3,19},{4,20},{5,21},{6,22},{7,23},{8,24},{9,... | collective-permute-start | bytes 393224 | tf_op jit(solution)/shard_map/ppermute | solution.py:53
  40.8 20.1 %collective-permute-start.16 = (f16[416,512]{1,0:T(8,128)(2,1)S(1)}, f16[416,512]{1,0:T(8,128)(2,1)S(1)}, u32[]{:S(2)}, u32[]{:S(2)}) collective-permute-start(f16[416,512]{1,0:T(8,128)(2,1)S(1)} %fusion.3), channel_id=1, source_target_pairs={{0,4},{1,5},{2,6},{3,7},{4,0},{5,1},{6,2},{7,3},{8,12},{9,13},{10,... | collective-permute-start | bytes 1277960 | tf_op jit(solution)/shard_map/ppermute | solution.py:53
  43.9 9.9 %collective-permute-start.18 = (f32[64,512]{1,0:T(8,128)S(1)}, f32[64,512]{1,0:T(8,128)S(1)}, u32[]{:S(2)}, u32[]{:S(2)}) collective-permute-start(f32[64,512]{1,0:T(8,128)S(1)} %after.11), channel_id=1, source_target_pairs={{0,2},{1,3},{2,0},{3,1},{4,6},{5,7},{6,4},{7,5},{8,10},{9,11},{10,... | collective-permute-start | bytes 393224 | tf_op jit(solution)/shard_map/ppermute | solution.py:53
  44.4 10.8 %collective-permute-start.19 = (f32[64,512]{1,0:T(8,128)S(1)}, f32[64,512]{1,0:T(8,128)S(1)}, u32[]{:S(2)}, u32[]{:S(2)}) collective-permute-start(f32[64,512]{1,0:T(8,128)S(1)} %after.11), channel_id=1, source_target_pairs={{0,18},{1,19},{2,16},{3,17},{4,22},{5,23},{6,20},{7,21},{8,26},{9,... | collective-permute-start | bytes 393224 | tf_op jit(solution)/shard_map/ppermute | solution.py:53
  47.4 8.5 %collective-permute-start.20 = (f32[64,512]{1,0:T(8,128)S(1)}, f32[64,512]{1,0:T(8,128)S(1)}, u32[]{:S(2)}, u32[]{:S(2)}) collective-permute-start(f32[64,512]{1,0:T(8,128)S(1)} %add.36.refs_1_.refs_0_), channel_id=1, source_target_pairs={{0,8},{1,9},{2,10},{3,11},{4,12},{5,13},{6,14},{7,15},{8,0},{9,1},... | collective-permute-start | bytes 393224 | tf_op jit(solution)/shard_map/ppermute | solution.py:53
  53.7 2.2 %collective-permute-start.21 = (f32[64,512]{1,0:T(8,128)S(1)}, f32[64,512]{1,0:T(8,128)S(1)}, u32[]{:S(2)}, u32[]{:S(2)}) collective-permute-start(f32[64,512]{1,0:T(8,128)S(1)} %collective-permute-done.17.refs_1_), channel_id=1, source_target_pairs={{0,8},{1,9},{2,10},{3,11},{4,12},{5,13},{6,14},{7,15},{8,0},{9,1},... | collective-permute-start | bytes 393224 | tf_op jit(solution)/shard_map/ppermute | solution.py:53
  55.1 1.3 %collective-permute-start.22 = (f32[64,512]{1,0:T(8,128)S(1)}, f32[64,512]{1,0:T(8,128)S(1)}, u32[]{:S(2)}, u32[]{:S(2)}) collective-permute-start(f32[64,512]{1,0:T(8,128)S(1)} %collective-permute-done.18.refs_2_), channel_id=1, source_target_pairs={{0,8},{1,9},{2,10},{3,11},{4,12},{5,13},{6,14},{7,15},{8,0},{9,1},... | collective-permute-start | bytes 393224 | tf_op jit(solution)/shard_map/ppermute | solution.py:53
  55.1 1.5 %collective-permute-start.23 = (f32[64,512]{1,0:T(8,128)S(1)}, f32[64,512]{1,0:T(8,128)S(1)}, u32[]{:S(2)}, u32[]{:S(2)}) collective-permute-start(f32[64,512]{1,0:T(8,128)S(1)} %collective-permute-done.19.refs_3_), channel_id=1, source_target_pairs={{0,8},{1,9},{2,10},{3,11},{4,12},{5,13},{6,14},{7,15},{8,0},{9,1},... | collective-permute-start | bytes 393224 | tf_op jit(solution)/shard_map/ppermute | solution.py:53
  (3 other events, 26.8 us)
